TPU v7x, 512 devices: a whole 4x4x16 slice. The times are simulated.
512 devices in a mesh: wide: 32 (over x, z_hi, y), narrow: 16 (over z_lo, core).
Axes of the slice: x: 4, y: 4, z: 16 (z_hi: 2, z_lo: 8; z = z_hi * 8 + z_lo), core: 2. Of those that a mesh axis runs over, the one named last changes fastest.
Arguments:
- query_key: bfloat16 [16384, 32, 256], P(('wide', 'narrow')), may hold values from -27 to 27
- value_heads: bfloat16 [16384, 32, 128], P(('wide', 'narrow')), may hold values from -6 to 6
- fast_inputs: bfloat16 [16384, 16, 768], P(('wide', 'narrow')), may hold values from -6 to 6
- rate_logits: bfloat16 [16384, 16, 3], P(('wide', 'narrow')), may hold values from -4 to 4
- gate_fast: float32 [16, 256, 512], P('narrow'), may hold values from -0.375 to 0.375
- up_fast: float32 [16, 256, 512], P('narrow'), may hold values from -0.375 to 0.375
- down_fast: float32 [16, 512, 256], P('narrow'), may hold values from -0.25 to 0.25
Outputs:
- window_out: float32 [16384, 32, 128], P('wide', 'narrow')
- fast_out: float32 [16384, 16, 256], P('wide', 'narrow')
All inputs are finite; a program needn't handle non-finite values.
Results may differ from a plain program's by a relative error of at most 0.009.
Values may be sent and summed in bfloat16 or wider, within the bound.
No kernel may reach another device: no remote copies, remote signals or barrier semaphores. Data moves between devices by JAX's collectives and lax.ppermute only.
A program may use at most 192 MiB of HBM per device.

v0:
```python
import math

import jax
import jax.numpy as jnp
from jax import lax
from jax.sharding import PartitionSpec as P

FD = 256
FHID = 512
WINDOW = 512
NS_STEPS = 5


coef_a = 3.4445
coef_b = -4.775
coef_c = 2.0315


def shifted(block, axis, distance):
    devices = range(lax.axis_size(axis))
    route = [(i - distance, i) for i in devices if i - distance in devices]
    return lax.ppermute(block, axis, route)


def attend_block(query_rows, key_all, value_all, offset, block_index, span):
    first_row = block_index * span
    scale = 1.0 / math.sqrt(query_rows.shape[-1])
    scores = (
        jnp.einsum("qhe,khe->hqk", query_rows, key_all, preferred_element_type=jnp.float32) * scale
    )
    query_pos = offset + first_row + jnp.arange(span, dtype=jnp.int32)[:, None]
    key_pos = offset + first_row - span + jnp.arange(2 * span, dtype=jnp.int32)[None, :]
    distance = query_pos - key_pos
    valid_mask = (distance >= 0) & (distance < span) & (key_pos >= 0)
    scores = jnp.where(valid_mask[None], scores, -1e30)
    row_max = jnp.max(scores, axis=-1, keepdims=True)
    exp_terms = jnp.exp(scores - row_max)
    probs = (exp_terms / jnp.sum(exp_terms, axis=-1, keepdims=True)).astype(jnp.bfloat16)
    return jnp.einsum("hqk,khe->qhe", probs, value_all, preferred_element_type=jnp.float32)


def head_gradient(key_part, value_part, rates, gate_w, up_w, down_w):
    gate_bf = gate_w.astype(jnp.bfloat16)
    up_bf = up_w.astype(jnp.bfloat16)
    down_bf = down_w.astype(jnp.bfloat16)
    gate_pre = jnp.dot(key_part, gate_bf, preferred_element_type=jnp.float32)
    up_pre = jnp.dot(key_part, up_bf, preferred_element_type=jnp.float32)
    sigmoid_gate = jax.nn.sigmoid(gate_pre)
    activated = gate_pre * sigmoid_gate
    hidden = (activated * up_pre).astype(jnp.bfloat16)
    scaled_v = (rates[:, 1:2] * value_part.astype(jnp.float32)).astype(jnp.bfloat16)
    back = jnp.dot(value_part, down_bf.T, preferred_element_type=jnp.float32)
    grad_gate = (
        rates[:, 0:1] * back * up_pre * sigmoid_gate * (1.0 + gate_pre * (1.0 - sigmoid_gate))
    ).astype(jnp.bfloat16)
    grad_up = (rates[:, 2:3] * back * activated).astype(jnp.bfloat16)
    delta_gate = jnp.dot(key_part.T, grad_gate, preferred_element_type=jnp.float32)
    delta_up = jnp.dot(key_part.T, grad_up, preferred_element_type=jnp.float32)
    delta_down = jnp.dot(scaled_v.T, hidden, preferred_element_type=jnp.float32)
    return jnp.stack([delta_gate, delta_up, delta_down])


def newton(ortho):
    best = lax.Precision.HIGHEST
    for _ in range(NS_STEPS):
        gram = jnp.einsum("bij,bkj->bik", ortho, ortho, precision=best)
        poly = coef_b * gram + coef_c * jnp.einsum("bij,bjk->bik", gram, gram, precision=best)
        ortho = coef_a * ortho + jnp.einsum("bij,bjk->bik", poly, ortho, precision=best)
    return ortho


def head_apply(query_part, gate_w, up_w, down_w, ortho):
    new_gate = (gate_w + ortho[0]).astype(jnp.bfloat16)
    new_up = (up_w + ortho[1]).astype(jnp.bfloat16)
    new_down = (down_w + ortho[2].T).astype(jnp.bfloat16)
    gate_pre = jnp.dot(query_part, new_gate, preferred_element_type=jnp.float32)
    up_pre = jnp.dot(query_part, new_up, preferred_element_type=jnp.float32)
    hidden = (jax.nn.silu(gate_pre) * up_pre).astype(jnp.bfloat16)
    return jnp.dot(hidden, new_down, preferred_element_type=jnp.float32)


def per_device(query_key, value_heads, fast_inputs, rate_logits, gate_fast, up_fast, down_fast):
    pair_rows, value_rows, fast_rows, logit_rows = (
        lax.all_to_all(query_key, "narrow", split_axis=1, concat_axis=0, tiled=True),
        lax.all_to_all(value_heads, "narrow", split_axis=1, concat_axis=0, tiled=True),
        lax.all_to_all(fast_inputs, "narrow", split_axis=1, concat_axis=0, tiled=True),
        lax.all_to_all(rate_logits, "narrow", split_axis=1, concat_axis=0, tiled=True),
    )
    rows_here = pair_rows.shape[0]
    head_size = pair_rows.shape[2] // 2
    query_rows = pair_rows[..., :head_size]
    key_rows = pair_rows[..., head_size:]
    tail_rows = jnp.stack([key_rows, value_rows])
    earlier = shifted(tail_rows, "wide", 1)
    key_all = jnp.concatenate([earlier[0], key_rows], axis=0)
    value_all = jnp.concatenate([earlier[1], value_rows], axis=0)
    offset = lax.axis_index("wide") * rows_here

    def one_block(block_index):
        return attend_block(query_rows, key_all, value_all, offset, block_index, WINDOW)

    count = rows_here // WINDOW
    window_out = lax.map(one_block, jnp.arange(count, dtype=jnp.int32)).reshape(
        rows_here, pair_rows.shape[1], head_size
    )
    fast_query = fast_rows[..., :FD]
    fast_key = fast_rows[..., FD : 2 * FD]
    fast_value = fast_rows[..., 2 * FD :]
    rates = jax.nn.softplus(logit_rows.astype(jnp.float32))
    grads = jax.vmap(head_gradient, in_axes=(1, 1, 1, 0, 0, 0))(
        fast_key, fast_value, rates, gate_fast, up_fast, down_fast
    )
    summed = lax.psum(grads, "wide")
    squares = jnp.sum(summed * summed, axis=(2, 3), keepdims=True)
    normed = summed / jnp.sqrt(squares + 1e-06)
    ortho = newton(normed.reshape(-1, FD, FHID)).reshape(normed.shape)
    fast_out = jax.vmap(head_apply, in_axes=(1, 0, 0, 0, 0), out_axes=1)(
        fast_query, gate_fast, up_fast, down_fast, ortho
    )
    return (window_out, fast_out)


def solution(mesh):
    return jax.shard_map(
        per_device,
        mesh=mesh,
        in_specs=(
            P(("wide", "narrow"), None, None),
            P(("wide", "narrow"), None, None),
            P(("wide", "narrow"), None, None),
            P(("wide", "narrow"), None, None),
            P("narrow", None, None),
            P("narrow", None, None),
            P("narrow", None, None),
        ),
        out_specs=(P("wide", "narrow", None), P("wide", "narrow", None)),
        check_vma=False,
    )
```

profile of v0, /device:TPU:8, one launch (start us, length us, event | category | flops | bytes accessed | tf_op | source)
XLA Modules:
  0.0 798.4 jit_solution(17318733938072786640)
XLA Ops:
  7.2 1.3 copy.77
  8.5 12.6 %all-to-all-start.2 = ((bf16[32,16,3]{0,2,1:T(4,128)(2,1)}), bf16[32,16,3]{0,2,1:T(4,128)(2,1)S(1)}, u32[]{:S(2)}, u32[]{:S(2)}) async-start(bf16[32,16,3]{0,2,1:T(4,128)(2,1)} %copy.77), calls=%async_computation.2 | async-start | bytes 32768 | tf_op jit(solution)/shard_map/all_to_all | solution.py:87
  21.1 1.8 copy.73
  23.0 8.6 %all-to-all-done.2 = bf16[32,16,3]{0,2,1:T(4,128)(2,1)S(1)} async-done(((bf16[32,16,3]{0,2,1:T(4,128)(2,1)}), bf16[32,16,3]{0,2,1:T(4,128)(2,1)S(1)}, u32[]{:S(2)}, u32[]{:S(2)}) %all-to-all-start.2) | async-done | bytes 3104 | tf_op jit(solution)/shard_map/all_to_all | solution.py:87
  31.5 3.5 all-to-all-start.1
  35.1 2.1 copy.71
  37.2 12.9 %all-to-all-done.1 = bf16[32,32,128]{2,0,1:T(8,128)(2,1)S(1)} async-done(((bf16[32,32,128]{2,0,1:T(8,128)(2,1)}), bf16[32,32,128]{2,0,1:T(8,128)(2,1)S(1)}, u32[]{:S(2)}, u32[]{:S(2)}) %all-to-all-start.1) | async-done | bytes 262176 | tf_op jit(solution)/shard_map/all_to_all | solution.py:85
  50.1 7.2 all-to-all-start
  57.4 1.1 copy.79
  58.5 24.6 %all-to-all-done = bf16[32,32,256]{2,0,1:T(8,128)(2,1)S(1)} async-done(((bf16[32,32,256]{2,0,1:T(8,128)(2,1)}), bf16[32,32,256]{2,0,1:T(8,128)(2,1)S(1)}, u32[]{:S(2)}, u32[]{:S(2)}) %all-to-all-start) | async-done | bytes 524320 | tf_op jit(solution)/shard_map/all_to_all | solution.py:84
  83.1 7.5 all-to-all-start.3
  90.9 1.0 copy.104
  92.0 1.6 fusion.5
  93.9 0.8 pad_maximum_fusion
  94.7 3.5 collective-permute-start
  98.2 27.4 %all-to-all-done.3 = bf16[32,16,768]{2,0,1:T(8,128)(2,1)S(1)} async-done(((bf16[32,16,768]{2,0,1:T(8,128)(2,1)}), bf16[32,16,768]{2,0,1:T(8,128)(2,1)S(1)}, u32[]{:S(2)}, u32[]{:S(2)}) %all-to-all-start.3) | async-done | bytes 786464 | tf_op jit(solution)/shard_map/all_to_all | solution.py:86
  126.2 0.4 copy-done.6
  126.6 0.3 fusion.60
  127.0 0.6 convolution_bitcast_fusion.3
  127.6 0.5 convolution_bitcast_fusion.4
  128.1 0.7 convolution_bitcast_fusion.5
  128.8 1.2 maximum_bitcast_fusion
  130.1 1.1 slice_bitcast_fusion.6
  131.2 0.7 fusion.38
  131.9 0.3 copy-done.8
  132.2 2.7 fusion.81
  135.0 0.5 fusion.22
  135.5 1.0 copy.106
  136.5 620.9 %all-reduce.2.cloned.1.call-done = f32[1,3,256,512]{2,3,1,0:T(8,128)} async-done(((f32[1,3,256,512]{2,3,1,0:T(8,128)}), f32[1,3,256,512]{2,3,1,0:T(8,128)}) %all-reduce.2.cloned.1.call-update) | async-done | bytes 1572880 | tf_op jit(solution)/shard_map/psum | solution.py:113
  757.4 1.8 multiply_reduce_fusion
  759.3 2.8 fusion.10
  762.1 0.9 fusion.21
  763.0 1.7 fusion.12
  764.7 2.8 fusion.82
  767.5 0.9 fusion.20
  768.5 1.7 multiply_add_fusion.2
  770.2 3.0 fusion.83
  773.2 0.9 fusion.19
  774.1 1.7 multiply_add_fusion.1
  775.9 2.8 fusion.84
  778.6 0.9 fusion.18
  779.6 1.7 multiply_add_fusion
  781.3 3.0 fusion.85
  784.3 0.9 fusion.17
  785.3 1.7 add_bitcast_fusion
  787.0 1.3 convolution_bitcast_fusion.1
  788.3 2.0 convolution_bitcast_fusion.2
  790.2 1.3 copy.107
  (34 shorter events, 1.3 us)
Async XLA Ops:
  8.5 23.1 %all-to-all-start.2 = ((bf16[32,16,3]{0,2,1:T(4,128)(2,1)}), bf16[32,16,3]{0,2,1:T(4,128)(2,1)S(1)}, u32[]{:S(2)}, u32[]{:S(2)}) async-start(bf16[32,16,3]{0,2,1:T(4,128)(2,1)} %copy.77), calls=%async_computation.2 | async-start | bytes 32768 | tf_op jit(solution)/shard_map/all_to_all | solution.py:87
  21.1 36.2 %copy-start.5 = (bf16[32,16,768]{2,1,0:T(8,128)(2,1)S(1)}, bf16[32,16,768]{2,1,0:T(8,128)(2,1)}, u32[]{:S(2)}) copy-start(bf16[32,16,768]{2,1,0:T(8,128)(2,1)} %param.9) | copy-start | bytes 2359300
  31.5 18.6 %all-to-all-start.1 = ((bf16[32,32,128]{2,0,1:T(8,128)(2,1)}), bf16[32,32,128]{2,0,1:T(8,128)(2,1)S(1)}, u32[]{:S(2)}, u32[]{:S(2)}) async-start(bf16[32,32,128]{2,0,1:T(8,128)(2,1)} %copy.73), calls=%async_computation.1 | async-start | bytes 524288 | tf_op jit(solution)/shard_map/all_to_all | solution.py:85
  50.1 33.0 %all-to-all-start = ((bf16[32,32,256]{2,0,1:T(8,128)(2,1)}), bf16[32,32,256]{2,0,1:T(8,128)(2,1)S(1)}, u32[]{:S(2)}, u32[]{:S(2)}) async-start(bf16[32,32,256]{2,0,1:T(8,128)(2,1)} %copy.71), calls=%async_computation | async-start | bytes 1048576 | tf_op jit(solution)/shard_map/all_to_all | solution.py:84
  57.3 33.4 %copy-start.1 = (f32[1,256,512]{2,1,0:T(8,128)S(1)}, f32[1,256,512]{2,1,0:T(8,128)}, u32[]{:S(2)}) copy-start(f32[1,256,512]{2,1,0:T(8,128)} %param.11) | copy-start | bytes 1572868
  58.5 32.5 %copy-start = (f32[1,256,512]{2,1,0:T(8,128)S(1)}, f32[1,256,512]{2,1,0:T(8,128)}, u32[]{:S(2)}) copy-start(f32[1,256,512]{2,1,0:T(8,128)} %param.12) | copy-start | bytes 1572868
  83.1 42.5 %all-to-all-start.3 = ((bf16[32,16,768]{2,0,1:T(8,128)(2,1)}), bf16[32,16,768]{2,0,1:T(8,128)(2,1)S(1)}, u32[]{:S(2)}, u32[]{:S(2)}) async-start(bf16[32,16,768]{2,0,1:T(8,128)(2,1)} %copy.79), calls=%async_computation.3 | async-start | bytes 1572864 | tf_op jit(solution)/shard_map/all_to_all | solution.py:86
  90.7 666.7 %all-reduce.2.cloned.1.call-start = ((), (), s32[]{:S(2)}) async-start(), calls=%async_computation.4 | async-start | bytes 3145728 | tf_op jit(solution)/shard_map/psum | solution.py:113
  93.8 1.0 copy-start.3
  94.7 35.4 %collective-permute-start = (bf16[2,512,2,128]{3,1,2,0:T(8,128)(2,1)}, bf16[2,512,2,128]{3,1,2,0:T(8,128)(2,1)}, u32[]{:S(2)}, u32[]{:S(2)}) collective-permute-start(bf16[2,512,2,128]{3,1,2,0:T(8,128)(2,1)} %pad_maximum_fusion), channel_id=1, source_target_pairs={{0,16},{16,32},{32,48},{48,64},{64,80},{80,96},{96,112},{112,128},... | collective-permute-start | bytes 1572872 | tf_op jit(solution)/shard_map/ppermute | solution.py:22
  125.6 1.0 copy-start.6
  131.2 1.0 copy-start.8
  132.2 2.7 copy-start.4
  757.4 1.9 copy-start.2
  787.0 1.3 copy-start.7
Sparse Core Ops, SparseCore 0:
  130.2 627.1 all-reduce.1
where the time goes:
time: 799 us; the launch traced here: 798 us
  waiting for transfers between devices  694 us (87%)
  matrix products  34.8 us (4%)
  starting transfers between devices  34.4 us (4%)
  between operations  14.4 us (2%)
  local copies, waits for them, and re-layouts  12.1 us (2%)
  other arithmetic  8.24 us (1%)
    psum x1, waiting for transfers between devices, per_device(): summed = lax.psum(grads, 'wide')  621 us
    all_to_all x1, waiting for transfers between devices, per_device(): lax.all_to_all(fast_inputs, 'narrow', split_axis=1, concat_axis=0, tiled=...  27.4 us
    all_to_all x1, waiting for transfers between devices, per_device(): lax.all_to_all(query_key, 'narrow', split_axis=1, concat_axis=0, tiled=True)  24.6 us
  transfers between devices with their start and end apart: 6, of which 5 were waited for; matrix products, arithmetic and copies ran while one was open for 2% of the time, Pallas kernels for 0%

commit v1 on v0

v1 whole, which is shorter than its diff:
```python
import math

import jax
import jax.numpy as jnp
from jax import lax
from jax.sharding import PartitionSpec as P

FD = 256
FHID = 512
WINDOW = 512
NS_STEPS = 5
LANES = 128

coef_a = 3.4445
coef_b = -4.775
coef_c = 2.0315

XS, HALVES, YS = 4, 2, 4
PLANE = XS * YS


def wide_index(x, half, y):
    return (x * HALVES + half) * YS + y


PLANES = [[wide_index(x, half, y) for x in range(XS) for y in range(YS)] for half in range(HALVES)]
SWAP = [
    (wide_index(x, half, y), wide_index(x, 1 - half, y))
    for x in range(XS)
    for half in range(HALVES)
    for y in range(YS)
]


def attend(query, key_all, value_all, offset):
    scale = 1.0 / math.sqrt(query.shape[-1])
    span = query.shape[1]
    scores = jnp.einsum("hqe,hke->hqk", query, key_all, preferred_element_type=jnp.float32) * scale
    query_pos = offset + jnp.arange(span, dtype=jnp.int32)[:, None]
    key_pos = offset - span + jnp.arange(2 * span, dtype=jnp.int32)[None, :]
    distance = query_pos - key_pos
    valid_mask = (distance >= 0) & (distance < span) & (key_pos >= 0)
    scores = jnp.where(valid_mask[None], scores, -1e30)
    row_max = jnp.max(scores, axis=-1, keepdims=True)
    exp_terms = jnp.exp(scores - row_max)
    probs = (exp_terms / jnp.sum(exp_terms, axis=-1, keepdims=True)).astype(jnp.bfloat16)
    return jnp.einsum("hqk,hke->qhe", probs, value_all, preferred_element_type=jnp.float32)


def head_gradient(key_part, value_part, rates, gate_w, up_w, down_w):
    gate_bf = gate_w.astype(jnp.bfloat16)
    up_bf = up_w.astype(jnp.bfloat16)
    down_bf = down_w.astype(jnp.bfloat16)
    gate_pre = jnp.dot(key_part, gate_bf, preferred_element_type=jnp.float32)
    up_pre = jnp.dot(key_part, up_bf, preferred_element_type=jnp.float32)
    sigmoid_gate = jax.nn.sigmoid(gate_pre)
    activated = gate_pre * sigmoid_gate
    hidden = (activated * up_pre).astype(jnp.bfloat16)
    scaled_v = (rates[:, 1:2] * value_part.astype(jnp.float32)).astype(jnp.bfloat16)
    back = jnp.dot(value_part, down_bf.T, preferred_element_type=jnp.float32)
    grad_gate = (
        rates[:, 0:1] * back * up_pre * sigmoid_gate * (1.0 + gate_pre * (1.0 - sigmoid_gate))
    ).astype(jnp.bfloat16)
    grad_up = (rates[:, 2:3] * back * activated).astype(jnp.bfloat16)
    delta_gate = jnp.dot(key_part.T, grad_gate, preferred_element_type=jnp.float32)
    delta_up = jnp.dot(key_part.T, grad_up, preferred_element_type=jnp.float32)
    delta_down = jnp.dot(scaled_v.T, hidden, preferred_element_type=jnp.float32)
    return jnp.stack([delta_gate, delta_up, delta_down])


def block_sum(grads):
    rows = FD // PLANE
    most = jnp.max(jnp.abs(grads), axis=(1, 2))
    power = jnp.floor(jnp.log2(jnp.maximum(most, 1e-30)))
    scaled = (grads * jnp.exp2(13.0 - power)[:, None, None]).astype(jnp.float16)
    pieces = scaled.reshape(3, PLANE, rows, FHID // LANES, LANES).transpose(1, 0, 3, 2, 4)
    pieces = pieces.reshape(PLANE, 3 * FHID // LANES * rows, LANES)
    count = pieces.shape[1]
    tag = jnp.zeros((16, LANES), jnp.float16).at[:3, :].set(
        jnp.broadcast_to(power.astype(jnp.float16)[:, None], (3, LANES))
    )
    sent = jnp.concatenate([pieces, jnp.broadcast_to(tag, (PLANE, 16, LANES))], axis=1)
    got = lax.all_to_all(sent, "wide", 0, 0, tiled=True, axis_index_groups=PLANES)
    powers = got[:, count : count + 3, 0].astype(jnp.float32)
    top = jnp.max(powers, axis=0)
    parts = got[:, :count].astype(jnp.float32).reshape(PLANE, 3, -1, LANES)
    half = jnp.sum(parts * (jnp.exp2(powers - top) * 0.0625)[:, :, None, None], axis=0)
    tag = jnp.zeros((16, LANES), jnp.float16).at[:3, :].set(
        jnp.broadcast_to(top.astype(jnp.float16)[:, None], (3, LANES))
    )
    sent = jnp.concatenate([half.astype(jnp.float16).reshape(count, LANES), tag], axis=0)
    other = lax.ppermute(sent, "wide", SWAP)
    other_top = other[count : count + 3, 0].astype(jnp.float32)
    both = jnp.maximum(top, other_top)
    whole = half * (jnp.exp2(top - both) * 0.5)[:, None, None]
    whole = whole + other[:count].astype(jnp.float32).reshape(3, -1, LANES) * (
        jnp.exp2(other_top - both) * 0.5
    )[:, None, None]
    every = lax.all_gather(
        whole.astype(jnp.float16).reshape(count, LANES), "wide", axis_index_groups=PLANES
    )
    every = every.reshape(PLANE, 3, FHID // LANES, rows, LANES).transpose(1, 0, 3, 2, 4)
    return every.reshape(3, FD, FHID).astype(jnp.float32) * jnp.exp2(both - 8.0)[:, None, None]


def newton(ortho):
    best = lax.Precision.HIGH
    for _ in range(NS_STEPS):
        gram = jnp.einsum("bij,bkj->bik", ortho, ortho, precision=best)
        poly = coef_b * gram + coef_c * jnp.einsum("bij,bjk->bik", gram, gram, precision=best)
        ortho = coef_a * ortho + jnp.einsum("bij,bjk->bik", poly, ortho, precision=best)
    return ortho


def head_apply(query_part, gate_w, up_w, down_w, ortho):
    new_gate = (gate_w + ortho[0]).astype(jnp.bfloat16)
    new_up = (up_w + ortho[1]).astype(jnp.bfloat16)
    new_down = (down_w + ortho[2].T).astype(jnp.bfloat16)
    gate_pre = jnp.dot(query_part, new_gate, preferred_element_type=jnp.float32)
    up_pre = jnp.dot(query_part, new_up, preferred_element_type=jnp.float32)
    hidden = (jax.nn.silu(gate_pre) * up_pre).astype(jnp.bfloat16)
    return jnp.dot(hidden, new_down, preferred_element_type=jnp.float32)


def per_device(query_key, value_heads, fast_inputs, rate_logits, gate_fast, up_fast, down_fast):
    group = lax.axis_size("narrow")
    rows = query_key.shape[0]
    own = query_key.shape[1] // group
    span = rows * group
    pair = query_key.reshape(rows, group, own, 2, LANES)
    query = pair[:, :, :, 0].transpose(1, 2, 0, 3)
    key = pair[:, :, :, 1].transpose(1, 2, 0, 3)
    value = value_heads.reshape(rows, group, own, LANES).transpose(1, 2, 0, 3)
    fast = fast_inputs.reshape(rows, group, 6, LANES).transpose(1, 2, 0, 3)
    logits = jnp.pad(rate_logits.transpose(1, 2, 0), ((0, 0), (0, 13), (0, LANES - rows)))
    first = jnp.concatenate([key, value, fast[:, 2:]], axis=1)
    blocks = first.shape[1]
    first = jnp.concatenate([first.reshape(group, blocks * rows, LANES), logits], axis=1)
    second = jnp.concatenate([query, fast[:, :2]], axis=1)

    first = lax.all_to_all(first, "narrow", 0, 0, tiled=True)
    second = lax.all_to_all(second, "narrow", 0, 0, tiled=True)

    parts = first[:, : blocks * rows].reshape(group, blocks, rows, LANES)
    logit_rows = first[:, blocks * rows : blocks * rows + 3, :rows]
    rates = jax.nn.softplus(logit_rows.transpose(0, 2, 1).reshape(span, 3).astype(jnp.float32))
    fast_key = parts[:, 4:6].transpose(0, 2, 1, 3).reshape(span, FD)
    fast_value = parts[:, 6:8].transpose(0, 2, 1, 3).reshape(span, FD)
    grads = head_gradient(fast_key, fast_value, rates, gate_fast[0], up_fast[0], down_fast[0])

    tail = parts[:, :4]
    devices = lax.axis_size("wide")
    earlier = lax.ppermute(tail, "wide", [(i, i + 1) for i in range(devices - 1)])
    near = tail.transpose(1, 0, 2, 3).reshape(4, span, LANES)
    far = earlier.transpose(1, 0, 2, 3).reshape(4, span, LANES)
    both = jnp.concatenate([far, near], axis=1)

    summed = block_sum(grads)
    squares = jnp.sum(summed * summed, axis=(1, 2), keepdims=True)
    ortho = newton(summed / jnp.sqrt(squares + 1e-06))

    chunks = second.transpose(1, 0, 2, 3).reshape(4, span, LANES)
    offset = lax.axis_index("wide") * span
    window_out = attend(chunks[:2], both[:2], both[2:], offset)
    fast_query = second[:, 2:].transpose(0, 2, 1, 3).reshape(span, FD)
    fast_out = head_apply(fast_query, gate_fast[0], up_fast[0], down_fast[0], ortho)
    return (window_out, fast_out[:, None, :])


def solution(mesh):
    return jax.shard_map(
        per_device,
        mesh=mesh,
        in_specs=(
            P(("wide", "narrow"), None, None),
            P(("wide", "narrow"), None, None),
            P(("wide", "narrow"), None, None),
            P(("wide", "narrow"), None, None),
            P("narrow", None, None),
            P("narrow", None, None),
            P("narrow", None, None),
        ),
        out_specs=(P("wide", "narrow", None), P("wide", "narrow", None)),
        check_vma=False,
    )
```

time: 799 us -> 243 us (0.30)
  the two profiles are of different devices: /device:TPU:8 before, /device:TPU:32 now
where the time goes in v1:
time: 243 us
  waiting for transfers between devices  77.7 us (32%)
  starting transfers between devices  63.8 us (26%)
  blocking collectives  38.2 us (16%)
  matrix products  28 us (12%)
  local copies, waits for them, and re-layouts  21.4 us (9%)
  other arithmetic  12.4 us (5%)
    all_to_all x1, waiting for transfers between devices, per_device(): first = lax.all_to_all(first, 'narrow', 0, 0, tiled=True)  45.3 us
    all_gather x1, blocking collectives, block_sum(): lax.all_gather(whole.astype(jnp.float16).reshape(count, LANES), 'wide', a...  38.2 us
    ppermute x1, starting transfers between devices, block_sum(): other = lax.ppermute(sent, 'wide', SWAP)  27.7 us
    all_to_all x1, waiting for transfers between devices, per_device(): second = lax.all_to_all(second, 'narrow', 0, 0, tiled=True)  21.9 us
    all_to_all x1, starting transfers between devices, per_device(): second = lax.all_to_all(second, 'narrow', 0, 0, tiled=True)  12.8 us
    all_to_all x1, starting transfers between devices, block_sum(): lax.all_to_all(sent, 'wide', 0, 0, tiled=True, axis_index_groups=PLANES)  10.8 us
    all_to_all x1, waiting for transfers between devices, block_sum(): lax.all_to_all(sent, 'wide', 0, 0, tiled=True, axis_index_groups=PLANES)  10.5 us
    all_to_all x1, starting transfers between devices, per_device(): first = lax.all_to_all(first, 'narrow', 0, 0, tiled=True)  8.19 us
  transfers between devices with their start and end apart: 5, of which 3 were waited for; matrix products, arithmetic and copies ran while one was open for 11% of the time, Pallas kernels for 0%

profile of v1, /device:TPU:32, one launch (start us, length us, event | category | flops | bytes accessed | tf_op | source)
XLA Modules:
  0.0 242.7 jit_solution(5184427491178675906)
XLA Ops:
  0.6 1.2 reshape.260
  1.8 0.7 fusion.100
  2.9 0.8 copy-done.10
  3.7 0.9 reshape.262
  5.3 1.0 copy.141
  6.4 12.8 %all-to-all-start.1 = ((bf16[16,4,32,128]{3,1,2,0:T(4,128)(2,1)}), bf16[16,4,32,128]{3,1,2,0:T(4,128)(2,1)S(1)}, u32[]{:S(2)}, u32[]{:S(2)}) async-start(bf16[16,4,32,128]{3,1,2,0:T(4,128)(2,1)} %copy.141), calls=%async_computation.1 | async-start | bytes 1048576 | tf_op jit(solution)/shard_map/all_to_all | solution.py:142
  19.7 0.9 pad_maximum_fusion
  21.3 1.1 fusion.20
  22.4 21.9 %all-to-all-done.1 = bf16[16,4,32,128]{3,1,2,0:T(4,128)(2,1)S(1)} async-done(((bf16[16,4,32,128]{3,1,2,0:T(4,128)(2,1)}), bf16[16,4,32,128]{3,1,2,0:T(4,128)(2,1)S(1)}, u32[]{:S(2)}, u32[]{:S(2)}) %all-to-all-start.1) | async-done | bytes 524320 | tf_op jit(solution)/shard_map/all_to_all | solution.py:142
  44.3 8.2 %all-to-all-start = ((bf16[16,272,128]{2,1,0:T(8,128)(2,1)}), bf16[16,272,128]{2,1,0:T(8,128)(2,1)S(1)}, u32[]{:S(2)}, u32[]{:S(2)}) async-start(bf16[16,272,128]{2,1,0:T(8,128)(2,1)} %fusion.20), calls=%async_computation | async-start | bytes 2228224 | tf_op jit(solution)/shard_map/all_to_all | solution.py:141
  52.5 1.0 copy.153
  53.5 1.4 fusion.7
  55.2 0.8 copy.142
  55.9 1.0 slice.135
  57.0 45.3 %all-to-all-done = bf16[16,272,128]{2,1,0:T(8,128)(2,1)S(1)} async-done(((bf16[16,272,128]{2,1,0:T(8,128)(2,1)}), bf16[16,272,128]{2,1,0:T(8,128)(2,1)S(1)}, u32[]{:S(2)}, u32[]{:S(2)}) %all-to-all-start) | async-done | bytes 1114144 | tf_op jit(solution)/shard_map/all_to_all | solution.py:141
  102.4 1.0 fusion.99
  104.1 0.8 copy.138
  104.9 4.3 %collective-permute-start = (bf16[16,4,32,128]{3,2,1,0:T(8,128)(2,1)}, bf16[16,4,32,128]{3,2,1,0:T(8,128)(2,1)}, u32[]{:S(2)}, u32[]{:S(2)}) collective-permute-start(bf16[16,4,32,128]{3,2,1,0:T(8,128)(2,1)} %get-tuple-element.44), channel_id=1, source_target_pairs={{0,16},{16,32},{32,48},{48,64},{64,80},{80,96},{96,112},{112,128},... | collective-permute-start | bytes 1572872 | tf_op jit(solution)/shard_map/ppermute | solution.py:153
  109.8 1.3 fusion.55
  111.9 2.3 fusion.43
  114.2 1.8 fusion.31
  116.0 0.8 copy-done.2
  117.2 1.2 fusion.12
  119.3 1.2 pad_maximum_fusion.1
  120.5 10.8 %all-to-all-start.2 = ((f16[16,208,128]{2,1,0:T(8,128)(2,1)}), f16[16,208,128]{2,1,0:T(8,128)(2,1)S(1)}, u32[]{:S(2)}, u32[]{:S(2)}) async-start(f16[16,208,128]{2,1,0:T(8,128)(2,1)} %pad_maximum_fusion.1), calls=%async_computation.2 | async-start | bytes 1703936 | tf_op jit(solution)/shard_map/all_to_all | solution.py:83
  131.3 1.1 copy.137
  132.4 0.7 fusion.37
  133.5 3.9 %fusion.102 = (f32[2,512]{1,0:T(2,128)S(1)}, f32[2,512,1024]{2,1,0:T(8,128)}) fusion(f32[2,512,1024]{2,1,0:T(8,128)S(1)} %fusion.37, pred[512,1024]{1,0:T(8,128)(4,1)S(1)} %copy-done.12), kind=kOutput, calls=%fused_computation.153 | output fusion | flops 6292479 | bytes 8916992 | tf_op jit(solution)/shard_map/sub | solution.py:45
  137.4 10.5 %all-to-all-done.2 = f16[16,208,128]{2,1,0:T(8,128)(2,1)S(1)} async-done(((f16[16,208,128]{2,1,0:T(8,128)(2,1)}), f16[16,208,128]{2,1,0:T(8,128)(2,1)S(1)}, u32[]{:S(2)}, u32[]{:S(2)}) %all-to-all-start.2) | async-done | bytes 852000 | tf_op jit(solution)/shard_map/all_to_all | solution.py:83
  149.2 27.7 %collective-permute-start.1 = (f16[208,128]{0,1:T(8,128)(2,1)S(1)}, f16[208,128]{0,1:T(8,128)(2,1)S(1)}, u32[]{:S(2)}, u32[]{:S(2)}) collective-permute-start(f16[208,128]{0,1:T(8,128)(2,1)S(1)} %pad_maximum_fusion.3), channel_id=1, source_target_pairs={{0,64},{16,80},{32,96},{48,112},{64,0},{80,16},{96,32},{112,48},{1... | collective-permute-start | bytes 159752 | tf_op jit(solution)/shard_map/ppermute | solution.py:92
  176.9 3.1 %fusion.19 = f32[512,2,128]{0,2,1:T(8,128)S(1)} fusion(f32[2,512,1024]{2,1,0:T(8,128)} %get-tuple-element.57, f32[2,512]{1,0:T(2,128)S(1)} %get-tuple-element.56, bf16[4,512,128]{2,1,0:T(8,128)(2,1)S(1)} %bitcast.175, bf16[4,512,128]{2,1,0:T(8,128)(2,1)S(1)} %bitcast.177), kind=kOutput, calls=%fused_computation.42 | convolution fusion | flops 272629760 | bytes 5771264 | tf_op jit(solution)/shard_map/hqk,hke->qhe/dot_general | solution.py:47
  180.0 1.0 copy.154
  181.6 38.2 %all-gather = f16[3072,128]{1,0:T(8,128)(2,1)S(1)} all-gather(f16[192,128]{1,0:T(8,128)(2,1)S(1)} %copy.151), channel_id=2, replica_groups={{0,16,32,48,128,144,160,176,256,272,288,304,384,400,416,432},{64,80,96,..., dimensions={0}, use_global_device_ids=true | all-gather | bytes 835584 | tf_op jit(solution)/shard_map/all_gather | solution.py:99
  220.3 0.7 copy.152
  221.0 1.8 reshape.273
  222.8 3.0 %fusion.98 = f32[3,256,256]{2,1,0:T(8,128)S(1)} fusion(f32[3,256,512]{2,1,0:T(8,128)} %reshape.273, f32[3]{0:T(128)S(1)} %add_sqrt_fusion, f32[3]{0:T(128)S(1)} %get-tuple-element.48), kind=kOutput, calls=%fused_computation.149 | convolution fusion | flops 604766208 | bytes 2359320 | tf_op jit(solution)/shard_map/bij,bkj->bik/dot_general | solution.py:109
  226.5 0.8 copy-done.4
  227.3 1.1 multiply_add_fusion.4
  228.4 0.9 fusion.103
  230.0 1.0 multiply_add_fusion.3
  231.1 0.9 fusion.104
  232.6 1.0 multiply_add_fusion.2
  233.7 0.9 fusion.105
  235.3 1.0 multiply_add_fusion.1
  236.3 1.2 fusion.106
  238.2 1.0 multiply_add_fusion
  239.6 1.7 convolution_bitcast_fusion
  241.3 1.3 copy.155
  (89 shorter events, 12.0 us)
Async XLA Ops:
  2.5 1.1 copy-start.10
  5.3 14.2 %copy-start.14 = (bf16[32,16,3]{0,1,2:T(8,128)(2,1)S(1)}, bf16[32,16,3]{0,1,2:T(8,128)(2,1)}, u32[]{:S(2)}) copy-start(bf16[32,16,3]{0,1,2:T(8,128)(2,1)} %param.14) | copy-start | bytes 9220
  6.4 13.3 %copy-start.13 = (bf16[32,32,128]{2,1,0:T(8,128)(2,1)S(1)}, bf16[32,32,128]{2,1,0:T(8,128)(2,1)}, u32[]{:S(2)}) copy-start(bf16[32,32,128]{2,1,0:T(8,128)(2,1)} %param.12) | copy-start | bytes 786436
  6.4 37.9 %all-to-all-start.1 = ((bf16[16,4,32,128]{3,1,2,0:T(4,128)(2,1)}), bf16[16,4,32,128]{3,1,2,0:T(4,128)(2,1)S(1)}, u32[]{:S(2)}, u32[]{:S(2)}) async-start(bf16[16,4,32,128]{3,1,2,0:T(4,128)(2,1)} %copy.141), calls=%async_computation.1 | async-start | bytes 1048576 | tf_op jit(solution)/shard_map/all_to_all | solution.py:142
  22.4 30.1 %copy-start = (f32[1,512,256]{2,1,0:T(8,128)S(1)}, f32[1,512,256]{2,1,0:T(8,128)}, u32[]{:S(2)}) copy-start(f32[1,512,256]{2,1,0:T(8,128)} %param.17) | copy-start | bytes 1572868
  44.3 58.0 %all-to-all-start = ((bf16[16,272,128]{2,1,0:T(8,128)(2,1)}), bf16[16,272,128]{2,1,0:T(8,128)(2,1)S(1)}, u32[]{:S(2)}, u32[]{:S(2)}) async-start(bf16[16,272,128]{2,1,0:T(8,128)(2,1)} %fusion.20), calls=%async_computation | async-start | bytes 2228224 | tf_op jit(solution)/shard_map/all_to_all | solution.py:141
  102.4 6.8 %copy-start.1 = (f32[1,256,512]{2,1,0:T(8,128)S(1)}, f32[1,256,512]{2,1,0:T(8,128)}, u32[]{:S(2)}) copy-start(f32[1,256,512]{2,1,0:T(8,128)} %param.15) | copy-start | bytes 1572868
  104.1 5.4 %copy-start.11 = (f32[1,256,512]{2,1,0:T(8,128)S(1)}, f32[1,256,512]{2,1,0:T(8,128)}, u32[]{:S(2)}) copy-start(f32[1,256,512]{2,1,0:T(8,128)} %param.16) | copy-start | bytes 1572868
  104.9 26.4 %collective-permute-start = (bf16[16,4,32,128]{3,2,1,0:T(8,128)(2,1)}, bf16[16,4,32,128]{3,2,1,0:T(8,128)(2,1)}, u32[]{:S(2)}, u32[]{:S(2)}) collective-permute-start(bf16[16,4,32,128]{3,2,1,0:T(8,128)(2,1)} %get-tuple-element.44), channel_id=1, source_target_pairs={{0,16},{16,32},{32,48},{48,64},{64,80},{80,96},{96,112},{112,128},... | collective-permute-start | bytes 1572872 | tf_op jit(solution)/shard_map/ppermute | solution.py:153
  109.5 2.4 copy-start.5
  109.8 1.3 copy-start.7
  111.9 2.3 copy-start.6
  116.0 0.8 copy-start.2
  120.5 11.9 %copy-start.3 = (bf16[4,16,32,128]{3,2,1,0:T(8,128)(2,1)S(1)}, bf16[4,16,32,128]{3,2,1,0:T(8,128)(2,1)}, u32[]{:S(2)}) copy-start(bf16[4,16,32,128]{3,2,1,0:T(8,128)(2,1)} %copy.138) | copy-start | bytes 1572868
  120.5 11.9 %copy-start.9 = (bf16[2,16,32,128]{3,2,1,0:T(8,128)(2,1)S(1)}, bf16[2,16,32,128]{3,2,1,0:T(8,128)(2,1)}, u32[]{:S(2)}) copy-start(bf16[2,16,32,128]{3,2,1,0:T(8,128)(2,1)} %copy.142) | copy-start | bytes 786436
  120.5 27.3 %all-to-all-start.2 = ((f16[16,208,128]{2,1,0:T(8,128)(2,1)}), f16[16,208,128]{2,1,0:T(8,128)(2,1)S(1)}, u32[]{:S(2)}, u32[]{:S(2)}) async-start(f16[16,208,128]{2,1,0:T(8,128)(2,1)} %pad_maximum_fusion.1), calls=%async_computation.2 | async-start | bytes 1703936 | tf_op jit(solution)/shard_map/all_to_all | solution.py:83
  132.4 1.0 copy-start.12
  149.2 31.9 %collective-permute-start.1 = (f16[208,128]{0,1:T(8,128)(2,1)S(1)}, f16[208,128]{0,1:T(8,128)(2,1)S(1)}, u32[]{:S(2)}, u32[]{:S(2)}) collective-permute-start(f16[208,128]{0,1:T(8,128)(2,1)S(1)} %pad_maximum_fusion.3), channel_id=1, source_target_pairs={{0,64},{16,80},{32,96},{48,112},{64,0},{80,16},{96,32},{112,48},{1... | collective-permute-start | bytes 159752 | tf_op jit(solution)/shard_map/ppermute | solution.py:92
  225.8 1.4 copy-start.4
  238.2 1.1 copy-start.8

commit v2 on v1

v2 whole, which is shorter than its diff:
```python
import math

import jax
import jax.numpy as jnp
from jax import lax
from jax.experimental import pallas as pl
from jax.experimental.pallas import tpu as pltpu
from jax.sharding import PartitionSpec as P

FD = 256
FHID = 512
WINDOW = 512
NS_STEPS = 5
LANES = 128
TOK = 32

coef_a = 3.4445
coef_b = -4.775
coef_c = 2.0315

XS, HALVES, YS = 4, 2, 4
PLANE = XS * YS
VMEM_LIMIT = 48 * 1024 * 1024


def dot(a, b, dims=((1,), (0,))):
    return lax.dot_general(a, b, (dims, ((), ())), preferred_element_type=jnp.float32)


def block_rows(ref, index, count):
    group = ref.shape[0]
    parts = [
        ref[:, (index + i) * TOK : (index + i + 1) * TOK, :].reshape(group * TOK, LANES)
        for i in range(count)
    ]
    return parts[0] if count == 1 else jnp.concatenate(parts, axis=1)


def gradient_kernel(first, gate, up, down, out):
    group = first.shape[0]
    span = group * TOK
    logits = first[:, 8 * TOK : 8 * TOK + 16, :].astype(jnp.float32)
    rate_blocks = []
    for source in range(group):
        turned = logits[source].T[:TOK]
        rate_blocks.append(jnp.maximum(turned, 0.0) + jnp.log1p(jnp.exp(-jnp.abs(turned))))
    rates = jnp.concatenate(rate_blocks, axis=0)
    key = block_rows(first, 4, 2)
    value = block_rows(first, 6, 2)
    gate_bf = gate[...].astype(jnp.bfloat16)
    up_bf = up[...].astype(jnp.bfloat16)
    down_bf = down[...].astype(jnp.bfloat16)
    totals = [None, None, None]
    half = span // 2
    for part in range(2):
        rows = slice(part * half, (part + 1) * half)
        key_part, value_part, rate = key[rows], value[rows], rates[rows]
        gate_pre = dot(key_part, gate_bf)
        up_pre = dot(key_part, up_bf)
        back = dot(value_part, down_bf, ((1,), (1,)))
        sigmoid_gate = 1.0 / (1.0 + jnp.exp(-gate_pre))
        activated = gate_pre * sigmoid_gate
        hidden = (activated * up_pre).astype(jnp.bfloat16)
        scaled_v = (rate[:, 1:2] * value_part.astype(jnp.float32)).astype(jnp.bfloat16)
        grad_gate = (
            rate[:, 0:1] * back * up_pre * sigmoid_gate * (1.0 + gate_pre * (1.0 - sigmoid_gate))
        ).astype(jnp.bfloat16)
        grad_up = (rate[:, 2:3] * back * activated).astype(jnp.bfloat16)
        fresh = (
            dot(key_part, grad_gate, ((0,), (0,))),
            dot(key_part, grad_up, ((0,), (0,))),
            dot(scaled_v, hidden, ((0,), (0,))),
        )
        totals = [new if old is None else old + new for old, new in zip(totals, fresh)]
    rows = FD // PLANE
    row = lax.broadcasted_iota(jnp.int32, (16, LANES), 0)
    tag = jnp.zeros((16, LANES), jnp.float32)
    for matrix, total in enumerate(totals):
        most = jnp.max(jnp.max(jnp.abs(total), axis=0, keepdims=True), axis=1, keepdims=True)
        power = jnp.floor(jnp.log(jnp.maximum(most, 1e-30)) * 1.4426950408889634)
        scaled = total * jnp.exp((13.0 - power) * 0.6931471805599453)
        tag = jnp.where(row == matrix, power, tag)
        for column in range(FHID // LANES):
            start = (matrix * (FHID // LANES) + column) * rows
            out[:, start : start + rows, :] = scaled[
                :, column * LANES : (column + 1) * LANES
            ].reshape(PLANE, rows, LANES)
    out[:, 3 * FHID // LANES * rows :, :] = jnp.broadcast_to(tag[None], (PLANE, 16, LANES))


def attention_kernel(place, first, earlier, second, out):
    span = first.shape[0] * TOK
    scale = 1.0 / math.sqrt(LANES)
    tile = 128
    reach = span + tile
    row = lax.broadcasted_iota(jnp.int32, (tile, reach), 0)
    col = lax.broadcasted_iota(jnp.int32, (tile, reach), 1)
    band = (col > row) & (col - row <= span)
    begin = jnp.where(place[0] == 0, span, 0)
    heads = second.shape[1] // TOK // 2
    for head in range(heads):
        query = block_rows(second, head, 1)
        key = jnp.concatenate([block_rows(earlier, head, 1), block_rows(first, head, 1)], axis=0)
        value = jnp.concatenate(
            [block_rows(earlier, heads + head, 1), block_rows(first, heads + head, 1)], axis=0
        )
        for step in range(span // tile):
            low = step * tile
            scores = dot(query[low : low + tile], key[low : low + reach], ((1,), (1,))) * scale
            keep = band & (col + low >= begin)
            scores = jnp.where(keep, scores, -1e30)
            terms = jnp.exp(scores - jnp.max(scores, axis=1, keepdims=True))
            probs = (terms * (1.0 / jnp.sum(terms, axis=1, keepdims=True))).astype(jnp.bfloat16)
            out[pl.ds(low * heads + head, tile, stride=heads), :] = dot(
                probs, value[low : low + reach]
            )


def split(a):
    high = a.astype(jnp.bfloat16)
    return high, (a - high.astype(jnp.float32)).astype(jnp.bfloat16)


def orthogonal(ortho_all):
    for _ in range(NS_STEPS):
        grams, polys, nexts = [], [], []
        halves = [split(ortho) for ortho in ortho_all]
        for high, low in halves:
            cross = dot(high, low, ((1,), (1,)))
            grams.append(dot(high, high, ((1,), (1,))) + (cross + cross.T))
        for gram in grams:
            high, low = split(gram)
            square = dot(high, high) + (dot(high, low) + dot(low, high))
            polys.append(coef_b * gram + coef_c * square)
        for ortho, poly, (high, low) in zip(ortho_all, polys, halves):
            top, rest = split(poly)
            nexts.append(coef_a * ortho + (dot(top, high) + (dot(top, low) + dot(rest, high))))
        ortho_all = nexts
    return ortho_all


def apply_kernel(powers, every, gate, up, down, second, out):
    rows = FD // PLANE
    starts = []
    for matrix in range(3):
        columns = []
        for column in range(FHID // LANES):
            start = (matrix * (FHID // LANES) + column) * rows
            columns.append(every[:, start : start + rows, :].reshape(FD, LANES))
        total = jnp.concatenate(columns, axis=1)
        squares = jnp.sum(jnp.sum(total * total, axis=0, keepdims=True), axis=1, keepdims=True)
        factor = powers[matrix : matrix + 1, 0:1]
        starts.append(total * (factor / jnp.sqrt(squares * factor * factor + 1e-6)))
    ortho = orthogonal(starts)
    new_gate = (gate[...] + ortho[0]).astype(jnp.bfloat16)
    new_up = (up[...] + ortho[1]).astype(jnp.bfloat16)
    new_down = (down[...] + ortho[2].T).astype(jnp.bfloat16)
    query = block_rows(second, 2, 2)
    gate_pre = dot(query, new_gate)
    up_pre = dot(query, new_up)
    hidden = (gate_pre * (1.0 / (1.0 + jnp.exp(-gate_pre))) * up_pre).astype(jnp.bfloat16)
    result = dot(hidden, new_down)
    span = result.shape[0]
    for column in range(FD // LANES):
        out[pl.ds(column, span, stride=FD // LANES), :] = result[
            :, column * LANES : (column + 1) * LANES
        ]


def call(kernel, shape, operands, flops, scalars=0):
    vmem = pl.BlockSpec(memory_space=pltpu.VMEM)
    smem = pl.BlockSpec(memory_space=pltpu.SMEM)
    return pl.pallas_call(
        kernel,
        out_shape=jax.ShapeDtypeStruct(shape, jnp.float32),
        in_specs=[smem] * scalars + [vmem] * (len(operands) - scalars),
        out_specs=vmem,
        compiler_params=pltpu.CompilerParams(vmem_limit_bytes=VMEM_LIMIT),
        cost_estimate=pl.CostEstimate(flops=flops, bytes_accessed=4 << 20, transcendentals=0),
    )(*operands)


def wide_index(x, half, y):
    return (x * HALVES + half) * YS + y


PLANES = [[wide_index(x, half, y) for x in range(XS) for y in range(YS)] for half in range(HALVES)]
SWAP = [
    (wide_index(x, half, y), wide_index(x, 1 - half, y))
    for x in range(XS)
    for half in range(HALVES)
    for y in range(YS)
]


def tag_rows(power):
    wide = jnp.broadcast_to(power.astype(jnp.float16)[:, None], (3, LANES))
    return jnp.concatenate([wide, jnp.zeros((13, LANES), jnp.float16)], axis=0)


def per_device(query_key, value_heads, fast_inputs, rate_logits, gate_fast, up_fast, down_fast):
    group = lax.axis_size("narrow")
    rows = query_key.shape[0]
    own = query_key.shape[1] // group
    span = rows * group
    pair = query_key.reshape(rows, group, own, 2, LANES)
    query = pair[:, :, :, 0].transpose(1, 2, 0, 3)
    key = pair[:, :, :, 1].transpose(1, 2, 0, 3)
    value = value_heads.reshape(rows, group, own, LANES).transpose(1, 2, 0, 3)
    fast = fast_inputs.reshape(rows, group, 6, LANES).transpose(1, 2, 0, 3)
    logits = jnp.pad(rate_logits.transpose(1, 2, 0), ((0, 0), (0, 13), (0, LANES - rows)))
    first = jnp.concatenate([key, value, fast[:, 2:]], axis=1)
    blocks = first.shape[1]
    first = jnp.concatenate([first.reshape(group, blocks * rows, LANES), logits], axis=1)
    second = jnp.concatenate([query, fast[:, :2]], axis=1).reshape(group, 4 * rows, LANES)

    first = lax.all_to_all(first, "narrow", 0, 0, tiled=True)
    devices = lax.axis_size("wide")
    earlier = lax.ppermute(
        first[:, : 4 * rows], "wide", [(i, i + 1) for i in range(devices - 1)]
    )

    weights = (gate_fast[0], up_fast[0], down_fast[0])
    count = 3 * FHID // LANES * FD // PLANE
    pieces = call(gradient_kernel, (PLANE, count + 16, LANES), (first, *weights), 1 << 30)
    got = lax.all_to_all(
        pieces.astype(jnp.float16), "wide", 0, 0, tiled=True, axis_index_groups=PLANES
    )
    second, got = lax.optimization_barrier((second, got))
    second = lax.all_to_all(second, "narrow", 0, 0, tiled=True)
    powers = got[:, count : count + 3, 0].astype(jnp.float32)
    top = jnp.max(powers, axis=0)
    parts = got[:, :count].astype(jnp.float32).reshape(PLANE, 3, -1, LANES)
    half = jnp.sum(parts * (jnp.exp2(powers - top) * 0.0625)[:, :, None, None], axis=0)
    sent = jnp.concatenate([half.astype(jnp.float16).reshape(count, LANES), tag_rows(top)], axis=0)
    other = lax.ppermute(sent, "wide", SWAP)
    other_top = other[count : count + 3, 0].astype(jnp.float32)
    both = jnp.maximum(top, other_top)
    whole = half * (jnp.exp2(top - both) * 0.5)[:, None, None]
    whole = whole + other[:count].astype(jnp.float32).reshape(3, -1, LANES) * (
        jnp.exp2(other_top - both) * 0.5
    )[:, None, None]
    every = lax.all_gather(
        whole.astype(jnp.float16).reshape(count, LANES), "wide", axis_index_groups=PLANES
    )
    factors = jnp.broadcast_to(
        jnp.concatenate([jnp.exp2(both - 8.0), jnp.zeros((5,), jnp.float32)])[:, None], (8, LANES)
    )
    fast_out = call(
        apply_kernel,
        (span * FD // LANES, LANES),
        (factors, every.astype(jnp.float32), *weights, second),
        10 << 30,
    )
    earlier, fast_out = lax.optimization_barrier((earlier, fast_out))
    place = lax.axis_index("wide").reshape(1)
    window_out = call(
        attention_kernel, (span * own, LANES), (place, first, earlier, second), 1 << 30, 1
    )
    return (window_out.reshape(span, own, LANES), fast_out.reshape(span, 1, FD))


def solution(mesh):
    return jax.shard_map(
        per_device,
        mesh=mesh,
        in_specs=(
            P(("wide", "narrow"), None, None),
            P(("wide", "narrow"), None, None),
            P(("wide", "narrow"), None, None),
            P(("wide", "narrow"), None, None),
            P("narrow", None, None),
            P("narrow", None, None),
            P("narrow", None, None),
        ),
        out_specs=(P("wide", "narrow", None), P("wide", "narrow", None)),
        check_vma=False,
    )
```

time: 243 us -> 216 us (0.89)
  the two profiles are of different devices: /device:TPU:32 before, /device:TPU:160 now
where the time goes in v2:
time: 216 us
  blocking collectives  121 us (56%)
  waiting for transfers between devices  32.1 us (15%)
  starting transfers between devices  28.6 us (13%)
  Pallas kernels  16.8 us (8%)
  local copies, waits for them, and re-layouts  12.4 us (6%)
  other arithmetic  3.73 us (2%)
    all_gather x1, blocking collectives, per_device(): lax.all_gather(whole.astype(jnp.float16).reshape(count, LANES), 'wide', a...  61.3 us
    all_to_all x1, blocking collectives, per_device(): first = lax.all_to_all(first, 'narrow', 0, 0, tiled=True)  60 us
    ppermute x1, waiting for transfers between devices, per_device(): other = lax.ppermute(sent, 'wide', SWAP)  19.5 us
    pallas_call x3, Pallas kernels, call(): pl.pallas_call(kernel, out_shape=jax.ShapeDtypeStruct(shape, jnp.float32)...  16.8 us
    all_to_all x1, waiting for transfers between devices, per_device(): lax.all_to_all(pieces.astype(jnp.float16), 'wide', 0, 0, tiled=True, axis...  12.6 us
    all_to_all x1, starting transfers between devices, per_device(): second = lax.all_to_all(second, 'narrow', 0, 0, tiled=True)  10.1 us
    ppermute x1, starting transfers between devices, per_device(): other = lax.ppermute(sent, 'wide', SWAP)  8.24 us
    all_to_all x1, starting transfers between devices, per_device(): lax.all_to_all(pieces.astype(jnp.float16), 'wide', 0, 0, tiled=True, axis...  7.05 us
  transfers between devices with their start and end apart: 4, of which 2 were waited for; matrix products, arithmetic and copies ran while one was open for 3% of the time, Pallas kernels for 5%

profile of v2, /device:TPU:160, one launch (start us, length us, event | category | flops | bytes accessed | tf_op | source)
XLA Modules:
  0.0 215.9 jit_solution(11648787317456715720)
XLA Ops:
  0.6 0.8 copy.78
  1.4 2.0 reshape.95
  3.4 0.3 slice.37
  3.7 0.1 reshape.93
  3.9 1.2 fusion.6
  5.1 0.8 copy_bitcast_fusion.1
  5.9 0.2 copy.64
  6.1 0.9 pad_maximum_fusion
  7.0 0.7 copy.65
  7.7 0.0 copy-start
  7.7 0.1 fusion.1
  7.8 60.0 %all_to_all.15.first = bf16[16,272,128]{2,1,0:T(8,128)(2,1)S(1)} all-to-all(bf16[16,272,128]{2,1,0:T(8,128)(2,1)S(1)} %fusion.1), channel_id=1, replica_groups=mesh['wide'=32,'narrow'=16] {'narrow'}, dimensions={0} | all-to-all | bytes 2228224 | tf_op jit(solution)/shard_map/all_to_all | solution.py:217
  67.8 1.8 shard_map.86
  69.5 1.0 convert_element_type.55
  70.6 7.0 %all-to-all-start.1 = ((f16[16,208,128]{2,1,0:T(8,128)(2,1)}), f16[16,208,128]{2,1,0:T(8,128)(2,1)S(1)}, u32[]{:S(2)}, u32[]{:S(2)}) async-start(f16[16,208,128]{2,1,0:T(8,128)(2,1)} %convert_element_type.55), calls=%async_computation.1 | async-start | bytes 1703936 | tf_op jit(solution)/shard_map/all_to_all | solution.py:226
  77.6 0.2 slice.40
  77.8 1.2 copy.77
  79.0 0.5 pad_maximum_fusion.1
  79.5 1.1 copy.69
  80.7 12.6 %all-to-all-done.1 = f16[16,208,128]{2,1,0:T(8,128)(2,1)S(1)} async-done(((f16[16,208,128]{2,1,0:T(8,128)(2,1)}), f16[16,208,128]{2,1,0:T(8,128)(2,1)S(1)}, u32[]{:S(2)}, u32[]{:S(2)}) %all-to-all-start.1) | async-done | bytes 852000 | tf_op jit(solution)/shard_map/all_to_all | solution.py:226
  93.3 10.1 %all-to-all-start.2 = ((bf16[16,128,128]{2,1,0:T(8,128)(2,1)}), bf16[16,128,128]{2,1,0:T(8,128)(2,1)}, u32[]{:S(2)}, u32[]{:S(2)}) async-start(bf16[16,128,128]{2,1,0:T(8,128)(2,1)} %bitcast.10), calls=%async_computation.2 | async-start | bytes 1048576 | tf_op jit(solution)/shard_map/all_to_all | solution.py:230
  103.4 0.1 pad.8.clone
  103.5 0.1 copy.70
  103.6 0.1 fusion.2
  103.7 0.1 fusion.5
  103.8 0.1 copy.71
  103.9 0.1 mul.67
  103.9 0.1 mul.68
  104.0 0.5 multiply_reduce_fusion
  104.5 0.1 pad.7.clone
  104.6 0.1 maximum_maximum_fusion
  104.7 8.2 %collective-permute-start.1 = (f16[208,128]{1,0:T(8,128)(2,1)S(1)}, f16[208,128]{1,0:T(8,128)(2,1)S(1)}, u32[]{:S(2)}, u32[]{:S(2)}) collective-permute-start(f16[208,128]{1,0:T(8,128)(2,1)S(1)} %maximum_maximum_fusion), channel_id=1, source_target_pairs={{0,64},{16,80},{32,96},{48,112},{64,0},{80,16},{96,32},{112,48},{1... | collective-permute-start | bytes 159752 | tf_op jit(solution)/shard_map/ppermute | solution.py:236
  113.0 0.8 slice.38
  113.8 3.3 %collective-permute-start = (bf16[16,128,128]{2,1,0:T(8,128)(2,1)}, bf16[16,128,128]{2,1,0:T(8,128)(2,1)}, u32[]{:S(2)}, u32[]{:S(2)}) collective-permute-start(bf16[16,128,128]{2,1,0:T(8,128)(2,1)} %slice.38), channel_id=1, source_target_pairs={{0,16},{16,32},{32,48},{48,64},{64,80},{80,96},{96,112},{112,128},... | collective-permute-start | bytes 1572872 | tf_op jit(solution)/shard_map/ppermute | solution.py:219
  117.1 19.5 %collective-permute-done.1 = f16[208,128]{1,0:T(8,128)(2,1)S(1)} collective-permute-done((f16[208,128]{1,0:T(8,128)(2,1)S(1)}, f16[208,128]{1,0:T(8,128)(2,1)S(1)}, u32[]{:S(2)}, u32[]{:S(2)}) %collective-permute-start.1) | collective-permute-done | bytes 53280 | tf_op jit(solution)/shard_map/ppermute | solution.py:236
  136.6 0.1 convert_reduce_fusion
  136.7 0.1 mul.77
  136.8 0.1 mul.78
  136.9 0.1 mul.72
  137.0 0.1 mul.73
  137.0 0.1 add_convert_fusion
  137.2 61.3 %all-gather = f16[3072,128]{1,0:T(8,128)(2,1)S(1)} all-gather(f16[192,128]{1,0:T(8,128)(2,1)S(1)} %add_convert_fusion), channel_id=2, replica_groups={{0,16,32,48,128,144,160,176,256,272,288,304,384,400,416,432},{64,80,96,..., dimensions={0}, use_global_device_ids=true | all-gather | bytes 835584 | tf_op jit(solution)/shard_map/all_gather | solution.py:243
  198.5 0.1 convert.1.every
  198.6 0.1 broadcast_in_dim.8.powers
  198.7 1.0 copy-done.2
  199.7 1.0 copy-done.4
  200.8 9.8 %shard_map.87 = f32[1024,128]{1,0:T(8,128)} custom-call(f32[8,128]{1,0:T(8,128)S(1)} %broadcast_in_dim.8.powers, f32[16,192,128]{2,1,0:T(8,128)S(1)} %convert.1.every, f32[256,512]{1,0:T(8,128)S(1)} %bitcast.35, f32[256,512]{1,0:T(8,128)S(1)} %bitcast.37, f32[512,256]{1,0:T(8,128)S(1)} %bitcast.39, bf16[16,128,128]{2,1,0:T(8,128)(2,1)} %all-to-all-done.2.second), custom_call_target="tpu_custom_call" | custom-call | flops 10737418240 | bytes 4194304 | tf_op jit(solution)/shard_map/pallas_call | solution.py:173
  210.6 5.3 %shard_map.88 = f32[1024,128]{1,0:T(8,128)} custom-call(s32[1]{0:T(128)} %bitcast.place, bf16[16,272,128]{2,1,0:T(8,128)(2,1)S(1)} %all_to_all.15.first, bf16[16,128,128]{2,1,0:T(8,128)(2,1)} %collective-permute-done.earlier, bf16[16,128,128]{2,1,0:T(8,128)(2,1)} %all-to-all-done.2.second), custom_call_target="tpu_custom_call" | custom-call | flops 1073741824 | bytes 4194304 | tf_op jit(solution)/shard_map/pallas_call | solution.py:173
  (19 shorter events, 0.1 us)
Async XLA Ops:
  0.6 3.1 %copy-start.5 = (bf16[32,32,256]{2,1,0:T(8,128)(2,1)S(1)}, bf16[32,32,256]{2,1,0:T(8,128)(2,1)}, u32[]{:S(2)}) copy-start(bf16[32,32,256]{2,1,0:T(8,128)(2,1)} %param.7) | copy-start | bytes 1572868
  3.9 2.2 %copy-start.6 = (bf16[32,32,128]{2,1,0:T(8,128)(2,1)S(1)}, bf16[32,32,128]{2,1,0:T(8,128)(2,1)}, u32[]{:S(2)}) copy-start(bf16[32,32,128]{2,1,0:T(8,128)(2,1)} %param.8) | copy-start | bytes 786436
  7.7 60.1 %copy-start = (f32[1,256,512]{2,1,0:T(8,128)S(1)}, f32[1,256,512]{2,1,0:T(8,128)}, u32[]{:S(2)}) copy-start(f32[1,256,512]{2,1,0:T(8,128)} %param.11) | copy-start | bytes 1572868
  7.7 60.1 %copy-start.1 = (f32[1,256,512]{2,1,0:T(8,128)S(1)}, f32[1,256,512]{2,1,0:T(8,128)}, u32[]{:S(2)}) copy-start(f32[1,256,512]{2,1,0:T(8,128)} %param.12) | copy-start | bytes 1572868
  7.7 60.1 %copy-start.3 = (f32[1,512,256]{2,1,0:T(8,128)S(1)}, f32[1,512,256]{2,1,0:T(8,128)}, u32[]{:S(2)}) copy-start(f32[1,512,256]{2,1,0:T(8,128)} %param.13) | copy-start | bytes 1572868
  70.6 22.7 %all-to-all-start.1 = ((f16[16,208,128]{2,1,0:T(8,128)(2,1)}), f16[16,208,128]{2,1,0:T(8,128)(2,1)S(1)}, u32[]{:S(2)}, u32[]{:S(2)}) async-start(f16[16,208,128]{2,1,0:T(8,128)(2,1)} %convert_element_type.55), calls=%async_computation.1 | async-start | bytes 1703936 | tf_op jit(solution)/shard_map/all_to_all | solution.py:226
  93.3 105.3 %all-to-all-start.2 = ((bf16[16,128,128]{2,1,0:T(8,128)(2,1)}), bf16[16,128,128]{2,1,0:T(8,128)(2,1)}, u32[]{:S(2)}, u32[]{:S(2)}) async-start(bf16[16,128,128]{2,1,0:T(8,128)(2,1)} %bitcast.10), calls=%async_computation.2 | async-start | bytes 1048576 | tf_op jit(solution)/shard_map/all_to_all | solution.py:230
  104.7 31.9 %collective-permute-start.1 = (f16[208,128]{1,0:T(8,128)(2,1)S(1)}, f16[208,128]{1,0:T(8,128)(2,1)S(1)}, u32[]{:S(2)}, u32[]{:S(2)}) collective-permute-start(f16[208,128]{1,0:T(8,128)(2,1)S(1)} %maximum_maximum_fusion), channel_id=1, source_target_pairs={{0,64},{16,80},{32,96},{48,112},{64,0},{80,16},{96,32},{112,48},{1... | collective-permute-start | bytes 159752 | tf_op jit(solution)/shard_map/ppermute | solution.py:236
  113.8 96.8 %collective-permute-start = (bf16[16,128,128]{2,1,0:T(8,128)(2,1)}, bf16[16,128,128]{2,1,0:T(8,128)(2,1)}, u32[]{:S(2)}, u32[]{:S(2)}) collective-permute-start(bf16[16,128,128]{2,1,0:T(8,128)(2,1)} %slice.38), channel_id=1, source_target_pairs={{0,16},{16,32},{32,48},{48,64},{64,80},{80,96},{96,112},{112,128},... | collective-permute-start | bytes 1572872 | tf_op jit(solution)/shard_map/ppermute | solution.py:219
  198.7 1.0 copy-start.2
  199.7 1.0 copy-start.4

commit v3 on v2

--- a/solution.py
+++ b/solution.py
@@ -39,14 +39,14 @@
 def gradient_kernel(first, gate, up, down, out):
     group = first.shape[0]
     span = group * TOK
-    logits = first[:, 8 * TOK : 8 * TOK + 16, :].astype(jnp.float32)
+    logits = first[:, 6 * TOK : 6 * TOK + 16, :].astype(jnp.float32)
     rate_blocks = []
     for source in range(group):
         turned = logits[source].T[:TOK]
         rate_blocks.append(jnp.maximum(turned, 0.0) + jnp.log1p(jnp.exp(-jnp.abs(turned))))
     rates = jnp.concatenate(rate_blocks, axis=0)
-    key = block_rows(first, 4, 2)
-    value = block_rows(first, 6, 2)
+    key = block_rows(first, 0, 2)
+    value = block_rows(first, 2, 2)
     gate_bf = gate[...].astype(jnp.bfloat16)
     up_bf = up[...].astype(jnp.bfloat16)
     down_bf = down[...].astype(jnp.bfloat16)
@@ -88,7 +88,9 @@
     out[:, 3 * FHID // LANES * rows :, :] = jnp.broadcast_to(tag[None], (PLANE, 16, LANES))
 
 
-def attention_kernel(place, first, earlier, second, out):
+def attention_kernel(
+    place, first, second, earlier_key, earlier_value, earlier_second, third, out
+):
     span = first.shape[0] * TOK
     scale = 1.0 / math.sqrt(LANES)
     tile = 128
@@ -97,12 +99,16 @@
     col = lax.broadcasted_iota(jnp.int32, (tile, reach), 1)
     band = (col > row) & (col - row <= span)
     begin = jnp.where(place[0] == 0, span, 0)
-    heads = second.shape[1] // TOK // 2
-    for head in range(heads):
-        query = block_rows(second, head, 1)
-        key = jnp.concatenate([block_rows(earlier, head, 1), block_rows(first, head, 1)], axis=0)
+    heads = 2
+    sources = (
+        (earlier_key, 0, earlier_value, 0, first, 4),
+        (earlier_second, 0, earlier_second, 1, second, 0),
+    )
+    for head, (far_key, far, far_value, other, near, at) in enumerate(sources):
+        query = block_rows(third, head, 1)
+        key = jnp.concatenate([block_rows(far_key, far, 1), block_rows(near, at, 1)], axis=0)
         value = jnp.concatenate(
-            [block_rows(earlier, heads + head, 1), block_rows(first, heads + head, 1)], axis=0
+            [block_rows(far_value, other, 1), block_rows(near, at + 1, 1)], axis=0
         )
         for step in range(span // tile):
             low = step * tile
@@ -139,7 +145,7 @@
     return ortho_all
 
 
-def apply_kernel(powers, every, gate, up, down, second, out):
+def update_kernel(powers, every, gate, up, down, new_gate, new_up, new_down):
     rows = FD // PLANE
     starts = []
     for matrix in range(3):
@@ -152,14 +158,17 @@
         factor = powers[matrix : matrix + 1, 0:1]
         starts.append(total * (factor / jnp.sqrt(squares * factor * factor + 1e-6)))
     ortho = orthogonal(starts)
-    new_gate = (gate[...] + ortho[0]).astype(jnp.bfloat16)
-    new_up = (up[...] + ortho[1]).astype(jnp.bfloat16)
-    new_down = (down[...] + ortho[2].T).astype(jnp.bfloat16)
-    query = block_rows(second, 2, 2)
-    gate_pre = dot(query, new_gate)
-    up_pre = dot(query, new_up)
+    new_gate[...] = (gate[...] + ortho[0]).astype(jnp.bfloat16)
+    new_up[...] = (up[...] + ortho[1]).astype(jnp.bfloat16)
+    new_down[...] = (down[...] + ortho[2].T).astype(jnp.bfloat16)
+
+
+def apply_kernel(third, new_gate, new_up, new_down, out):
+    query = block_rows(third, 2, 2)
+    gate_pre = dot(query, new_gate[...])
+    up_pre = dot(query, new_up[...])
     hidden = (gate_pre * (1.0 / (1.0 + jnp.exp(-gate_pre))) * up_pre).astype(jnp.bfloat16)
-    result = dot(hidden, new_down)
+    result = dot(hidden, new_down[...])
     span = result.shape[0]
     for column in range(FD // LANES):
         out[pl.ds(column, span, stride=FD // LANES), :] = result[
@@ -167,16 +176,16 @@
         ]
 
 
-def call(kernel, shape, operands, flops, scalars=0):
+def call(kernel, shapes, operands, flops, scalars=0):
     vmem = pl.BlockSpec(memory_space=pltpu.VMEM)
     smem = pl.BlockSpec(memory_space=pltpu.SMEM)
     return pl.pallas_call(
         kernel,
-        out_shape=jax.ShapeDtypeStruct(shape, jnp.float32),
+        out_shape=[jax.ShapeDtypeStruct(shape, dtype) for shape, dtype in shapes],
         in_specs=[smem] * scalars + [vmem] * (len(operands) - scalars),
-        out_specs=vmem,
+        out_specs=[vmem] * len(shapes),
         compiler_params=pltpu.CompilerParams(vmem_limit_bytes=VMEM_LIMIT),
-        cost_estimate=pl.CostEstimate(flops=flops, bytes_accessed=4 << 20, transcendentals=0),
+        cost_estimate=pl.CostEstimate(flops=flops, bytes_accessed=1 << 20, transcendentals=0),
     )(*operands)
 
 
@@ -191,6 +200,9 @@
     for half in range(HALVES)
     for y in range(YS)
 ]
+
+
+FLOPS = 1 << 20
 
 
 def tag_rows(power):
@@ -209,53 +221,68 @@
     value = value_heads.reshape(rows, group, own, LANES).transpose(1, 2, 0, 3)
     fast = fast_inputs.reshape(rows, group, 6, LANES).transpose(1, 2, 0, 3)
     logits = jnp.pad(rate_logits.transpose(1, 2, 0), ((0, 0), (0, 13), (0, LANES - rows)))
-    first = jnp.concatenate([key, value, fast[:, 2:]], axis=1)
-    blocks = first.shape[1]
-    first = jnp.concatenate([first.reshape(group, blocks * rows, LANES), logits], axis=1)
-    second = jnp.concatenate([query, fast[:, :2]], axis=1).reshape(group, 4 * rows, LANES)
+    pairs = jnp.stack([key, value], axis=2)
+    first = jnp.concatenate([fast[:, 2:], pairs[:, 0]], axis=1).reshape(group, 6 * rows, LANES)
+    first = jnp.concatenate([first, logits], axis=1)
+    second = pairs[:, 1].reshape(group, 2 * rows, LANES)
+    third = jnp.concatenate([query, fast[:, :2]], axis=1).reshape(group, 4 * rows, LANES)
+    float32, bfloat16 = jnp.float32, jnp.bfloat16
+    devices = lax.axis_size("wide")
+    later = [(i, i + 1) for i in range(devices - 1)]
 
     first = lax.all_to_all(first, "narrow", 0, 0, tiled=True)
-    devices = lax.axis_size("wide")
-    earlier = lax.ppermute(
-        first[:, : 4 * rows], "wide", [(i, i + 1) for i in range(devices - 1)]
-    )
+    earlier_key = lax.ppermute(first[:, 4 * rows : 5 * rows], "wide", later)
+    earlier_value = lax.ppermute(first[:, 5 * rows : 6 * rows], "wide", later)
 
     weights = (gate_fast[0], up_fast[0], down_fast[0])
     count = 3 * FHID // LANES * FD // PLANE
-    pieces = call(gradient_kernel, (PLANE, count + 16, LANES), (first, *weights), 1 << 30)
+    (pieces,) = call(
+        gradient_kernel, [((PLANE, count + 16, LANES), float32)], (first, *weights), FLOPS
+    )
     got = lax.all_to_all(
         pieces.astype(jnp.float16), "wide", 0, 0, tiled=True, axis_index_groups=PLANES
     )
-    second, got = lax.optimization_barrier((second, got))
+    second, got, earlier_key = lax.optimization_barrier((second, got, earlier_key))
     second = lax.all_to_all(second, "narrow", 0, 0, tiled=True)
-    powers = got[:, count : count + 3, 0].astype(jnp.float32)
+    powers = got[:, count : count + 3, 0].astype(float32)
     top = jnp.max(powers, axis=0)
-    parts = got[:, :count].astype(jnp.float32).reshape(PLANE, 3, -1, LANES)
+    parts = got[:, :count].astype(float32).reshape(PLANE, 3, -1, LANES)
     half = jnp.sum(parts * (jnp.exp2(powers - top) * 0.0625)[:, :, None, None], axis=0)
     sent = jnp.concatenate([half.astype(jnp.float16).reshape(count, LANES), tag_rows(top)], axis=0)
     other = lax.ppermute(sent, "wide", SWAP)
-    other_top = other[count : count + 3, 0].astype(jnp.float32)
+    third, second, other, earlier_value = lax.optimization_barrier(
+        (third, second, other, earlier_value)
+    )
+    third = lax.all_to_all(third, "narrow", 0, 0, tiled=True)
+    earlier_second = lax.ppermute(second, "wide", later)
+    other_top = other[count : count + 3, 0].astype(float32)
     both = jnp.maximum(top, other_top)
     whole = half * (jnp.exp2(top - both) * 0.5)[:, None, None]
-    whole = whole + other[:count].astype(jnp.float32).reshape(3, -1, LANES) * (
+    whole = whole + other[:count].astype(float32).reshape(3, -1, LANES) * (
         jnp.exp2(other_top - both) * 0.5
     )[:, None, None]
-    every = lax.all_gather(
-        whole.astype(jnp.float16).reshape(count, LANES), "wide", axis_index_groups=PLANES
-    )
+    whole = whole.astype(jnp.float16).reshape(count, LANES)
+    every = lax.all_gather(whole, "wide", axis_index_groups=PLANES)
     factors = jnp.broadcast_to(
-        jnp.concatenate([jnp.exp2(both - 8.0), jnp.zeros((5,), jnp.float32)])[:, None], (8, LANES)
-    )
-    fast_out = call(
-        apply_kernel,
-        (span * FD // LANES, LANES),
-        (factors, every.astype(jnp.float32), *weights, second),
-        10 << 30,
-    )
-    earlier, fast_out = lax.optimization_barrier((earlier, fast_out))
+        jnp.concatenate([jnp.exp2(both - 8.0), jnp.zeros((5,), float32)])[:, None], (8, LANES)
+    )
+    fresh = call(
+        update_kernel,
+        [((FD, FHID), bfloat16), ((FD, FHID), bfloat16), ((FHID, FD), bfloat16)],
+        (factors, every.astype(float32), *weights),
+        FLOPS,
+    )
+    (fast_out,) = call(
+        apply_kernel, [((span * FD // LANES, LANES), float32)], (third, *fresh), FLOPS
+    )
     place = lax.axis_index("wide").reshape(1)
-    window_out = call(
-        attention_kernel, (span * own, LANES), (place, first, earlier, second), 1 << 30, 1
+    earlier_second, fast_out = lax.optimization_barrier((earlier_second, fast_out))
+    (window_out,) = call(
+        attention_kernel,
+        [((span * own, LANES), float32)],
+        (place, first, second, earlier_key, earlier_value, earlier_second, third),
+        FLOPS,
+        1,
     )
     return (window_out.reshape(span, own, LANES), fast_out.reshape(span, 1, FD))
 

time: 216 us -> 205 us (0.949)
  the two profiles are of different devices: /device:TPU:160 before, /device:TPU:2 now
where the time goes in v3:
time: 205 us; the launch traced here: 204 us
  blocking collectives  88.8 us (43%)
  starting transfers between devices  47.2 us (23%)
  waiting for transfers between devices  22.8 us (11%)
  local copies, waits for them, and re-layouts  21.2 us (10%)
  Pallas kernels  15 us (7%)
  other arithmetic  7.66 us (4%)
    all_to_all x1, blocking collectives, per_device(): first = lax.all_to_all(first, 'narrow', 0, 0, tiled=True)  53.1 us
    all_gather x1, blocking collectives, per_device(): every = lax.all_gather(whole, 'wide', axis_index_groups=PLANES)  35.8 us
    ppermute x1, waiting for transfers between devices, per_device(): earlier_key = lax.ppermute(first[:, 4 * rows:5 * rows], 'wide', later)  17.6 us
    pallas_call x4, Pallas kernels, call(): pl.pallas_call(kernel, out_shape=[jax.ShapeDtypeStruct(shape, dtype) for...  15 us
    all_to_all x1, starting transfers between devices, per_device(): third = lax.all_to_all(third, 'narrow', 0, 0, tiled=True)  12 us
    all_to_all x1, starting transfers between devices, per_device(): second = lax.all_to_all(second, 'narrow', 0, 0, tiled=True)  11.6 us
    unnamed x40, local copies, waits for them, and re-layouts  10.2 us
    all_to_all x1, starting transfers between devices, per_device(): lax.all_to_all(pieces.astype(jnp.float16), 'wide', 0, 0, tiled=True, axis...  7.61 us
  transfers between devices with their start and end apart: 7, of which 2 were waited for; matrix products, arithmetic and copies ran while one was open for 6% of the time, Pallas kernels for 4%

profile of v3, /device:TPU:2, one launch (start us, length us, event | category | flops | bytes accessed | tf_op | source)
XLA Modules:
  0.0 203.6 jit_solution(18416552703576292255)
XLA Ops:
  0.6 0.7 copy.102
  1.3 1.0 copy.100
  2.3 1.2 reshape.94
  3.5 1.2 fusion.9
  4.8 0.8 pad_maximum_fusion.2
  5.5 0.3 copy.81
  5.8 0.1 copy-done.18
  5.9 0.9 reshape.93
  6.8 1.0 copy-done.13
  7.8 0.3 slice.48
  8.2 0.5 pad_maximum_fusion
  8.7 0.5 copy.82
  9.3 53.1 %all_to_all.20.first = bf16[16,208,128]{2,1,0:T(8,128)(2,1)S(1)} all-to-all(bf16[16,208,128]{2,1,0:T(8,128)(2,1)S(1)} %fusion.1), channel_id=1, replica_groups=mesh['wide'=32,'narrow'=16] {'narrow'}, dimensions={0} | all-to-all | bytes 1703936 | tf_op jit(solution)/shard_map/all_to_all | solution.py:233
  62.4 1.8 shard_map.86
  64.2 1.0 convert_element_type.55
  65.2 7.6 %all-to-all-start.1 = ((f16[16,208,128]{2,1,0:T(8,128)(2,1)}), f16[16,208,128]{2,1,0:T(8,128)(2,1)}, u32[]{:S(2)}, u32[]{:S(2)}) async-start(f16[16,208,128]{2,1,0:T(8,128)(2,1)} %convert_element_type.55), calls=%async_computation.1 | async-start | bytes 1703936 | tf_op jit(solution)/shard_map/all_to_all | solution.py:242
  72.8 0.7 fusion.8
  73.5 3.4 %collective-permute-start = (bf16[16,32,128]{2,1,0:T(8,128)(2,1)S(1)}, bf16[16,32,128]{2,1,0:T(8,128)(2,1)S(1)}, u32[]{:S(2)}, u32[]{:S(2)}) collective-permute-start(bf16[16,32,128]{2,1,0:T(8,128)(2,1)S(1)} %get-tuple-element.41), channel_id=1, source_target_pairs={{0,16},{16,32},{32,48},{48,64},{64,80},{80,96},{96,112},{112,128},... | collective-permute-start | bytes 393224 | tf_op jit(solution)/shard_map/ppermute | solution.py:234
  76.9 2.1 %slice.53 = bf16[16,2,32,128]{3,1,0,2:T(2,128)(2,1)} slice(bf16[16,6,32,128]{3,1,0,2:T(8,128)(2,1)} %bitcast.50), slice={[0:16], [0:2], [0:32], [0:128]} | slice | bytes 524288 | tf_op jit(solution)/shard_map/slice | solution.py:228
  79.0 0.9 copy.99
  79.9 0.8 copy.86
  80.7 3.4 %collective-permute-start.2 = (bf16[16,32,128]{2,1,0:T(8,128)(2,1)}, bf16[16,32,128]{2,1,0:T(8,128)(2,1)S(1)}, u32[]{:S(2)}, u32[]{:S(2)}) collective-permute-start(bf16[16,32,128]{2,1,0:T(8,128)(2,1)} %get-tuple-element.40), channel_id=1, source_target_pairs={{0,16},{16,32},{32,48},{48,64},{64,80},{80,96},{96,112},{112,128},... | collective-permute-start | bytes 393224 | tf_op jit(solution)/shard_map/ppermute | solution.py:235
  84.1 17.6 %collective-permute-done.earlier_key = bf16[16,32,128]{2,1,0:T(8,128)(2,1)S(1)} collective-permute-done((bf16[16,32,128]{2,1,0:T(8,128)(2,1)S(1)}, bf16[16,32,128]{2,1,0:T(8,128)(2,1)S(1)}, u32[]{:S(2)}, u32[]{:S(2)}) %collective-permute-start) | collective-permute-done | bytes 131104 | tf_op jit(solution)/shard_map/ppermute | solution.py:234
  101.7 11.6 %all-to-all-start.2 = ((bf16[16,64,128]{2,1,0:T(8,128)(2,1)}), bf16[16,64,128]{2,1,0:T(8,128)(2,1)S(1)}, u32[]{:S(2)}, u32[]{:S(2)}) async-start(bf16[16,64,128]{2,1,0:T(8,128)(2,1)} %bitcast.14), calls=%async_computation.2 | async-start | bytes 524288 | tf_op jit(solution)/shard_map/all_to_all | solution.py:246
  113.3 0.9 fusion.4
  114.3 0.8 slice_convert_fusion
  115.5 1.6 multiply_reduce_fusion
  117.1 0.1 maximum_maximum_fusion
  117.3 7.4 %collective-permute-start.1 = (f16[208,128]{1,0:T(8,128)(2,1)S(1)}, f16[208,128]{1,0:T(8,128)(2,1)S(1)}, u32[]{:S(2)}, u32[]{:S(2)}) collective-permute-start(f16[208,128]{1,0:T(8,128)(2,1)S(1)} %maximum_maximum_fusion), channel_id=1, source_target_pairs={{0,64},{16,80},{32,96},{48,112},{64,0},{80,16},{96,32},{112,48},{1... | collective-permute-start | bytes 159752 | tf_op jit(solution)/shard_map/ppermute | solution.py:252
  124.6 0.5 pad_maximum_fusion.1
  125.2 1.1 copy.85
  126.4 0.6 copy-done.11
  127.0 5.2 %collective-permute-done.1 = f16[208,128]{1,0:T(8,128)(2,1)S(1)} collective-permute-done((f16[208,128]{1,0:T(8,128)(2,1)S(1)}, f16[208,128]{1,0:T(8,128)(2,1)S(1)}, u32[]{:S(2)}, u32[]{:S(2)}) %collective-permute-start.1) | collective-permute-done | bytes 53280 | tf_op jit(solution)/shard_map/ppermute | solution.py:252
  132.2 12.0 %all-to-all-start.3 = ((bf16[16,128,128]{2,1,0:T(8,128)(2,1)}), bf16[16,128,128]{2,1,0:T(8,128)(2,1)S(1)}, u32[]{:S(2)}, u32[]{:S(2)}) async-start(bf16[16,128,128]{2,1,0:T(8,128)(2,1)} %bitcast.53), calls=%async_computation.3 | async-start | bytes 1048576 | tf_op jit(solution)/shard_map/all_to_all | solution.py:256
  144.7 1.9 collective-permute-start.3
  146.6 1.0 add_convert_fusion
  147.7 35.8 %all-gather = f16[3072,128]{1,0:T(8,128)(2,1)S(1)} all-gather(f16[192,128]{1,0:T(8,128)(2,1)S(1)} %add_convert_fusion), channel_id=2, replica_groups={{0,16,32,48,128,144,160,176,256,272,288,304,384,400,416,432},{64,80,96,..., dimensions={0}, use_global_device_ids=true | all-gather | bytes 835584 | tf_op jit(solution)/shard_map/all_gather | solution.py:265
  183.6 7.7 %shard_map.87 = (bf16[256,512]{1,0:T(8,128)(2,1)S(1)}, bf16[256,512]{1,0:T(8,128)(2,1)S(1)}, bf16[512,256]{1,0:T(8,128)(2,1)S(1)}) custom-call(f32[8,128]{1,0:T(8,128)S(1)} %broadcast_in_dim.8.powers, f32[16,192,128]{2,1,0:T(8,128)S(1)} %convert.1.every, f32[256,512]{1,0:T(8,128)S(1)} %bitcast.44, f32[256,512]{1,0:T(8,128)S(1)} %bitcast.46, ...), custom_call_target="tpu_custom_call" | custom-call | flops 1048576 | bytes 1048576 | tf_op jit(solution)/shard_map/pallas_call | solution.py:182
  191.3 0.7 copy-done.3
  192.0 0.7 copy-done.5
  192.7 0.7 copy-done.7
  193.4 0.9 copy-done.4
  194.3 0.9 copy-done.6
  195.3 0.9 copy-done.8
  196.2 1.5 shard_map.88
  197.7 0.9 copy-done.10
  198.6 0.9 copy-done.12
  199.5 4.1 %shard_map.89 = f32[1024,128]{1,0:T(8,128)} custom-call(s32[1]{0:T(128)} %bitcast.place, bf16[16,208,128]{2,1,0:T(8,128)(2,1)S(1)} %all_to_all.20.first, bf16[16,64,128]{2,1,0:T(8,128)(2,1)S(1)} %all-to-all-done.2.second, bf16[16,32,128]{2,1,0:T(8,128)(2,1)S(1)} %copy-done.10, bf16[16,32,128]{2,1,0:T(8,128)(2,1)S(1)} %copy-done.12, ...), custom_call_target="tpu_custom_call" | custom-call | flops 1048576 | bytes 1048576 | tf_op jit(solution)/shard_map/pallas_call | solution.py:182
  (53 shorter events, 1.4 us)
Async XLA Ops:
  4.7 1.2 copy-start.18
  6.8 1.0 copy-start.13
  9.2 53.2 %copy-start = (f32[1,256,512]{2,1,0:T(8,128)S(1)}, f32[1,256,512]{2,1,0:T(8,128)}, u32[]{:S(2)}) copy-start(f32[1,256,512]{2,1,0:T(8,128)} %param.11) | copy-start | bytes 1572868
  9.2 53.2 %copy-start.1 = (f32[1,256,512]{2,1,0:T(8,128)S(1)}, f32[1,256,512]{2,1,0:T(8,128)}, u32[]{:S(2)}) copy-start(f32[1,256,512]{2,1,0:T(8,128)} %param.12) | copy-start | bytes 1572868
  9.2 53.2 %copy-start.2 = (f32[1,512,256]{2,1,0:T(8,128)S(1)}, f32[1,512,256]{2,1,0:T(8,128)}, u32[]{:S(2)}) copy-start(f32[1,512,256]{2,1,0:T(8,128)} %param.13) | copy-start | bytes 1572868
  65.2 14.7 %copy-start.16 = (bf16[16,1,2,32,128]{4,0,1,3,2:T(8,128)(2,1)S(1)}, bf16[16,1,2,32,128]{4,0,1,3,2:T(8,128)(2,1)}, u32[]{:S(2)}) copy-start(bf16[16,1,2,32,128]{4,0,1,3,2:T(8,128)(2,1)} %get-tuple-element.42) | copy-start | bytes 786436
  65.2 36.5 %all-to-all-start.1 = ((f16[16,208,128]{2,1,0:T(8,128)(2,1)}), f16[16,208,128]{2,1,0:T(8,128)(2,1)}, u32[]{:S(2)}, u32[]{:S(2)}) async-start(f16[16,208,128]{2,1,0:T(8,128)(2,1)} %convert_element_type.55), calls=%async_computation.1 | async-start | bytes 1703936 | tf_op jit(solution)/shard_map/all_to_all | solution.py:242
  73.5 28.2 %collective-permute-start = (bf16[16,32,128]{2,1,0:T(8,128)(2,1)S(1)}, bf16[16,32,128]{2,1,0:T(8,128)(2,1)S(1)}, u32[]{:S(2)}, u32[]{:S(2)}) collective-permute-start(bf16[16,32,128]{2,1,0:T(8,128)(2,1)S(1)} %get-tuple-element.41), channel_id=1, source_target_pairs={{0,16},{16,32},{32,48},{48,64},{64,80},{80,96},{96,112},{112,128},... | collective-permute-start | bytes 393224 | tf_op jit(solution)/shard_map/ppermute | solution.py:234
  79.9 44.8 %copy-start.14 = (bf16[32,16,2,1,128]{4,2,1,0,3:T(2,128)(2,1)S(1)}, bf16[32,16,2,1,128]{4,2,1,0,3:T(2,128)(2,1)}, u32[]{:S(2)}) copy-start(bf16[32,16,2,1,128]{4,2,1,0,3:T(2,128)(2,1)} %copy.99) | copy-start | bytes 786436
  79.9 44.8 %copy-start.15 = (bf16[16,2,32,128]{3,1,0,2:T(2,128)(2,1)S(1)}, bf16[16,2,32,128]{3,1,0,2:T(2,128)(2,1)}, u32[]{:S(2)}) copy-start(bf16[16,2,32,128]{3,1,0,2:T(2,128)(2,1)} %slice.53) | copy-start | bytes 786436
  80.7 45.6 %collective-permute-start.2 = (bf16[16,32,128]{2,1,0:T(8,128)(2,1)}, bf16[16,32,128]{2,1,0:T(8,128)(2,1)S(1)}, u32[]{:S(2)}, u32[]{:S(2)}) collective-permute-start(bf16[16,32,128]{2,1,0:T(8,128)(2,1)} %get-tuple-element.40), channel_id=1, source_target_pairs={{0,16},{16,32},{32,48},{48,64},{64,80},{80,96},{96,112},{112,128},... | collective-permute-start | bytes 393224 | tf_op jit(solution)/shard_map/ppermute | solution.py:235
  101.7 24.6 %copy-start.9 = (bf16[16,32,128]{2,1,0:T(8,128)(2,1)}, bf16[16,32,128]{2,1,0:T(8,128)(2,1)S(1)}, u32[]{:S(2)}) copy-start(bf16[16,32,128]{2,1,0:T(8,128)(2,1)S(1)} %collective-permute-done.earlier_key) | copy-start | bytes 393220
  101.7 30.5 %all-to-all-start.2 = ((bf16[16,64,128]{2,1,0:T(8,128)(2,1)}), bf16[16,64,128]{2,1,0:T(8,128)(2,1)S(1)}, u32[]{:S(2)}, u32[]{:S(2)}) async-start(bf16[16,64,128]{2,1,0:T(8,128)(2,1)} %bitcast.14), calls=%async_computation.2 | async-start | bytes 524288 | tf_op jit(solution)/shard_map/all_to_all | solution.py:246
  117.1 9.2 %copy-start.17 = (f32[192,128]{1,0:T(8,128)}, f32[192,128]{1,0:T(8,128)S(1)}, u32[]{:S(2)}) copy-start(f32[192,128]{1,0:T(8,128)S(1)} %multiply_reduce_fusion) | copy-start | bytes 294916
  117.3 15.0 %collective-permute-start.1 = (f16[208,128]{1,0:T(8,128)(2,1)S(1)}, f16[208,128]{1,0:T(8,128)(2,1)S(1)}, u32[]{:S(2)}, u32[]{:S(2)}) collective-permute-start(f16[208,128]{1,0:T(8,128)(2,1)S(1)} %maximum_maximum_fusion), channel_id=1, source_target_pairs={{0,64},{16,80},{32,96},{48,112},{64,0},{80,16},{96,32},{112,48},{1... | collective-permute-start | bytes 159752 | tf_op jit(solution)/shard_map/ppermute | solution.py:252
  126.3 0.6 copy-start.11
  132.2 61.2 %all-to-all-start.3 = ((bf16[16,128,128]{2,1,0:T(8,128)(2,1)}), bf16[16,128,128]{2,1,0:T(8,128)(2,1)S(1)}, u32[]{:S(2)}, u32[]{:S(2)}) async-start(bf16[16,128,128]{2,1,0:T(8,128)(2,1)} %bitcast.53), calls=%async_computation.3 | async-start | bytes 1048576 | tf_op jit(solution)/shard_map/all_to_all | solution.py:256
  144.7 53.0 %collective-permute-start.3 = (bf16[16,64,128]{2,1,0:T(8,128)(2,1)S(1)}, bf16[16,64,128]{2,1,0:T(8,128)(2,1)S(1)}, u32[]{:S(2)}, u32[]{:S(2)}) collective-permute-start(bf16[16,64,128]{2,1,0:T(8,128)(2,1)S(1)} %all-to-all-done.2.second), channel_id=1, source_target_pairs={{0,16},{16,32},{32,48},{48,64},{64,80},{80,96},{96,112},{112,128},... | collective-permute-start | bytes 786440 | tf_op jit(solution)/shard_map/ppermute | solution.py:257
  191.3 0.7 copy-start.3
  192.0 0.7 copy-start.5
  192.7 0.7 copy-start.7
  193.4 1.0 copy-start.4
  194.3 0.9 copy-start.6
  195.3 0.9 copy-start.8
  197.7 0.9 copy-start.10
  198.6 0.9 copy-start.12

commit v4 on v2

--- a/solution.py
+++ b/solution.py
@@ -39,7 +39,7 @@
 def gradient_kernel(first, gate, up, down, out):
     group = first.shape[0]
     span = group * TOK
-    logits = first[:, 8 * TOK : 8 * TOK + 16, :].astype(jnp.float32)
+    logits = first[:, 12 * TOK : 12 * TOK + 16, :].astype(jnp.float32)
     rate_blocks = []
     for source in range(group):
         turned = logits[source].T[:TOK]
@@ -88,7 +88,7 @@
     out[:, 3 * FHID // LANES * rows :, :] = jnp.broadcast_to(tag[None], (PLANE, 16, LANES))
 
 
-def attention_kernel(place, first, earlier, second, out):
+def attention_kernel(place, first, side, edge_low, edge_high, out, earlier):
     span = first.shape[0] * TOK
     scale = 1.0 / math.sqrt(LANES)
     tile = 128
@@ -97,9 +97,20 @@
     col = lax.broadcasted_iota(jnp.int32, (tile, reach), 1)
     band = (col > row) & (col - row <= span)
     begin = jnp.where(place[0] == 0, span, 0)
-    heads = second.shape[1] // TOK // 2
+    edge = lax.rem(place[0], YS) == 0
+    heads = 2
+
+    @pl.when(edge)
+    def _():
+        earlier[:, : 2 * TOK, :] = edge_low[...]
+        earlier[:, 2 * TOK :, :] = edge_high[...]
+
+    @pl.when(jnp.logical_not(edge))
+    def _():
+        earlier[...] = side[...]
+
     for head in range(heads):
-        query = block_rows(second, head, 1)
+        query = block_rows(first, 8 + head, 1)
         key = jnp.concatenate([block_rows(earlier, head, 1), block_rows(first, head, 1)], axis=0)
         value = jnp.concatenate(
             [block_rows(earlier, heads + head, 1), block_rows(first, heads + head, 1)], axis=0
@@ -139,7 +150,7 @@
     return ortho_all
 
 
-def apply_kernel(powers, every, gate, up, down, second, out):
+def apply_kernel(powers, every, gate, up, down, first, out):
     rows = FD // PLANE
     starts = []
     for matrix in range(3):
@@ -155,7 +166,7 @@
     new_gate = (gate[...] + ortho[0]).astype(jnp.bfloat16)
     new_up = (up[...] + ortho[1]).astype(jnp.bfloat16)
     new_down = (down[...] + ortho[2].T).astype(jnp.bfloat16)
-    query = block_rows(second, 2, 2)
+    query = block_rows(first, 10, 2)
     gate_pre = dot(query, new_gate)
     up_pre = dot(query, new_up)
     hidden = (gate_pre * (1.0 / (1.0 + jnp.exp(-gate_pre))) * up_pre).astype(jnp.bfloat16)
@@ -167,7 +178,7 @@
         ]
 
 
-def call(kernel, shape, operands, flops, scalars=0):
+def call(kernel, shape, operands, flops, scalars=0, scratch=()):
     vmem = pl.BlockSpec(memory_space=pltpu.VMEM)
     smem = pl.BlockSpec(memory_space=pltpu.SMEM)
     return pl.pallas_call(
@@ -175,6 +186,7 @@
         out_shape=jax.ShapeDtypeStruct(shape, jnp.float32),
         in_specs=[smem] * scalars + [vmem] * (len(operands) - scalars),
         out_specs=vmem,
+        scratch_shapes=scratch,
         compiler_params=pltpu.CompilerParams(vmem_limit_bytes=VMEM_LIMIT),
         cost_estimate=pl.CostEstimate(flops=flops, bytes_accessed=4 << 20, transcendentals=0),
     )(*operands)
@@ -191,6 +203,16 @@
     for half in range(HALVES)
     for y in range(YS)
 ]
+AROUND = [
+    (wide_index(x, half, y), wide_index(x, half, (y + 1) % YS))
+    for x in range(XS)
+    for half in range(HALVES)
+    for y in range(YS)
+]
+ENDS = [(x, half, x + half, 1 - half) for x in range(XS) for half in range(HALVES)][:-1]
+EDGE_LOW = [(wide_index(x, half, 0), wide_index(*after, 0)) for x, half, *after in ENDS]
+EDGE_HIGH = [(wide_index(x, half, YS - 1), wide_index(*after, 0)) for x, half, *after in ENDS]
+FLOPS = 1 << 20
 
 
 def tag_rows(power):
@@ -209,39 +231,45 @@
     value = value_heads.reshape(rows, group, own, LANES).transpose(1, 2, 0, 3)
     fast = fast_inputs.reshape(rows, group, 6, LANES).transpose(1, 2, 0, 3)
     logits = jnp.pad(rate_logits.transpose(1, 2, 0), ((0, 0), (0, 13), (0, LANES - rows)))
-    first = jnp.concatenate([key, value, fast[:, 2:]], axis=1)
-    blocks = first.shape[1]
-    first = jnp.concatenate([first.reshape(group, blocks * rows, LANES), logits], axis=1)
-    second = jnp.concatenate([query, fast[:, :2]], axis=1).reshape(group, 4 * rows, LANES)
-
+    blocks = jnp.concatenate([key, value, fast[:, 2:], query, fast[:, :2]], axis=1)
+    blocks = blocks.reshape(group, 12 * rows, LANES)
+    first = jnp.concatenate([blocks, logits], axis=1)
     first = lax.all_to_all(first, "narrow", 0, 0, tiled=True)
-    devices = lax.axis_size("wide")
-    earlier = lax.ppermute(
-        first[:, : 4 * rows], "wide", [(i, i + 1) for i in range(devices - 1)]
-    )
+    tail = first[:, : 4 * rows]
+    side = lax.ppermute(tail, "wide", AROUND)
 
     weights = (gate_fast[0], up_fast[0], down_fast[0])
     count = 3 * FHID // LANES * FD // PLANE
-    pieces = call(gradient_kernel, (PLANE, count + 16, LANES), (first, *weights), 1 << 30)
+    pieces = call(gradient_kernel, (PLANE, count + 16, LANES), (first, *weights), FLOPS)
     got = lax.all_to_all(
         pieces.astype(jnp.float16), "wide", 0, 0, tiled=True, axis_index_groups=PLANES
     )
-    second, got = lax.optimization_barrier((second, got))
-    second = lax.all_to_all(second, "narrow", 0, 0, tiled=True)
+    got, side = lax.optimization_barrier((got, side))
     powers = got[:, count : count + 3, 0].astype(jnp.float32)
     top = jnp.max(powers, axis=0)
     parts = got[:, :count].astype(jnp.float32).reshape(PLANE, 3, -1, LANES)
     half = jnp.sum(parts * (jnp.exp2(powers - top) * 0.0625)[:, :, None, None], axis=0)
     sent = jnp.concatenate([half.astype(jnp.float16).reshape(count, LANES), tag_rows(top)], axis=0)
     other = lax.ppermute(sent, "wide", SWAP)
+    other, low_part, high_part = lax.optimization_barrier(
+        (other, side[:, : 2 * rows], tail[:, 2 * rows :])
+    )
+    edge_low = lax.ppermute(low_part, "wide", EDGE_LOW)
+    edge_high = lax.ppermute(high_part, "wide", EDGE_HIGH)
     other_top = other[count : count + 3, 0].astype(jnp.float32)
     both = jnp.maximum(top, other_top)
     whole = half * (jnp.exp2(top - both) * 0.5)[:, None, None]
     whole = whole + other[:count].astype(jnp.float32).reshape(3, -1, LANES) * (
         jnp.exp2(other_top - both) * 0.5
     )[:, None, None]
-    every = lax.all_gather(
-        whole.astype(jnp.float16).reshape(count, LANES), "wide", axis_index_groups=PLANES
+    whole = whole.astype(jnp.float16).reshape(count, LANES)
+    every = lax.all_to_all(
+        jnp.broadcast_to(whole[None], (PLANE, count, LANES)),
+        "wide",
+        0,
+        0,
+        tiled=True,
+        axis_index_groups=PLANES,
     )
     factors = jnp.broadcast_to(
         jnp.concatenate([jnp.exp2(both - 8.0), jnp.zeros((5,), jnp.float32)])[:, None], (8, LANES)
@@ -249,13 +277,18 @@
     fast_out = call(
         apply_kernel,
         (span * FD // LANES, LANES),
-        (factors, every.astype(jnp.float32), *weights, second),
-        10 << 30,
-    )
-    earlier, fast_out = lax.optimization_barrier((earlier, fast_out))
+        (factors, every.astype(jnp.float32), *weights, first),
+        FLOPS,
+    )
     place = lax.axis_index("wide").reshape(1)
+    edge_low, edge_high, fast_out = lax.optimization_barrier((edge_low, edge_high, fast_out))
     window_out = call(
-        attention_kernel, (span * own, LANES), (place, first, earlier, second), 1 << 30, 1
+        attention_kernel,
+        (span * own, LANES),
+        (place, first, side, edge_low, edge_high),
+        FLOPS,
+        1,
+        [pltpu.VMEM((PLANE, 4 * TOK, LANES), jnp.bfloat16)],
     )
     return (window_out.reshape(span, own, LANES), fast_out.reshape(span, 1, FD))
 

time: 216 us -> 211 us (0.977)
  the two profiles are of different devices: /device:TPU:160 before, /device:TPU:7 now
where the time goes in v4:
time: 211 us; the launch traced here: 210 us
  blocking collectives  89.8 us (43%)
  waiting for transfers between devices  48 us (23%)
  starting transfers between devices  34.5 us (16%)
  Pallas kernels  15.7 us (7%)
  local copies, waits for them, and re-layouts  14.7 us (7%)
  other arithmetic  6.11 us (3%)
    all_to_all x1, blocking collectives, per_device(): first = lax.all_to_all(first, 'narrow', 0, 0, tiled=True)  89.8 us
    ppermute x1, waiting for transfers between devices, per_device(): side = lax.ppermute(tail, 'wide', AROUND)  20.7 us
    pallas_call x3, Pallas kernels, call(): pl.pallas_call(kernel, out_shape=jax.ShapeDtypeStruct(shape, jnp.float32)...  15.7 us
    ppermute x1, waiting for transfers between devices, per_device(): edge_low = lax.ppermute(low_part, 'wide', EDGE_LOW)  11.3 us
    ppermute x1, waiting for transfers between devices, per_device(): edge_high = lax.ppermute(high_part, 'wide', EDGE_HIGH)  10 us
    ppermute x1, starting transfers between devices, per_device(): other = lax.ppermute(sent, 'wide', SWAP)  7.94 us
    all_to_all x1, starting transfers between devices, per_device(): lax.all_to_all(jnp.broadcast_to(whole[None], (PLANE, count, LANES)), 'wid...  7.85 us
    ppermute x1, starting transfers between devices, per_device(): edge_low = lax.ppermute(low_part, 'wide', EDGE_LOW)  7.25 us
  transfers between devices with their start and end apart: 6, of which 5 were waited for; matrix products, arithmetic and copies ran while one was open for 2% of the time, Pallas kernels for 4%

profile of v4, /device:TPU:7, one launch (start us, length us, event | category | flops | bytes accessed | tf_op | source)
XLA Modules:
  0.0 209.8 jit_solution(2031620160615291671)
XLA Ops:
  0.6 2.0 reshape.93
  2.7 0.3 slice.46
  3.0 0.2 slice.48
  3.2 0.1 reshape.91
  3.3 1.2 fusion.6
  4.5 0.1 copy_bitcast_fusion.1
  4.7 0.2 copy.62
  4.9 0.2 copy.52
  5.1 4.9 %concatenate.12 = bf16[16,12,32,128]{3,1,0,2:T(8,128)(2,1)S(1)} concatenate(bf16[16,2,32,128]{3,1,0,2:T(2,128)(2,1)S(1)} %copy.52, bf16[16,2,32,128]{3,1,0,2:T(2,128)(2,1)} %bitcast.43, bf16[16,4,32,128]{3,1,0,2:T(4,128)(2,1)S(1)} %slice.46, bf16[16,2,32,128]{3,1,0,2:T(2,128)(2,1)S(1)} %bitcast.40, bf16[16,2,32,128]{3,1,0,2:T(2,128)(2,1)S(1)} %slice.48), dimensions={1} | concatenate | bytes 3145728 | tf_op jit(solution)/shard_map/concatenate | solution.py:234
  10.0 1.0 copy.53
  11.1 0.1 fusion.1
  11.2 89.8 %all_to_all.15.first = bf16[16,400,128]{2,1,0:T(8,128)(2,1)S(1)} all-to-all(bf16[16,400,128]{2,1,0:T(8,128)(2,1)S(1)} %fusion.1), channel_id=1, replica_groups=mesh['wide'=32,'narrow'=16] {'narrow'}, dimensions={0} | all-to-all | bytes 3276800 | tf_op jit(solution)/shard_map/all_to_all | solution.py:237
  101.1 1.8 shard_map.86
  102.9 1.0 convert_element_type.53
  103.9 6.9 %all-to-all-start.1 = ((f16[16,208,128]{2,1,0:T(8,128)(2,1)}), f16[16,208,128]{2,1,0:T(8,128)(2,1)}, u32[]{:S(2)}, u32[]{:S(2)}) async-start(f16[16,208,128]{2,1,0:T(8,128)(2,1)} %convert_element_type.53), calls=%async_computation.1 | async-start | bytes 1703936 | tf_op jit(solution)/shard_map/all_to_all | solution.py:244
  110.8 3.1 %collective-permute-start = (bf16[16,128,128]{2,1,0:T(8,128)(2,1)S(1)}, bf16[16,128,128]{2,1,0:T(8,128)(2,1)}, u32[]{:S(2)}, u32[]{:S(2)}) collective-permute-start(bf16[16,128,128]{2,1,0:T(8,128)(2,1)S(1)} %slice.49), channel_id=1, source_target_pairs={{0,16},{16,32},{32,48},{48,0},{64,80},{80,96},{96,112},{112,64},{1... | collective-permute-start | bytes 1572872 | tf_op jit(solution)/shard_map/ppermute | solution.py:239
  113.9 0.1 pad.8.clone
  114.0 20.7 %collective-permute-done.side = bf16[16,128,128]{2,1,0:T(8,128)(2,1)} collective-permute-done((bf16[16,128,128]{2,1,0:T(8,128)(2,1)S(1)}, bf16[16,128,128]{2,1,0:T(8,128)(2,1)}, u32[]{:S(2)}, u32[]{:S(2)}) %collective-permute-start) | collective-permute-done | bytes 524320 | tf_op jit(solution)/shard_map/ppermute | solution.py:239
  134.7 0.9 fusion.2
  135.5 0.8 slice_convert_fusion
  136.3 0.1 copy.55
  136.4 0.1 fusion.5
  136.5 0.1 copy.56
  136.6 0.1 mul.67
  136.7 0.1 mul.68
  136.8 1.6 multiply_reduce_fusion
  138.4 0.1 pad.7.clone
  138.5 0.1 maximum_maximum_fusion
  138.6 7.9 %collective-permute-start.1 = (f16[208,128]{1,0:T(8,128)(2,1)S(1)}, f16[208,128]{1,0:T(8,128)(2,1)S(1)}, u32[]{:S(2)}, u32[]{:S(2)}) collective-permute-start(f16[208,128]{1,0:T(8,128)(2,1)S(1)} %maximum_maximum_fusion), channel_id=1, source_target_pairs={{0,64},{16,80},{32,96},{48,112},{64,0},{80,16},{96,32},{112,48},{1... | collective-permute-start | bytes 159752 | tf_op jit(solution)/shard_map/ppermute | solution.py:253
  146.6 0.7 slice.50
  147.3 1.7 slice.41
  148.9 3.3 %collective-permute-done.1 = f16[208,128]{1,0:T(8,128)(2,1)S(1)} collective-permute-done((f16[208,128]{1,0:T(8,128)(2,1)S(1)}, f16[208,128]{1,0:T(8,128)(2,1)S(1)}, u32[]{:S(2)}, u32[]{:S(2)}) %collective-permute-start.1) | collective-permute-done | bytes 53280 | tf_op jit(solution)/shard_map/ppermute | solution.py:253
  152.3 0.1 convert_reduce_fusion
  152.4 0.1 mul.72
  152.5 0.1 mul.73
  152.7 0.1 mul.78
  152.7 0.1 add_convert_fusion
  152.9 1.0 broadcast_in_dim.11
  153.9 7.8 %all-to-all-start.2 = ((f16[16,192,128]{2,1,0:T(8,128)(2,1)}), f16[16,192,128]{2,1,0:T(8,128)(2,1)}, u32[]{:S(2)}, u32[]{:S(2)}) async-start(f16[16,192,128]{2,1,0:T(8,128)(2,1)} %broadcast_in_dim.11), calls=%async_computation.2 | async-start | bytes 1572864 | tf_op jit(solution)/shard_map/all_to_all | solution.py:266
  161.8 7.2 %collective-permute-start.2 = (bf16[16,64,128]{2,1,0:T(8,128)(2,1)}, bf16[16,64,128]{2,1,0:T(8,128)(2,1)S(1)}, u32[]{:S(2)}, u32[]{:S(2)}) collective-permute-start(bf16[16,64,128]{2,1,0:T(8,128)(2,1)} %slice.41), channel_id=1, source_target_pairs={{0,64},{64,128},{128,192},{192,256},{256,320},{320,384},{384,448},... | collective-permute-start | bytes 786440 | tf_op jit(solution)/shard_map/ppermute | solution.py:257
  169.0 1.5 collective-permute-start.3
  170.5 2.7 %all-to-all-done.2 = f16[16,192,128]{2,1,0:T(8,128)(2,1)} async-done(((f16[16,192,128]{2,1,0:T(8,128)(2,1)}), f16[16,192,128]{2,1,0:T(8,128)(2,1)}, u32[]{:S(2)}, u32[]{:S(2)}) %all-to-all-start.2) | async-done | bytes 786464 | tf_op jit(solution)/shard_map/all_to_all | solution.py:266
  173.2 1.2 convert_element_type.63.every
  174.5 0.1 broadcast_in_dim.10.powers
  174.5 8.7 %shard_map.87 = f32[1024,128]{1,0:T(8,128)} custom-call(f32[8,128]{1,0:T(8,128)S(1)} %broadcast_in_dim.10.powers, f32[16,192,128]{2,1,0:T(8,128)S(1)} %convert_element_type.63.every, f32[256,512]{1,0:T(8,128)S(1)} %bitcast.32, f32[256,512]{1,0:T(8,128)S(1)} %bitcast.34, f32[512,256]{1,0:T(8,128)S(1)} %bitcast.36, bf16[16,400,128]{2,1,0:T(8,128)(2,1)S(1)} %all_to_all.15.first), custom_call_target="tpu_custom_call" | custom-call | flops 1048576 | bytes 4194304 | tf_op jit(solution)/shard_map/pallas_call | solution.py:184
  183.3 11.3 %collective-permute-done.2.edge_low = bf16[16,64,128]{2,1,0:T(8,128)(2,1)S(1)} collective-permute-done((bf16[16,64,128]{2,1,0:T(8,128)(2,1)}, bf16[16,64,128]{2,1,0:T(8,128)(2,1)S(1)}, u32[]{:S(2)}, u32[]{:S(2)}) %collective-permute-start.2) | collective-permute-done | bytes 262176 | tf_op jit(solution)/shard_map/ppermute | solution.py:257
  194.6 10.0 %collective-permute-done.3.edge_high = bf16[16,64,128]{2,1,0:T(8,128)(2,1)} collective-permute-done((bf16[16,64,128]{2,1,0:T(8,128)(2,1)}, bf16[16,64,128]{2,1,0:T(8,128)(2,1)}, u32[]{:S(2)}, u32[]{:S(2)}) %collective-permute-start.3) | collective-permute-done | bytes 262176 | tf_op jit(solution)/shard_map/ppermute | solution.py:258
  204.6 5.2 %shard_map.88 = f32[1024,128]{1,0:T(8,128)} custom-call(s32[1]{0:T(128)} %bitcast.place, bf16[16,400,128]{2,1,0:T(8,128)(2,1)S(1)} %all_to_all.15.first, bf16[16,128,128]{2,1,0:T(8,128)(2,1)} %collective-permute-done.side, bf16[16,64,128]{2,1,0:T(8,128)(2,1)S(1)} %collective-permute-done.2.edge_low, bf16[16,64,128]{2,1,0:T(8,128)(2,1)} %collective-permute-done.3.edge_high), custom_call_target="tpu_custom_call" | custom-call | flops 1048576 | bytes 4194304 | tf_op jit(solution)/shard_map/pallas_call | solution.py:184
  (19 shorter events, 0.2 us)
Async XLA Ops:
  0.6 2.6 %copy-start.3 = (bf16[32,32,256]{2,1,0:T(8,128)(2,1)S(1)}, bf16[32,32,256]{2,1,0:T(8,128)(2,1)}, u32[]{:S(2)}) copy-start(bf16[32,32,256]{2,1,0:T(8,128)(2,1)} %param.7) | copy-start | bytes 1572868
  10.0 1.0 copy-start.4
  11.2 89.9 %copy-start = (f32[1,256,512]{2,1,0:T(8,128)S(1)}, f32[1,256,512]{2,1,0:T(8,128)}, u32[]{:S(2)}) copy-start(f32[1,256,512]{2,1,0:T(8,128)} %param.11) | copy-start | bytes 1572868
  11.2 89.9 %copy-start.1 = (f32[1,256,512]{2,1,0:T(8,128)S(1)}, f32[1,256,512]{2,1,0:T(8,128)}, u32[]{:S(2)}) copy-start(f32[1,256,512]{2,1,0:T(8,128)} %param.12) | copy-start | bytes 1572868
  11.2 89.9 %copy-start.2 = (f32[1,512,256]{2,1,0:T(8,128)S(1)}, f32[1,512,256]{2,1,0:T(8,128)}, u32[]{:S(2)}) copy-start(f32[1,512,256]{2,1,0:T(8,128)} %param.13) | copy-start | bytes 1572868
  103.9 30.8 %all-to-all-start.1 = ((f16[16,208,128]{2,1,0:T(8,128)(2,1)}), f16[16,208,128]{2,1,0:T(8,128)(2,1)}, u32[]{:S(2)}, u32[]{:S(2)}) async-start(f16[16,208,128]{2,1,0:T(8,128)(2,1)} %convert_element_type.53), calls=%async_computation.1 | async-start | bytes 1703936 | tf_op jit(solution)/shard_map/all_to_all | solution.py:244
  110.8 23.9 %collective-permute-start = (bf16[16,128,128]{2,1,0:T(8,128)(2,1)S(1)}, bf16[16,128,128]{2,1,0:T(8,128)(2,1)}, u32[]{:S(2)}, u32[]{:S(2)}) collective-permute-start(bf16[16,128,128]{2,1,0:T(8,128)(2,1)S(1)} %slice.49), channel_id=1, source_target_pairs={{0,16},{16,32},{32,48},{48,0},{64,80},{80,96},{96,112},{112,64},{1... | collective-permute-start | bytes 1572872 | tf_op jit(solution)/shard_map/ppermute | solution.py:239
  138.6 13.7 %collective-permute-start.1 = (f16[208,128]{1,0:T(8,128)(2,1)S(1)}, f16[208,128]{1,0:T(8,128)(2,1)S(1)}, u32[]{:S(2)}, u32[]{:S(2)}) collective-permute-start(f16[208,128]{1,0:T(8,128)(2,1)S(1)} %maximum_maximum_fusion), channel_id=1, source_target_pairs={{0,64},{16,80},{32,96},{48,112},{64,0},{80,16},{96,32},{112,48},{1... | collective-permute-start | bytes 159752 | tf_op jit(solution)/shard_map/ppermute | solution.py:253
  153.9 19.3 %all-to-all-start.2 = ((f16[16,192,128]{2,1,0:T(8,128)(2,1)}), f16[16,192,128]{2,1,0:T(8,128)(2,1)}, u32[]{:S(2)}, u32[]{:S(2)}) async-start(f16[16,192,128]{2,1,0:T(8,128)(2,1)} %broadcast_in_dim.11), calls=%async_computation.2 | async-start | bytes 1572864 | tf_op jit(solution)/shard_map/all_to_all | solution.py:266
  161.8 32.8 %collective-permute-start.2 = (bf16[16,64,128]{2,1,0:T(8,128)(2,1)}, bf16[16,64,128]{2,1,0:T(8,128)(2,1)S(1)}, u32[]{:S(2)}, u32[]{:S(2)}) collective-permute-start(bf16[16,64,128]{2,1,0:T(8,128)(2,1)} %slice.41), channel_id=1, source_target_pairs={{0,64},{64,128},{128,192},{192,256},{256,320},{320,384},{384,448},... | collective-permute-start | bytes 786440 | tf_op jit(solution)/shard_map/ppermute | solution.py:257
  169.0 35.6 %collective-permute-start.3 = (bf16[16,64,128]{2,1,0:T(8,128)(2,1)}, bf16[16,64,128]{2,1,0:T(8,128)(2,1)}, u32[]{:S(2)}, u32[]{:S(2)}) collective-permute-start(bf16[16,64,128]{2,1,0:T(8,128)(2,1)} %slice.50), channel_id=1, source_target_pairs={{48,64},{112,128},{176,192},{240,256},{304,320},{368,384},{432,448... | collective-permute-start | bytes 786440 | tf_op jit(solution)/shard_map/ppermute | solution.py:258

commit v5 on v4

--- a/solution.py
+++ b/solution.py
@@ -215,28 +215,21 @@
 FLOPS = 1 << 20
 
 
-def tag_rows(power):
-    wide = jnp.broadcast_to(power.astype(jnp.float16)[:, None], (3, LANES))
-    return jnp.concatenate([wide, jnp.zeros((13, LANES), jnp.float16)], axis=0)
-
-
 def per_device(query_key, value_heads, fast_inputs, rate_logits, gate_fast, up_fast, down_fast):
     group = lax.axis_size("narrow")
     rows = query_key.shape[0]
     own = query_key.shape[1] // group
     span = rows * group
-    pair = query_key.reshape(rows, group, own, 2, LANES)
-    query = pair[:, :, :, 0].transpose(1, 2, 0, 3)
-    key = pair[:, :, :, 1].transpose(1, 2, 0, 3)
-    value = value_heads.reshape(rows, group, own, LANES).transpose(1, 2, 0, 3)
-    fast = fast_inputs.reshape(rows, group, 6, LANES).transpose(1, 2, 0, 3)
+    pair = query_key.transpose(1, 0, 2).reshape(group, own * rows, 2 * LANES)
+    value = value_heads.transpose(1, 0, 2).reshape(group, own * rows, LANES)
+    fast = fast_inputs.transpose(1, 0, 2)
+    fast = [fast[:, :, i * LANES : (i + 1) * LANES] for i in range(6)]
     logits = jnp.pad(rate_logits.transpose(1, 2, 0), ((0, 0), (0, 13), (0, LANES - rows)))
-    blocks = jnp.concatenate([key, value, fast[:, 2:], query, fast[:, :2]], axis=1)
-    blocks = blocks.reshape(group, 12 * rows, LANES)
-    first = jnp.concatenate([blocks, logits], axis=1)
+    first = jnp.concatenate(
+        [pair[:, :, LANES:], value, *fast[2:], pair[:, :, :LANES], *fast[:2], logits], axis=1
+    )
     first = lax.all_to_all(first, "narrow", 0, 0, tiled=True)
     tail = first[:, : 4 * rows]
-    side = lax.ppermute(tail, "wide", AROUND)
 
     weights = (gate_fast[0], up_fast[0], down_fast[0])
     count = 3 * FHID // LANES * FD // PLANE
@@ -244,24 +237,28 @@
     got = lax.all_to_all(
         pieces.astype(jnp.float16), "wide", 0, 0, tiled=True, axis_index_groups=PLANES
     )
-    got, side = lax.optimization_barrier((got, side))
-    powers = got[:, count : count + 3, 0].astype(jnp.float32)
+    got, tail = lax.optimization_barrier((got, tail))
+    side = lax.ppermute(tail, "wide", AROUND)
+    powers = got[:, count : count + 3].astype(jnp.float32)
     top = jnp.max(powers, axis=0)
     parts = got[:, :count].astype(jnp.float32).reshape(PLANE, 3, -1, LANES)
-    half = jnp.sum(parts * (jnp.exp2(powers - top) * 0.0625)[:, :, None, None], axis=0)
-    sent = jnp.concatenate([half.astype(jnp.float16).reshape(count, LANES), tag_rows(top)], axis=0)
+    half = jnp.sum(parts * (jnp.exp2(powers - top) * 0.0625)[:, :, None], axis=0)
+    sent = jnp.concatenate(
+        [half.reshape(count, LANES), top, jnp.zeros((13, LANES), jnp.float32)], axis=0
+    )
+    sent = sent.astype(jnp.float16)
     other = lax.ppermute(sent, "wide", SWAP)
     other, low_part, high_part = lax.optimization_barrier(
         (other, side[:, : 2 * rows], tail[:, 2 * rows :])
     )
     edge_low = lax.ppermute(low_part, "wide", EDGE_LOW)
     edge_high = lax.ppermute(high_part, "wide", EDGE_HIGH)
-    other_top = other[count : count + 3, 0].astype(jnp.float32)
+    other_top = other[count : count + 3].astype(jnp.float32)
     both = jnp.maximum(top, other_top)
-    whole = half * (jnp.exp2(top - both) * 0.5)[:, None, None]
+    whole = half * (jnp.exp2(top - both) * 0.5)[:, None]
     whole = whole + other[:count].astype(jnp.float32).reshape(3, -1, LANES) * (
         jnp.exp2(other_top - both) * 0.5
-    )[:, None, None]
+    )[:, None]
     whole = whole.astype(jnp.float16).reshape(count, LANES)
     every = lax.all_to_all(
         jnp.broadcast_to(whole[None], (PLANE, count, LANES)),
@@ -271,9 +268,7 @@
         tiled=True,
         axis_index_groups=PLANES,
     )
-    factors = jnp.broadcast_to(
-        jnp.concatenate([jnp.exp2(both - 8.0), jnp.zeros((5,), jnp.float32)])[:, None], (8, LANES)
-    )
+    factors = jnp.concatenate([jnp.exp2(both - 8.0), jnp.zeros((5, LANES), jnp.float32)], axis=0)
     fast_out = call(
         apply_kernel,
         (span * FD // LANES, LANES),

time: 211 us -> 193 us (0.915)
  waiting for transfers between devices: 48 us -> 39.9 us
  local copies, waits for them, and re-layouts: 14.7 us -> 7.68 us
    ppermute x1, waiting for transfers between devices: 20.7 us -> 0.01 us  [per_device(): side = lax.ppermute(tail, 'wide', AROUND)]
    all_to_all x1, waiting for transfers between devices: 0.01 us -> 11.3 us  [per_device(): lax.all_to_all(pieces.astype(jnp.float16), 'wide', 0, 0, tiled=True, axis...]
    concatenate x5 -> x3, local copies, waits for them, and re-layouts: 6.09 us -> 0.11 us  [the longest x1 0.08 us: per_device(): jnp.concatenate([half.reshape(count, LANES), top, jnp.zeros((13, LANES),...]
    ppermute x1, waiting for transfers between devices: 11.3 us -> 15.9 us  [per_device(): edge_low = lax.ppermute(low_part, 'wide', EDGE_LOW)]
    unnamed x11 -> x27, local copies, waits for them, and re-layouts: 0.04 us -> 2.84 us
    all_to_all x1, waiting for transfers between devices: 2.71 us -> 0.17 us  [per_device(): lax.all_to_all(jnp.broadcast_to(whole[None], (PLANE, count, LANES)), 'wid...]
    reshape x2 -> x0, local copies, waits for them, and re-layouts: 2.16 us -> none  [the longest x1 2.03 us: per_device(): fast = fast_inputs.reshape(rows, group, 6, LANES).transpose(1, 2, 0, 3)]
  transfers between devices with their start and end apart: 6 -> 6, of which waited for: 5 -> 5; matrix products, arithmetic and copies ran while one was open for 2% -> 4% of each run, Pallas kernels for 4% -> 5%
where the time goes in v5:
time: 193 us; the launch traced here: 192 us
  blocking collectives  89.8 us (47%)
  waiting for transfers between devices  39.9 us (21%)
  starting transfers between devices  32.6 us (17%)
  Pallas kernels  15.6 us (8%)
  local copies, waits for them, and re-layouts  7.68 us (4%)
  other arithmetic  5.3 us (3%)
    all_to_all x1, blocking collectives, per_device(): first = lax.all_to_all(first, 'narrow', 0, 0, tiled=True)  89.8 us
    ppermute x1, waiting for transfers between devices, per_device(): edge_low = lax.ppermute(low_part, 'wide', EDGE_LOW)  15.9 us
    pallas_call x3, Pallas kernels, call(): pl.pallas_call(kernel, out_shape=jax.ShapeDtypeStruct(shape, jnp.float32)...  15.6 us
    all_to_all x1, waiting for transfers between devices, per_device(): lax.all_to_all(pieces.astype(jnp.float16), 'wide', 0, 0, tiled=True, axis...  11.3 us
    ppermute x1, waiting for transfers between devices, per_device(): edge_high = lax.ppermute(high_part, 'wide', EDGE_HIGH)  10.1 us
    ppermute x1, starting transfers between devices, per_device(): other = lax.ppermute(sent, 'wide', SWAP)  7.93 us
    all_to_all x1, starting transfers between devices, per_device(): lax.all_to_all(jnp.broadcast_to(whole[None], (PLANE, count, LANES)), 'wid...  7.13 us
    ppermute x1, starting transfers between devices, per_device(): edge_low = lax.ppermute(low_part, 'wide', EDGE_LOW)  7.02 us
  transfers between devices with their start and end apart: 6, of which 5 were waited for; matrix products, arithmetic and copies ran while one was open for 4% of the time, Pallas kernels for 5%

profile of v5, /device:TPU:7, one launch (start us, length us, event | category | flops | bytes accessed | tf_op | source)
XLA Modules:
  0.0 191.8 jit_solution(16312625500014093851)
XLA Ops:
  0.6 0.0 copy-start.5
  0.6 0.0 copy-start.6
  0.6 1.4 copy.16
  2.1 0.0 copy-done.5
  2.1 0.3 copy.9
  2.5 0.0 copy-start.7
  2.5 0.0 copy-done.6
  2.5 0.1 copy.10
  2.8 0.1 slice_dynamic-update-slice_fusion
  3.0 0.2 copy-done.7
  3.2 0.0 copy-start
  3.2 0.0 copy-start.1
  3.2 0.0 copy-start.2
  3.2 89.8 %all_to_all.15.first = bf16[16,400,128]{2,1,0:T(8,128)(2,1)S(1)} all-to-all(bf16[16,400,128]{2,1,0:T(8,128)(2,1)S(1)} %pad_dynamic-update-slice_fusion), channel_id=1, replica_groups=mesh['wide'=32,'narrow'=16] {'narrow'}, dimensions={0} | all-to-all | bytes 3276800 | tf_op jit(solution)/shard_map/all_to_all | solution.py:231
  93.1 0.0 copy-done
  93.1 0.0 copy-done.1
  93.1 0.0 copy-done.2
  93.1 1.8 shard_map.86
  94.8 1.0 convert_element_type.26
  95.9 6.9 %all-to-all-start.1 = ((f16[16,208,128]{2,1,0:T(8,128)(2,1)}), f16[16,208,128]{2,1,0:T(8,128)(2,1)}, u32[]{:S(2)}, u32[]{:S(2)}) async-start(f16[16,208,128]{2,1,0:T(8,128)(2,1)} %convert_element_type.26), calls=%async_computation.1 | async-start | bytes 1703936 | tf_op jit(solution)/shard_map/all_to_all | solution.py:237
  102.8 0.1 pad.8.clone
  102.8 0.8 slice.68
  103.7 11.3 %all-to-all-done.1 = f16[16,208,128]{2,1,0:T(8,128)(2,1)} async-done(((f16[16,208,128]{2,1,0:T(8,128)(2,1)}), f16[16,208,128]{2,1,0:T(8,128)(2,1)}, u32[]{:S(2)}, u32[]{:S(2)}) %all-to-all-start.1) | async-done | bytes 852000 | tf_op jit(solution)/shard_map/all_to_all | solution.py:237
  115.0 2.2 %collective-permute-start = (bf16[16,128,128]{2,1,0:T(8,128)(2,1)}, bf16[16,128,128]{2,1,0:T(8,128)(2,1)S(1)}, u32[]{:S(2)}, u32[]{:S(2)}) collective-permute-start(bf16[16,128,128]{2,1,0:T(8,128)(2,1)} %slice.68), channel_id=1, source_target_pairs={{0,16},{16,32},{32,48},{48,0},{64,80},{80,96},{96,112},{112,64},{1... | collective-permute-start | bytes 1572872 | tf_op jit(solution)/shard_map/ppermute | solution.py:241
  117.2 0.8 convert_reduce_fusion
  118.0 0.8 fusion.5
  118.8 1.3 fusion
  120.1 0.1 maximum_maximum_fusion
  120.2 7.9 %collective-permute-start.1 = (f16[208,128]{1,0:T(8,128)(2,1)S(1)}, f16[208,128]{1,0:T(8,128)(2,1)S(1)}, u32[]{:S(2)}, u32[]{:S(2)}) collective-permute-start(f16[208,128]{1,0:T(8,128)(2,1)S(1)} %maximum_maximum_fusion), channel_id=1, source_target_pairs={{0,64},{16,80},{32,96},{48,112},{64,0},{80,16},{96,32},{112,48},{1... | collective-permute-start | bytes 159752 | tf_op jit(solution)/shard_map/ppermute | solution.py:250
  128.1 1.7 slice.57
  129.8 0.0 collective-permute-done.side
  129.8 0.7 slice.69
  130.5 0.0 copy-start.3
  130.5 0.8 copy-done.3
  131.3 2.4 %collective-permute-done.1 = f16[208,128]{1,0:T(8,128)(2,1)S(1)} collective-permute-done((f16[208,128]{1,0:T(8,128)(2,1)S(1)}, f16[208,128]{1,0:T(8,128)(2,1)S(1)}, u32[]{:S(2)}, u32[]{:S(2)}) %collective-permute-start.1) | collective-permute-done | bytes 53280 | tf_op jit(solution)/shard_map/ppermute | solution.py:250
  133.8 1.1 broadcast_in_dim.5
  134.9 7.1 %all-to-all-start.2 = ((f16[16,192,128]{2,1,0:T(8,128)(2,1)}), f16[16,192,128]{2,1,0:T(8,128)(2,1)}, u32[]{:S(2)}, u32[]{:S(2)}) async-start(f16[16,192,128]{2,1,0:T(8,128)(2,1)} %broadcast_in_dim.5), calls=%async_computation.2 | async-start | bytes 1572864 | tf_op jit(solution)/shard_map/all_to_all | solution.py:263
  142.0 7.0 %collective-permute-start.2 = (bf16[16,64,128]{2,1,0:T(8,128)(2,1)}, bf16[16,64,128]{2,1,0:T(8,128)(2,1)S(1)}, u32[]{:S(2)}, u32[]{:S(2)}) collective-permute-start(bf16[16,64,128]{2,1,0:T(8,128)(2,1)} %slice.69), channel_id=1, source_target_pairs={{0,64},{64,128},{128,192},{192,256},{256,320},{320,384},{384,448},... | collective-permute-start | bytes 786440 | tf_op jit(solution)/shard_map/ppermute | solution.py:254
  149.0 1.5 collective-permute-start.3
  150.5 0.2 all-to-all-done.2
  150.7 1.2 convert_element_type.32.every
  152.0 0.0 copy-start.4
  152.0 8.7 %shard_map.87 = f32[1024,128]{1,0:T(8,128)} custom-call(f32[8,128]{1,0:T(8,128)S(1)} %concatenate.12.powers, f32[16,192,128]{2,1,0:T(8,128)S(1)} %convert_element_type.32.every, f32[256,512]{1,0:T(8,128)S(1)} %bitcast.33, f32[256,512]{1,0:T(8,128)S(1)} %bitcast.35, f32[512,256]{1,0:T(8,128)S(1)} %bitcast.37, bf16[16,400,128]{2,1,0:T(8,128)(2,1)S(1)} %all_to_all.15.first), custom_call_target="tpu_custom_call" | custom-call | flops 1048576 | bytes 4194304 | tf_op jit(solution)/shard_map/pallas_call | solution.py:184
  160.7 15.9 %collective-permute-done.2.edge_low = bf16[16,64,128]{2,1,0:T(8,128)(2,1)S(1)} collective-permute-done((bf16[16,64,128]{2,1,0:T(8,128)(2,1)}, bf16[16,64,128]{2,1,0:T(8,128)(2,1)S(1)}, u32[]{:S(2)}, u32[]{:S(2)}) %collective-permute-start.2) | collective-permute-done | bytes 262176 | tf_op jit(solution)/shard_map/ppermute | solution.py:254
  176.6 10.1 %collective-permute-done.3.edge_high = bf16[16,64,128]{2,1,0:T(8,128)(2,1)} collective-permute-done((bf16[16,64,128]{2,1,0:T(8,128)(2,1)}, bf16[16,64,128]{2,1,0:T(8,128)(2,1)}, u32[]{:S(2)}, u32[]{:S(2)}) %collective-permute-start.3) | collective-permute-done | bytes 262176 | tf_op jit(solution)/shard_map/ppermute | solution.py:255
  186.7 0.0 copy-done.4
  186.7 5.1 %shard_map.88 = f32[1024,128]{1,0:T(8,128)} custom-call(s32[1]{0:T(128)} %bitcast.place, bf16[16,400,128]{2,1,0:T(8,128)(2,1)S(1)} %all_to_all.15.first, bf16[16,128,128]{2,1,0:T(8,128)(2,1)S(1)} %copy-done.4, bf16[16,64,128]{2,1,0:T(8,128)(2,1)S(1)} %collective-permute-done.2.edge_low, bf16[16,64,128]{2,1,0:T(8,128)(2,1)} %collective-permute-done.3.edge_high), custom_call_target="tpu_custom_call" | custom-call | flops 1048576 | bytes 4194304 | tf_op jit(solution)/shard_map/pallas_call | solution.py:184
  (16 shorter events, 0.4 us)
Async XLA Ops:
  0.6 1.5 copy-start.5
  0.6 1.8 copy-start.6
  2.5 0.7 copy-start.7
  3.2 89.9 %copy-start = (f32[1,256,512]{2,1,0:T(8,128)S(1)}, f32[1,256,512]{2,1,0:T(8,128)}, u32[]{:S(2)}) copy-start(f32[1,256,512]{2,1,0:T(8,128)} %param.11) | copy-start | bytes 1572868
  3.2 89.9 %copy-start.1 = (f32[1,256,512]{2,1,0:T(8,128)S(1)}, f32[1,256,512]{2,1,0:T(8,128)}, u32[]{:S(2)}) copy-start(f32[1,256,512]{2,1,0:T(8,128)} %param.12) | copy-start | bytes 1572868
  3.2 89.9 %copy-start.2 = (f32[1,512,256]{2,1,0:T(8,128)S(1)}, f32[1,512,256]{2,1,0:T(8,128)}, u32[]{:S(2)}) copy-start(f32[1,512,256]{2,1,0:T(8,128)} %param.13) | copy-start | bytes 1572868
  95.9 19.1 %all-to-all-start.1 = ((f16[16,208,128]{2,1,0:T(8,128)(2,1)}), f16[16,208,128]{2,1,0:T(8,128)(2,1)}, u32[]{:S(2)}, u32[]{:S(2)}) async-start(f16[16,208,128]{2,1,0:T(8,128)(2,1)} %convert_element_type.26), calls=%async_computation.1 | async-start | bytes 1703936 | tf_op jit(solution)/shard_map/all_to_all | solution.py:237
  115.0 14.8 %collective-permute-start = (bf16[16,128,128]{2,1,0:T(8,128)(2,1)}, bf16[16,128,128]{2,1,0:T(8,128)(2,1)S(1)}, u32[]{:S(2)}, u32[]{:S(2)}) collective-permute-start(bf16[16,128,128]{2,1,0:T(8,128)(2,1)} %slice.68), channel_id=1, source_target_pairs={{0,16},{16,32},{32,48},{48,0},{64,80},{80,96},{96,112},{112,64},{1... | collective-permute-start | bytes 1572872 | tf_op jit(solution)/shard_map/ppermute | solution.py:241
  120.2 13.6 %collective-permute-start.1 = (f16[208,128]{1,0:T(8,128)(2,1)S(1)}, f16[208,128]{1,0:T(8,128)(2,1)S(1)}, u32[]{:S(2)}, u32[]{:S(2)}) collective-permute-start(f16[208,128]{1,0:T(8,128)(2,1)S(1)} %maximum_maximum_fusion), channel_id=1, source_target_pairs={{0,64},{16,80},{32,96},{48,112},{64,0},{80,16},{96,32},{112,48},{1... | collective-permute-start | bytes 159752 | tf_op jit(solution)/shard_map/ppermute | solution.py:250
  130.5 0.8 copy-start.3
  134.9 15.8 %all-to-all-start.2 = ((f16[16,192,128]{2,1,0:T(8,128)(2,1)}), f16[16,192,128]{2,1,0:T(8,128)(2,1)}, u32[]{:S(2)}, u32[]{:S(2)}) async-start(f16[16,192,128]{2,1,0:T(8,128)(2,1)} %broadcast_in_dim.5), calls=%async_computation.2 | async-start | bytes 1572864 | tf_op jit(solution)/shard_map/all_to_all | solution.py:263
  142.0 34.6 %collective-permute-start.2 = (bf16[16,64,128]{2,1,0:T(8,128)(2,1)}, bf16[16,64,128]{2,1,0:T(8,128)(2,1)S(1)}, u32[]{:S(2)}, u32[]{:S(2)}) collective-permute-start(bf16[16,64,128]{2,1,0:T(8,128)(2,1)} %slice.69), channel_id=1, source_target_pairs={{0,64},{64,128},{128,192},{192,256},{256,320},{320,384},{384,448},... | collective-permute-start | bytes 786440 | tf_op jit(solution)/shard_map/ppermute | solution.py:254
  149.0 37.7 %collective-permute-start.3 = (bf16[16,64,128]{2,1,0:T(8,128)(2,1)}, bf16[16,64,128]{2,1,0:T(8,128)(2,1)}, u32[]{:S(2)}, u32[]{:S(2)}) collective-permute-start(bf16[16,64,128]{2,1,0:T(8,128)(2,1)} %slice.57), channel_id=1, source_target_pairs={{48,64},{112,128},{176,192},{240,256},{304,320},{368,384},{432,448... | collective-permute-start | bytes 786440 | tf_op jit(solution)/shard_map/ppermute | solution.py:255
  152.0 34.8 %copy-start.4 = (bf16[16,128,128]{2,1,0:T(8,128)(2,1)S(1)}, bf16[16,128,128]{2,1,0:T(8,128)(2,1)}, u32[]{:S(2)}) copy-start(bf16[16,128,128]{2,1,0:T(8,128)(2,1)} %copy-done.3) | copy-start | bytes 1572868

commit v6 on v5

--- a/solution.py
+++ b/solution.py
@@ -230,6 +230,7 @@
     )
     first = lax.all_to_all(first, "narrow", 0, 0, tiled=True)
     tail = first[:, : 4 * rows]
+    edge_high = lax.ppermute(first[:, 2 * rows : 4 * rows], "wide", EDGE_HIGH)
 
     weights = (gate_fast[0], up_fast[0], down_fast[0])
     count = 3 * FHID // LANES * FD // PLANE
@@ -248,11 +249,8 @@
     )
     sent = sent.astype(jnp.float16)
     other = lax.ppermute(sent, "wide", SWAP)
-    other, low_part, high_part = lax.optimization_barrier(
-        (other, side[:, : 2 * rows], tail[:, 2 * rows :])
-    )
+    other, low_part, edge_high = lax.optimization_barrier((other, side[:, : 2 * rows], edge_high))
     edge_low = lax.ppermute(low_part, "wide", EDGE_LOW)
-    edge_high = lax.ppermute(high_part, "wide", EDGE_HIGH)
     other_top = other[count : count + 3].astype(jnp.float32)
     both = jnp.maximum(top, other_top)
     whole = half * (jnp.exp2(top - both) * 0.5)[:, None]
@@ -276,7 +274,7 @@
         FLOPS,
     )
     place = lax.axis_index("wide").reshape(1)
-    edge_low, edge_high, fast_out = lax.optimization_barrier((edge_low, edge_high, fast_out))
+    edge_low, fast_out = lax.optimization_barrier((edge_low, fast_out))
     window_out = call(
         attention_kernel,
         (span * own, LANES),

time: 193 us -> 189 us (0.979)
    ppermute x1, waiting for transfers between devices: 15.9 us -> 9.9 us  [per_device(): edge_low = lax.ppermute(low_part, 'wide', EDGE_LOW)]
    ppermute x1, waiting for transfers between devices: 10.1 us -> 14.4 us  [per_device(): edge_high = lax.ppermute(first[:, 2 * rows:4 * rows], 'wide', EDGE_HIGH)]
    all_to_all x1, waiting for transfers between devices: 0.17 us -> 3.81 us  [per_device(): lax.all_to_all(jnp.broadcast_to(whole[None], (PLANE, count, LANES)), 'wid...]
    ppermute x1, waiting for transfers between devices: 2.44 us -> 0.01 us  [per_device(): other = lax.ppermute(sent, 'wide', SWAP)]
    all_to_all x1, waiting for transfers between devices: 11.3 us -> 9.27 us  [per_device(): lax.all_to_all(pieces.astype(jnp.float16), 'wide', 0, 0, tiled=True, axis...]
    all_to_all x1, starting transfers between devices: 7.13 us -> 5.11 us  [per_device(): lax.all_to_all(jnp.broadcast_to(whole[None], (PLANE, count, LANES)), 'wid...]
where the time goes in v6:
time: 189 us; the launch traced here: 188 us
  blocking collectives  89.8 us (48%)
  waiting for transfers between devices  38.9 us (21%)
  starting transfers between devices  30.9 us (16%)
  Pallas kernels  15.6 us (8%)
  local copies, waits for them, and re-layouts  6.73 us (4%)
  other arithmetic  5.3 us (3%)
    all_to_all x1, blocking collectives, per_device(): first = lax.all_to_all(first, 'narrow', 0, 0, tiled=True)  89.8 us
    pallas_call x3, Pallas kernels, call(): pl.pallas_call(kernel, out_shape=jax.ShapeDtypeStruct(shape, jnp.float32)...  15.6 us
    ppermute x1, waiting for transfers between devices, per_device(): edge_high = lax.ppermute(first[:, 2 * rows:4 * rows], 'wide', EDGE_HIGH)  14.4 us
    ppermute x1, waiting for transfers between devices, per_device(): edge_low = lax.ppermute(low_part, 'wide', EDGE_LOW)  9.9 us
    all_to_all x1, waiting for transfers between devices, per_device(): lax.all_to_all(pieces.astype(jnp.float16), 'wide', 0, 0, tiled=True, axis...  9.27 us
    ppermute x1, starting transfers between devices, per_device(): other = lax.ppermute(sent, 'wide', SWAP)  7.93 us
    ppermute x1, starting transfers between devices, per_device(): edge_low = lax.ppermute(low_part, 'wide', EDGE_LOW)  7.54 us
    all_to_all x1, starting transfers between devices, per_device(): lax.all_to_all(pieces.astype(jnp.float16), 'wide', 0, 0, tiled=True, axis...  6.88 us
  transfers between devices with their start and end apart: 6, of which 5 were waited for; matrix products, arithmetic and copies ran while one was open for 4% of the time, Pallas kernels for 5%

profile of v6, /device:TPU:7, one launch (start us, length us, event | category | flops | bytes accessed | tf_op | source)
XLA Modules:
  0.0 188.2 jit_solution(3561352220455971600)
XLA Ops:
  0.6 0.0 copy-start.5
  0.6 0.0 copy-start.6
  0.6 1.4 copy.16
  2.1 0.0 copy-done.5
  2.1 0.3 copy.9
  2.5 0.0 copy-start.7
  2.5 0.0 copy-done.6
  2.5 0.1 copy.10
  2.8 0.1 slice_dynamic-update-slice_fusion
  3.0 0.2 copy-done.7
  3.2 0.0 copy-start
  3.2 0.0 copy-start.1
  3.2 0.0 copy-start.2
  3.2 89.8 %all_to_all.15.first = bf16[16,400,128]{2,1,0:T(8,128)(2,1)S(1)} all-to-all(bf16[16,400,128]{2,1,0:T(8,128)(2,1)S(1)} %pad_dynamic-update-slice_fusion), channel_id=1, replica_groups=mesh['wide'=32,'narrow'=16] {'narrow'}, dimensions={0} | all-to-all | bytes 3276800 | tf_op jit(solution)/shard_map/all_to_all | solution.py:231
  93.1 0.0 copy-done
  93.1 0.0 copy-done.1
  93.1 0.0 copy-done.2
  93.1 1.8 shard_map.86
  94.8 1.0 convert_element_type.26
  95.9 6.9 %all-to-all-start.1 = ((f16[16,208,128]{2,1,0:T(8,128)(2,1)}), f16[16,208,128]{2,1,0:T(8,128)(2,1)}, u32[]{:S(2)}, u32[]{:S(2)}) async-start(f16[16,208,128]{2,1,0:T(8,128)(2,1)} %convert_element_type.26), calls=%async_computation.1 | async-start | bytes 1703936 | tf_op jit(solution)/shard_map/all_to_all | solution.py:238
  102.8 0.1 pad.8.clone
  102.8 0.7 slice.70
  103.6 1.3 collective-permute-start.2
  104.9 0.8 slice.68
  105.7 9.3 %all-to-all-done.1 = f16[16,208,128]{2,1,0:T(8,128)(2,1)} async-done(((f16[16,208,128]{2,1,0:T(8,128)(2,1)}), f16[16,208,128]{2,1,0:T(8,128)(2,1)}, u32[]{:S(2)}, u32[]{:S(2)}) %all-to-all-start.1) | async-done | bytes 852000 | tf_op jit(solution)/shard_map/all_to_all | solution.py:238
  115.0 2.2 %collective-permute-start = (bf16[16,128,128]{2,1,0:T(8,128)(2,1)}, bf16[16,128,128]{2,1,0:T(8,128)(2,1)S(1)}, u32[]{:S(2)}, u32[]{:S(2)}) collective-permute-start(bf16[16,128,128]{2,1,0:T(8,128)(2,1)} %slice.68), channel_id=1, source_target_pairs={{0,16},{16,32},{32,48},{48,0},{64,80},{80,96},{96,112},{112,64},{1... | collective-permute-start | bytes 1572872 | tf_op jit(solution)/shard_map/ppermute | solution.py:242
  117.2 0.8 convert_reduce_fusion
  118.0 0.8 fusion.5
  118.8 1.3 fusion
  120.1 0.1 maximum_maximum_fusion
  120.2 7.9 %collective-permute-start.1 = (f16[208,128]{1,0:T(8,128)(2,1)S(1)}, f16[208,128]{1,0:T(8,128)(2,1)S(1)}, u32[]{:S(2)}, u32[]{:S(2)}) collective-permute-start(f16[208,128]{1,0:T(8,128)(2,1)S(1)} %maximum_maximum_fusion), channel_id=1, source_target_pairs={{0,64},{16,80},{32,96},{48,112},{64,0},{80,16},{96,32},{112,48},{1... | collective-permute-start | bytes 159752 | tf_op jit(solution)/shard_map/ppermute | solution.py:251
  128.1 1.6 collective-permute-done.side
  129.7 0.7 slice.69
  130.4 0.0 copy-start.3
  130.4 0.8 copy-done.3
  131.2 14.4 %collective-permute-done.2.edge_high = bf16[16,64,128]{2,1,0:T(8,128)(2,1)S(1)} collective-permute-done((bf16[16,64,128]{2,1,0:T(8,128)(2,1)}, bf16[16,64,128]{2,1,0:T(8,128)(2,1)S(1)}, u32[]{:S(2)}, u32[]{:S(2)}) %collective-permute-start.2) | collective-permute-done | bytes 262176 | tf_op jit(solution)/shard_map/ppermute | solution.py:233
  145.6 0.0 collective-permute-done.1
  145.6 1.1 broadcast_in_dim.5
  146.7 5.1 %all-to-all-start.2 = ((f16[16,192,128]{2,1,0:T(8,128)(2,1)}), f16[16,192,128]{2,1,0:T(8,128)(2,1)}, u32[]{:S(2)}, u32[]{:S(2)}) async-start(f16[16,192,128]{2,1,0:T(8,128)(2,1)} %broadcast_in_dim.5), calls=%async_computation.2 | async-start | bytes 1572864 | tf_op jit(solution)/shard_map/all_to_all | solution.py:261
  151.8 7.5 %collective-permute-start.3 = (bf16[16,64,128]{2,1,0:T(8,128)(2,1)}, bf16[16,64,128]{2,1,0:T(8,128)(2,1)}, u32[]{:S(2)}, u32[]{:S(2)}) collective-permute-start(bf16[16,64,128]{2,1,0:T(8,128)(2,1)} %slice.69), channel_id=1, source_target_pairs={{0,64},{64,128},{128,192},{192,256},{256,320},{320,384},{384,448},... | collective-permute-start | bytes 786440 | tf_op jit(solution)/shard_map/ppermute | solution.py:253
  159.4 3.8 %all-to-all-done.2 = f16[16,192,128]{2,1,0:T(8,128)(2,1)} async-done(((f16[16,192,128]{2,1,0:T(8,128)(2,1)}), f16[16,192,128]{2,1,0:T(8,128)(2,1)}, u32[]{:S(2)}, u32[]{:S(2)}) %all-to-all-start.2) | async-done | bytes 786464 | tf_op jit(solution)/shard_map/all_to_all | solution.py:261
  163.2 1.2 convert_element_type.32.every
  164.4 0.0 copy-start.4
  164.5 8.7 %shard_map.87 = f32[1024,128]{1,0:T(8,128)} custom-call(f32[8,128]{1,0:T(8,128)S(1)} %concatenate.12.powers, f32[16,192,128]{2,1,0:T(8,128)S(1)} %convert_element_type.32.every, f32[256,512]{1,0:T(8,128)S(1)} %bitcast.33, f32[256,512]{1,0:T(8,128)S(1)} %bitcast.35, f32[512,256]{1,0:T(8,128)S(1)} %bitcast.37, bf16[16,400,128]{2,1,0:T(8,128)(2,1)S(1)} %all_to_all.15.first), custom_call_target="tpu_custom_call" | custom-call | flops 1048576 | bytes 4194304 | tf_op jit(solution)/shard_map/pallas_call | solution.py:184
  173.2 9.9 %collective-permute-done.3.edge_low = bf16[16,64,128]{2,1,0:T(8,128)(2,1)} collective-permute-done((bf16[16,64,128]{2,1,0:T(8,128)(2,1)}, bf16[16,64,128]{2,1,0:T(8,128)(2,1)}, u32[]{:S(2)}, u32[]{:S(2)}) %collective-permute-start.3) | collective-permute-done | bytes 262176 | tf_op jit(solution)/shard_map/ppermute | solution.py:253
  183.1 0.0 copy-done.4
  183.1 5.1 %shard_map.88 = f32[1024,128]{1,0:T(8,128)} custom-call(s32[1]{0:T(128)} %bitcast.place, bf16[16,400,128]{2,1,0:T(8,128)(2,1)S(1)} %all_to_all.15.first, bf16[16,128,128]{2,1,0:T(8,128)(2,1)S(1)} %copy-done.4, bf16[16,64,128]{2,1,0:T(8,128)(2,1)} %collective-permute-done.3.edge_low, bf16[16,64,128]{2,1,0:T(8,128)(2,1)S(1)} %collective-permute-done.2.edge_high), custom_call_target="tpu_custom_call" | custom-call | flops 1048576 | bytes 4194304 | tf_op jit(solution)/shard_map/pallas_call | solution.py:184
  (16 shorter events, 0.4 us)
Async XLA Ops:
  0.6 1.5 copy-start.5
  0.6 1.8 copy-start.6
  2.5 0.7 copy-start.7
  3.2 89.9 %copy-start = (f32[1,256,512]{2,1,0:T(8,128)S(1)}, f32[1,256,512]{2,1,0:T(8,128)}, u32[]{:S(2)}) copy-start(f32[1,256,512]{2,1,0:T(8,128)} %param.11) | copy-start | bytes 1572868
  3.2 89.9 %copy-start.1 = (f32[1,256,512]{2,1,0:T(8,128)S(1)}, f32[1,256,512]{2,1,0:T(8,128)}, u32[]{:S(2)}) copy-start(f32[1,256,512]{2,1,0:T(8,128)} %param.12) | copy-start | bytes 1572868
  3.2 89.9 %copy-start.2 = (f32[1,512,256]{2,1,0:T(8,128)S(1)}, f32[1,512,256]{2,1,0:T(8,128)}, u32[]{:S(2)}) copy-start(f32[1,512,256]{2,1,0:T(8,128)} %param.13) | copy-start | bytes 1572868
  95.9 19.1 %all-to-all-start.1 = ((f16[16,208,128]{2,1,0:T(8,128)(2,1)}), f16[16,208,128]{2,1,0:T(8,128)(2,1)}, u32[]{:S(2)}, u32[]{:S(2)}) async-start(f16[16,208,128]{2,1,0:T(8,128)(2,1)} %convert_element_type.26), calls=%async_computation.1 | async-start | bytes 1703936 | tf_op jit(solution)/shard_map/all_to_all | solution.py:238
  103.6 42.0 %collective-permute-start.2 = (bf16[16,64,128]{2,1,0:T(8,128)(2,1)}, bf16[16,64,128]{2,1,0:T(8,128)(2,1)S(1)}, u32[]{:S(2)}, u32[]{:S(2)}) collective-permute-start(bf16[16,64,128]{2,1,0:T(8,128)(2,1)} %slice.70), channel_id=1, source_target_pairs={{48,64},{112,128},{176,192},{240,256},{304,320},{368,384},{432,448... | collective-permute-start | bytes 786440 | tf_op jit(solution)/shard_map/ppermute | solution.py:233
  115.0 14.7 %collective-permute-start = (bf16[16,128,128]{2,1,0:T(8,128)(2,1)}, bf16[16,128,128]{2,1,0:T(8,128)(2,1)S(1)}, u32[]{:S(2)}, u32[]{:S(2)}) collective-permute-start(bf16[16,128,128]{2,1,0:T(8,128)(2,1)} %slice.68), channel_id=1, source_target_pairs={{0,16},{16,32},{32,48},{48,0},{64,80},{80,96},{96,112},{112,64},{1... | collective-permute-start | bytes 1572872 | tf_op jit(solution)/shard_map/ppermute | solution.py:242
  120.2 25.4 %collective-permute-start.1 = (f16[208,128]{1,0:T(8,128)(2,1)S(1)}, f16[208,128]{1,0:T(8,128)(2,1)S(1)}, u32[]{:S(2)}, u32[]{:S(2)}) collective-permute-start(f16[208,128]{1,0:T(8,128)(2,1)S(1)} %maximum_maximum_fusion), channel_id=1, source_target_pairs={{0,64},{16,80},{32,96},{48,112},{64,0},{80,16},{96,32},{112,48},{1... | collective-permute-start | bytes 159752 | tf_op jit(solution)/shard_map/ppermute | solution.py:251
  130.4 0.8 copy-start.3
  146.7 16.5 %all-to-all-start.2 = ((f16[16,192,128]{2,1,0:T(8,128)(2,1)}), f16[16,192,128]{2,1,0:T(8,128)(2,1)}, u32[]{:S(2)}, u32[]{:S(2)}) async-start(f16[16,192,128]{2,1,0:T(8,128)(2,1)} %broadcast_in_dim.5), calls=%async_computation.2 | async-start | bytes 1572864 | tf_op jit(solution)/shard_map/all_to_all | solution.py:261
  151.8 31.3 %collective-permute-start.3 = (bf16[16,64,128]{2,1,0:T(8,128)(2,1)}, bf16[16,64,128]{2,1,0:T(8,128)(2,1)}, u32[]{:S(2)}, u32[]{:S(2)}) collective-permute-start(bf16[16,64,128]{2,1,0:T(8,128)(2,1)} %slice.69), channel_id=1, source_target_pairs={{0,64},{64,128},{128,192},{192,256},{256,320},{320,384},{384,448},... | collective-permute-start | bytes 786440 | tf_op jit(solution)/shard_map/ppermute | solution.py:253
  164.4 18.7 %copy-start.4 = (bf16[16,128,128]{2,1,0:T(8,128)(2,1)S(1)}, bf16[16,128,128]{2,1,0:T(8,128)(2,1)}, u32[]{:S(2)}) copy-start(bf16[16,128,128]{2,1,0:T(8,128)(2,1)} %copy-done.3) | copy-start | bytes 1572868

commit v7 on v5

--- a/solution.py
+++ b/solution.py
@@ -39,7 +39,7 @@
 def gradient_kernel(first, gate, up, down, out):
     group = first.shape[0]
     span = group * TOK
-    logits = first[:, 12 * TOK : 12 * TOK + 16, :].astype(jnp.float32)
+    logits = first[:, 8 * TOK : 8 * TOK + 16, :].astype(jnp.float32)
     rate_blocks = []
     for source in range(group):
         turned = logits[source].T[:TOK]
@@ -88,7 +88,7 @@
     out[:, 3 * FHID // LANES * rows :, :] = jnp.broadcast_to(tag[None], (PLANE, 16, LANES))
 
 
-def attention_kernel(place, first, side, edge_low, edge_high, out, earlier):
+def attention_kernel(place, first, second, side, edge_low, edge_high, out, earlier):
     span = first.shape[0] * TOK
     scale = 1.0 / math.sqrt(LANES)
     tile = 128
@@ -110,7 +110,7 @@
         earlier[...] = side[...]
 
     for head in range(heads):
-        query = block_rows(first, 8 + head, 1)
+        query = block_rows(second, head, 1)
         key = jnp.concatenate([block_rows(earlier, head, 1), block_rows(first, head, 1)], axis=0)
         value = jnp.concatenate(
             [block_rows(earlier, heads + head, 1), block_rows(first, heads + head, 1)], axis=0
@@ -150,7 +150,7 @@
     return ortho_all
 
 
-def apply_kernel(powers, every, gate, up, down, first, out):
+def apply_kernel(powers, every, gate, up, down, second, out):
     rows = FD // PLANE
     starts = []
     for matrix in range(3):
@@ -166,7 +166,7 @@
     new_gate = (gate[...] + ortho[0]).astype(jnp.bfloat16)
     new_up = (up[...] + ortho[1]).astype(jnp.bfloat16)
     new_down = (down[...] + ortho[2].T).astype(jnp.bfloat16)
-    query = block_rows(first, 10, 2)
+    query = block_rows(second, 2, 2)
     gate_pre = dot(query, new_gate)
     up_pre = dot(query, new_up)
     hidden = (gate_pre * (1.0 / (1.0 + jnp.exp(-gate_pre))) * up_pre).astype(jnp.bfloat16)
@@ -225,19 +225,18 @@
     fast = fast_inputs.transpose(1, 0, 2)
     fast = [fast[:, :, i * LANES : (i + 1) * LANES] for i in range(6)]
     logits = jnp.pad(rate_logits.transpose(1, 2, 0), ((0, 0), (0, 13), (0, LANES - rows)))
-    first = jnp.concatenate(
-        [pair[:, :, LANES:], value, *fast[2:], pair[:, :, :LANES], *fast[:2], logits], axis=1
-    )
+    first = jnp.concatenate([pair[:, :, LANES:], value, *fast[2:], logits], axis=1)
+    second = jnp.concatenate([pair[:, :, :LANES], *fast[:2]], axis=1)
     first = lax.all_to_all(first, "narrow", 0, 0, tiled=True)
     tail = first[:, : 4 * rows]
-
     weights = (gate_fast[0], up_fast[0], down_fast[0])
     count = 3 * FHID // LANES * FD // PLANE
     pieces = call(gradient_kernel, (PLANE, count + 16, LANES), (first, *weights), FLOPS)
     got = lax.all_to_all(
         pieces.astype(jnp.float16), "wide", 0, 0, tiled=True, axis_index_groups=PLANES
     )
-    got, tail = lax.optimization_barrier((got, tail))
+    got, tail, second = lax.optimization_barrier((got, tail, second))
+    second = lax.all_to_all(second, "narrow", 0, 0, tiled=True)
     side = lax.ppermute(tail, "wide", AROUND)
     powers = got[:, count : count + 3].astype(jnp.float32)
     top = jnp.max(powers, axis=0)
@@ -260,19 +259,12 @@
         jnp.exp2(other_top - both) * 0.5
     )[:, None]
     whole = whole.astype(jnp.float16).reshape(count, LANES)
-    every = lax.all_to_all(
-        jnp.broadcast_to(whole[None], (PLANE, count, LANES)),
-        "wide",
-        0,
-        0,
-        tiled=True,
-        axis_index_groups=PLANES,
-    )
+    every = lax.all_gather(whole, "wide", axis_index_groups=PLANES)
     factors = jnp.concatenate([jnp.exp2(both - 8.0), jnp.zeros((5, LANES), jnp.float32)], axis=0)
     fast_out = call(
         apply_kernel,
         (span * FD // LANES, LANES),
-        (factors, every.astype(jnp.float32), *weights, first),
+        (factors, every.astype(jnp.float32), *weights, second),
         FLOPS,
     )
     place = lax.axis_index("wide").reshape(1)
@@ -280,7 +272,7 @@
     window_out = call(
         attention_kernel,
         (span * own, LANES),
-        (place, first, side, edge_low, edge_high),
+        (place, first, second, side, edge_low, edge_high),
         FLOPS,
         1,
         [pltpu.VMEM((PLANE, 4 * TOK, LANES), jnp.bfloat16)],

time: 193 us -> 196 us (1.016)
  the two profiles are of different devices: /device:TPU:7 before, /device:TPU:162 now
where the time goes in v7:
time: 196 us; the launch traced here: 195 us
  blocking collectives  98.4 us (50%)
  waiting for transfers between devices  35.6 us (18%)
  starting transfers between devices  32.6 us (17%)
  Pallas kernels  15.6 us (8%)
  local copies, waits for them, and re-layouts  9.69 us (5%)
  other arithmetic  2.32 us (1%)
    all_to_all x1, blocking collectives, per_device(): first = lax.all_to_all(first, 'narrow', 0, 0, tiled=True)  60 us
    all_gather x1, blocking collectives, per_device(): every = lax.all_gather(whole, 'wide', axis_index_groups=PLANES)  38.4 us
    ppermute x1, waiting for transfers between devices, per_device(): other = lax.ppermute(sent, 'wide', SWAP)  19.6 us
    pallas_call x3, Pallas kernels, call(): pl.pallas_call(kernel, out_shape=jax.ShapeDtypeStruct(shape, jnp.float32)...  15.6 us
    all_to_all x1, waiting for transfers between devices, per_device(): lax.all_to_all(pieces.astype(jnp.float16), 'wide', 0, 0, tiled=True, axis...  11.4 us
    all_to_all x1, starting transfers between devices, per_device(): second = lax.all_to_all(second, 'narrow', 0, 0, tiled=True)  10.1 us
    ppermute x1, starting transfers between devices, per_device(): other = lax.ppermute(sent, 'wide', SWAP)  8.23 us
    all_to_all x1, starting transfers between devices, per_device(): lax.all_to_all(pieces.astype(jnp.float16), 'wide', 0, 0, tiled=True, axis...  7.48 us
  transfers between devices with their start and end apart: 6, of which 3 were waited for; matrix products, arithmetic and copies ran while one was open for 2% of the time, Pallas kernels for 4%

profile of v7, /device:TPU:162, one launch (start us, length us, event | category | flops | bytes accessed | tf_op | source)
XLA Modules:
  0.0 195.1 jit_solution(16550170527849661008)
XLA Ops:
  0.6 0.0 copy-start.8
  0.6 1.4 copy.16
  2.1 0.0 copy-start.9
  2.1 0.0 copy-done.8
  2.1 0.3 copy.9
  2.4 0.1 fusion.17
  2.5 0.5 copy-done.9
  3.0 0.1 copy.10
  3.1 0.0 copy-start.10
  3.3 0.1 fusion.16
  3.4 0.4 copy-done.10
  3.9 0.0 copy-start
  3.9 0.0 copy-start.2
  3.9 0.0 copy-start.4
  3.9 60.0 %all_to_all.15.first = bf16[16,272,128]{2,1,0:T(8,128)(2,1)S(1)} all-to-all(bf16[16,272,128]{2,1,0:T(8,128)(2,1)S(1)} %pad_dynamic-update-slice_fusion), channel_id=1, replica_groups=mesh['wide'=32,'narrow'=16] {'narrow'}, dimensions={0} | all-to-all | bytes 2228224 | tf_op jit(solution)/shard_map/all_to_all | solution.py:230
  63.9 0.0 copy-done
  63.9 0.0 copy-done.2
  63.9 0.0 copy-done.4
  63.9 1.8 shard_map.86
  65.7 1.0 convert_element_type.28
  66.7 7.5 %all-to-all-start.1 = ((f16[16,208,128]{2,1,0:T(8,128)(2,1)}), f16[16,208,128]{2,1,0:T(8,128)(2,1)S(1)}, u32[]{:S(2)}, u32[]{:S(2)}) async-start(f16[16,208,128]{2,1,0:T(8,128)(2,1)} %convert_element_type.28), calls=%async_computation.1 | async-start | bytes 1703936 | tf_op jit(solution)/shard_map/all_to_all | solution.py:235
  74.2 0.8 pad_maximum_fusion
  75.0 0.8 slice.65
  75.8 11.4 %all-to-all-done.1 = f16[16,208,128]{2,1,0:T(8,128)(2,1)S(1)} async-done(((f16[16,208,128]{2,1,0:T(8,128)(2,1)}), f16[16,208,128]{2,1,0:T(8,128)(2,1)S(1)}, u32[]{:S(2)}, u32[]{:S(2)}) %all-to-all-start.1) | async-done | bytes 852000 | tf_op jit(solution)/shard_map/all_to_all | solution.py:235
  87.3 10.1 %all-to-all-start.2 = ((bf16[16,128,128]{2,1,0:T(8,128)(2,1)}), bf16[16,128,128]{2,1,0:T(8,128)(2,1)S(1)}, u32[]{:S(2)}, u32[]{:S(2)}) async-start(bf16[16,128,128]{2,1,0:T(8,128)(2,1)} %pad_maximum_fusion), calls=%async_computation.2 | async-start | bytes 1048576 | tf_op jit(solution)/shard_map/all_to_all | solution.py:239
  97.4 0.1 pad.8.clone
  97.5 2.5 %collective-permute-start = (bf16[16,128,128]{2,1,0:T(8,128)(2,1)}, bf16[16,128,128]{2,1,0:T(8,128)(2,1)S(1)}, u32[]{:S(2)}, u32[]{:S(2)}) collective-permute-start(bf16[16,128,128]{2,1,0:T(8,128)(2,1)} %slice.65), channel_id=1, source_target_pairs={{0,16},{16,32},{32,48},{48,0},{64,80},{80,96},{96,112},{112,64},{1... | collective-permute-start | bytes 1572872 | tf_op jit(solution)/shard_map/ppermute | solution.py:240
  100.0 0.2 fusion
  100.2 0.1 maximum_maximum_fusion
  100.3 8.2 %collective-permute-start.1 = (f16[208,128]{1,0:T(8,128)(2,1)S(1)}, f16[208,128]{1,0:T(8,128)(2,1)S(1)}, u32[]{:S(2)}, u32[]{:S(2)}) collective-permute-start(f16[208,128]{1,0:T(8,128)(2,1)S(1)} %maximum_maximum_fusion), channel_id=1, source_target_pairs={{0,64},{16,80},{32,96},{48,112},{64,0},{80,16},{96,32},{112,48},{1... | collective-permute-start | bytes 159752 | tf_op jit(solution)/shard_map/ppermute | solution.py:249
  108.5 1.7 slice.57
  110.2 4.6 %collective-permute-done.side = bf16[16,128,128]{2,1,0:T(8,128)(2,1)S(1)} collective-permute-done((bf16[16,128,128]{2,1,0:T(8,128)(2,1)}, bf16[16,128,128]{2,1,0:T(8,128)(2,1)S(1)}, u32[]{:S(2)}, u32[]{:S(2)}) %collective-permute-start) | collective-permute-done | bytes 524320 | tf_op jit(solution)/shard_map/ppermute | solution.py:240
  114.8 0.8 slice.69
  115.5 19.6 %collective-permute-done.1 = f16[208,128]{1,0:T(8,128)(2,1)S(1)} collective-permute-done((f16[208,128]{1,0:T(8,128)(2,1)S(1)}, f16[208,128]{1,0:T(8,128)(2,1)S(1)}, u32[]{:S(2)}, u32[]{:S(2)}) %collective-permute-start.1) | collective-permute-done | bytes 53280 | tf_op jit(solution)/shard_map/ppermute | solution.py:249
  135.2 3.0 %collective-permute-start.2 = (bf16[16,64,128]{2,1,0:T(8,128)(2,1)}, bf16[16,64,128]{2,1,0:T(8,128)(2,1)S(1)}, u32[]{:S(2)}, u32[]{:S(2)}) collective-permute-start(bf16[16,64,128]{2,1,0:T(8,128)(2,1)} %slice.69), channel_id=1, source_target_pairs={{0,64},{64,128},{128,192},{192,256},{256,320},{320,384},{384,448},... | collective-permute-start | bytes 786440 | tf_op jit(solution)/shard_map/ppermute | solution.py:253
  138.2 1.3 collective-permute-start.3
  139.6 38.4 %all-gather = f16[3072,128]{1,0:T(8,128)(2,1)S(1)} all-gather(f16[192,128]{1,0:T(8,128)(2,1)S(1)} %fusion.2), channel_id=2, replica_groups={{0,16,32,48,128,144,160,176,256,272,288,304,384,400,416,432},{64,80,96,..., dimensions={0}, use_global_device_ids=true | all-gather | bytes 835584 | tf_op jit(solution)/shard_map/all_gather | solution.py:262
  178.0 0.1 convert.10.every
  178.2 0.0 all-to-all-done.2.second
  178.2 0.0 copy-start.1
  178.2 1.0 copy-done.1
  179.2 1.0 copy-done.3
  180.3 1.0 copy-done.5
  181.3 8.7 %shard_map.87 = f32[1024,128]{1,0:T(8,128)} custom-call(f32[8,128]{1,0:T(8,128)S(1)} %concatenate.16.powers, f32[16,192,128]{2,1,0:T(8,128)S(1)} %convert.10.every, f32[256,512]{1,0:T(8,128)S(1)} %bitcast.35, f32[256,512]{1,0:T(8,128)S(1)} %bitcast.37, f32[512,256]{1,0:T(8,128)S(1)} %bitcast.39, bf16[16,128,128]{2,1,0:T(8,128)(2,1)S(1)} %all-to-all-done.2.second), custom_call_target="tpu_custom_call" | custom-call | flops 1048576 | bytes 4194304 | tf_op jit(solution)/shard_map/pallas_call | solution.py:184
  190.0 0.0 collective-permute-done.2.edge_low
  190.0 0.0 collective-permute-done.3.edge_high
  190.1 0.0 copy-done.7
  190.1 5.1 %shard_map.88 = f32[1024,128]{1,0:T(8,128)} custom-call(s32[1]{0:T(128)} %bitcast.place, bf16[16,272,128]{2,1,0:T(8,128)(2,1)S(1)} %all_to_all.15.first, bf16[16,128,128]{2,1,0:T(8,128)(2,1)S(1)} %all-to-all-done.2.second, bf16[16,128,128]{2,1,0:T(8,128)(2,1)S(1)} %copy-done.7, bf16[16,64,128]{2,1,0:T(8,128)(2,1)S(1)} %collective-permute-done.2.edge_low, ...), custom_call_target="tpu_custom_call" | custom-call | flops 1048576 | bytes 4194304 | tf_op jit(solution)/shard_map/pallas_call | solution.py:184
  (19 shorter events, 0.3 us)
Async XLA Ops:
  0.6 1.5 copy-start.8
  2.1 1.0 copy-start.9
  3.1 0.7 copy-start.10
  3.9 60.0 %copy-start = (f32[1,256,512]{2,1,0:T(8,128)S(1)}, f32[1,256,512]{2,1,0:T(8,128)}, u32[]{:S(2)}) copy-start(f32[1,256,512]{2,1,0:T(8,128)} %param.11) | copy-start | bytes 1572868
  3.9 60.0 %copy-start.2 = (f32[1,256,512]{2,1,0:T(8,128)S(1)}, f32[1,256,512]{2,1,0:T(8,128)}, u32[]{:S(2)}) copy-start(f32[1,256,512]{2,1,0:T(8,128)} %param.12) | copy-start | bytes 1572868
  3.9 60.0 %copy-start.4 = (f32[1,512,256]{2,1,0:T(8,128)S(1)}, f32[1,512,256]{2,1,0:T(8,128)}, u32[]{:S(2)}) copy-start(f32[1,512,256]{2,1,0:T(8,128)} %param.13) | copy-start | bytes 1572868
  66.7 20.6 %all-to-all-start.1 = ((f16[16,208,128]{2,1,0:T(8,128)(2,1)}), f16[16,208,128]{2,1,0:T(8,128)(2,1)S(1)}, u32[]{:S(2)}, u32[]{:S(2)}) async-start(f16[16,208,128]{2,1,0:T(8,128)(2,1)} %convert_element_type.28), calls=%async_computation.1 | async-start | bytes 1703936 | tf_op jit(solution)/shard_map/all_to_all | solution.py:235
  87.3 90.9 %all-to-all-start.2 = ((bf16[16,128,128]{2,1,0:T(8,128)(2,1)}), bf16[16,128,128]{2,1,0:T(8,128)(2,1)S(1)}, u32[]{:S(2)}, u32[]{:S(2)}) async-start(bf16[16,128,128]{2,1,0:T(8,128)(2,1)} %pad_maximum_fusion), calls=%async_computation.2 | async-start | bytes 1048576 | tf_op jit(solution)/shard_map/all_to_all | solution.py:239
  97.5 17.3 %collective-permute-start = (bf16[16,128,128]{2,1,0:T(8,128)(2,1)}, bf16[16,128,128]{2,1,0:T(8,128)(2,1)S(1)}, u32[]{:S(2)}, u32[]{:S(2)}) collective-permute-start(bf16[16,128,128]{2,1,0:T(8,128)(2,1)} %slice.65), channel_id=1, source_target_pairs={{0,16},{16,32},{32,48},{48,0},{64,80},{80,96},{96,112},{112,64},{1... | collective-permute-start | bytes 1572872 | tf_op jit(solution)/shard_map/ppermute | solution.py:240
  100.3 34.9 %collective-permute-start.1 = (f16[208,128]{1,0:T(8,128)(2,1)S(1)}, f16[208,128]{1,0:T(8,128)(2,1)S(1)}, u32[]{:S(2)}, u32[]{:S(2)}) collective-permute-start(f16[208,128]{1,0:T(8,128)(2,1)S(1)} %maximum_maximum_fusion), channel_id=1, source_target_pairs={{0,64},{16,80},{32,96},{48,112},{64,0},{80,16},{96,32},{112,48},{1... | collective-permute-start | bytes 159752 | tf_op jit(solution)/shard_map/ppermute | solution.py:249
  114.7 63.3 %copy-start.6 = (bf16[16,128,128]{2,1,0:T(8,128)(2,1)}, bf16[16,128,128]{2,1,0:T(8,128)(2,1)S(1)}, u32[]{:S(2)}) copy-start(bf16[16,128,128]{2,1,0:T(8,128)(2,1)S(1)} %collective-permute-done.side) | copy-start | bytes 1572868
  135.2 54.9 %collective-permute-start.2 = (bf16[16,64,128]{2,1,0:T(8,128)(2,1)}, bf16[16,64,128]{2,1,0:T(8,128)(2,1)S(1)}, u32[]{:S(2)}, u32[]{:S(2)}) collective-permute-start(bf16[16,64,128]{2,1,0:T(8,128)(2,1)} %slice.69), channel_id=1, source_target_pairs={{0,64},{64,128},{128,192},{192,256},{256,320},{320,384},{384,448},... | collective-permute-start | bytes 786440 | tf_op jit(solution)/shard_map/ppermute | solution.py:253
  138.2 51.8 %collective-permute-start.3 = (bf16[16,64,128]{2,1,0:T(8,128)(2,1)}, bf16[16,64,128]{2,1,0:T(8,128)(2,1)}, u32[]{:S(2)}, u32[]{:S(2)}) collective-permute-start(bf16[16,64,128]{2,1,0:T(8,128)(2,1)} %slice.57), channel_id=1, source_target_pairs={{48,64},{112,128},{176,192},{240,256},{304,320},{368,384},{432,448... | collective-permute-start | bytes 786440 | tf_op jit(solution)/shard_map/ppermute | solution.py:254
  178.2 1.0 copy-start.1
  179.2 1.0 copy-start.3
  180.3 1.0 copy-start.5
  181.3 8.8 %copy-start.7 = (bf16[16,128,128]{2,1,0:T(8,128)(2,1)S(1)}, bf16[16,128,128]{2,1,0:T(8,128)(2,1)}, u32[]{:S(2)}) copy-start(bf16[16,128,128]{2,1,0:T(8,128)(2,1)} %copy-done.6) | copy-start | bytes 1572868

commit v8 on v6

--- a/solution.py
+++ b/solution.py
@@ -20,6 +20,7 @@
 
 XS, HALVES, YS = 4, 2, 4
 PLANE = XS * YS
+GROUP = 16
 VMEM_LIMIT = 48 * 1024 * 1024
 
 
@@ -88,7 +89,7 @@
     out[:, 3 * FHID // LANES * rows :, :] = jnp.broadcast_to(tag[None], (PLANE, 16, LANES))
 
 
-def attention_kernel(place, first, side, edge_low, edge_high, out, earlier):
+def attention_kernel(place, first, side, edge, out, earlier):
     span = first.shape[0] * TOK
     scale = 1.0 / math.sqrt(LANES)
     tile = 128
@@ -97,15 +98,14 @@
     col = lax.broadcasted_iota(jnp.int32, (tile, reach), 1)
     band = (col > row) & (col - row <= span)
     begin = jnp.where(place[0] == 0, span, 0)
-    edge = lax.rem(place[0], YS) == 0
+    on_edge = lax.rem(place[0], YS) == 0
     heads = 2
 
-    @pl.when(edge)
+    @pl.when(on_edge)
     def _():
-        earlier[:, : 2 * TOK, :] = edge_low[...]
-        earlier[:, 2 * TOK :, :] = edge_high[...]
-
-    @pl.when(jnp.logical_not(edge))
+        earlier[...] = edge[...]
+
+    @pl.when(jnp.logical_not(on_edge))
     def _():
         earlier[...] = side[...]
 
@@ -203,15 +203,27 @@
     for half in range(HALVES)
     for y in range(YS)
 ]
-AROUND = [
-    (wide_index(x, half, y), wide_index(x, half, (y + 1) % YS))
-    for x in range(XS)
-    for half in range(HALVES)
+LINES = [(x, half) for x in range(XS) for half in range(HALVES)]
+NEXT = [
+    (wide_index(*line, y), wide_index(*line, y + 1)) for line in LINES for y in range(YS - 1)
+]
+RELAY = [
+    [(wide_index(*line, YS - 1), wide_index(*line, y)) for line in LINES] for y in range(YS - 1)
+]
+ENDS = [(x, half, x + half, 1 - half) for x in range(XS) for half in range(HALVES)][:-1]
+
+
+def other_core(pairs):
+    return [
+        (a * GROUP + i, b * GROUP + (i ^ 1)) for a, b in pairs for i in range(GROUP)
+    ]
+
+
+EDGES = [
+    other_core([(wide_index(x, half, y), wide_index(*after, 0)) for x, half, *after in ENDS])
     for y in range(YS)
 ]
-ENDS = [(x, half, x + half, 1 - half) for x in range(XS) for half in range(HALVES)][:-1]
-EDGE_LOW = [(wide_index(x, half, 0), wide_index(*after, 0)) for x, half, *after in ENDS]
-EDGE_HIGH = [(wide_index(x, half, YS - 1), wide_index(*after, 0)) for x, half, *after in ENDS]
+CORES = other_core([(wide_index(*line, 0), wide_index(*line, 0)) for line in LINES])
 FLOPS = 1 << 20
 
 
@@ -230,7 +242,10 @@
     )
     first = lax.all_to_all(first, "narrow", 0, 0, tiled=True)
     tail = first[:, : 4 * rows]
-    edge_high = lax.ppermute(first[:, 2 * rows : 4 * rows], "wide", EDGE_HIGH)
+    quarters = [first[:, i * rows : (i + 1) * rows] for i in range(YS)]
+    quarters = [
+        lax.ppermute(part, "wide", pairs) for part, pairs in zip(quarters, RELAY)
+    ] + quarters[-1:]
 
     weights = (gate_fast[0], up_fast[0], down_fast[0])
     count = 3 * FHID // LANES * FD // PLANE
@@ -238,8 +253,11 @@
     got = lax.all_to_all(
         pieces.astype(jnp.float16), "wide", 0, 0, tiled=True, axis_index_groups=PLANES
     )
-    got, tail = lax.optimization_barrier((got, tail))
-    side = lax.ppermute(tail, "wide", AROUND)
+    got, tail, quarters = lax.optimization_barrier((got, tail, quarters))
+    edges = [
+        lax.ppermute(part, ("wide", "narrow"), pairs) for part, pairs in zip(quarters, EDGES)
+    ]
+    side = lax.ppermute(tail, "wide", NEXT)
     powers = got[:, count : count + 3].astype(jnp.float32)
     top = jnp.max(powers, axis=0)
     parts = got[:, :count].astype(jnp.float32).reshape(PLANE, 3, -1, LANES)
@@ -249,8 +267,7 @@
     )
     sent = sent.astype(jnp.float16)
     other = lax.ppermute(sent, "wide", SWAP)
-    other, low_part, edge_high = lax.optimization_barrier((other, side[:, : 2 * rows], edge_high))
-    edge_low = lax.ppermute(low_part, "wide", EDGE_LOW)
+    other, side = lax.optimization_barrier((other, side))
     other_top = other[count : count + 3].astype(jnp.float32)
     both = jnp.maximum(top, other_top)
     whole = half * (jnp.exp2(top - both) * 0.5)[:, None]
@@ -266,6 +283,8 @@
         tiled=True,
         axis_index_groups=PLANES,
     )
+    edge = jnp.concatenate(edges, axis=1)
+    edge = lax.ppermute(edge, ("wide", "narrow"), CORES)
     factors = jnp.concatenate([jnp.exp2(both - 8.0), jnp.zeros((5, LANES), jnp.float32)], axis=0)
     fast_out = call(
         apply_kernel,
@@ -274,11 +293,11 @@
         FLOPS,
     )
     place = lax.axis_index("wide").reshape(1)
-    edge_low, fast_out = lax.optimization_barrier((edge_low, fast_out))
+    edge, fast_out = lax.optimization_barrier((edge, fast_out))
     window_out = call(
         attention_kernel,
         (span * own, LANES),
-        (place, first, side, edge_low, edge_high),
+        (place, first, side, edge),
         FLOPS,
         1,
         [pltpu.VMEM((PLANE, 4 * TOK, LANES), jnp.bfloat16)],

time: 189 us -> 192 us (1.016)
  waiting for transfers between devices: 38.9 us -> 22.8 us
  starting transfers between devices: 30.9 us -> 46.8 us
  other arithmetic: 5.3 us -> 7.24 us
    all_to_all x1, waiting for transfers between devices: 9.27 us -> 0.01 us  [per_device(): lax.all_to_all(pieces.astype(jnp.float16), 'wide', 0, 0, tiled=True, axis...]
    all_to_all x1, starting transfers between devices: 5.11 us -> 13.1 us  [per_device(): lax.all_to_all(jnp.broadcast_to(whole[None], (PLANE, count, LANES)), 'wid...]
    ppermute x3 -> x9, starting transfers between devices: 11 us -> 18.9 us  [the longest x4 11.7 us: per_device(): lax.ppermute(part, ('wide', 'narrow'), pairs)]
    all_to_all x1, waiting for transfers between devices: 3.81 us -> 0.01 us  [per_device(): lax.all_to_all(jnp.broadcast_to(whole[None], (PLANE, count, LANES)), 'wid...]
    ppermute x3 -> x9, waiting for transfers between devices: 25.9 us -> 22.8 us  [the longest x4 11.6 us: per_device(): lax.ppermute(part, ('wide', 'narrow'), pairs)]
    unnamed x27 -> x31, local copies, waits for them, and re-layouts: 2.84 us -> 4.12 us
  transfers between devices with their start and end apart: 6 -> 12, of which waited for: 5 -> 3; matrix products, arithmetic and copies ran while one was open for 4% -> 4% of each run, Pallas kernels for 5% -> 5%
where the time goes in v8:
time: 192 us; the launch traced here: 190 us
  blocking collectives  89.8 us (47%)
  starting transfers between devices  46.8 us (24%)
  waiting for transfers between devices  22.8 us (12%)
  Pallas kernels  15.7 us (8%)
  other arithmetic  7.24 us (4%)
  local copies, waits for them, and re-layouts  6.59 us (3%)
    all_to_all x1, blocking collectives, per_device(): first = lax.all_to_all(first, 'narrow', 0, 0, tiled=True)  89.8 us
    pallas_call x3, Pallas kernels, call(): pl.pallas_call(kernel, out_shape=jax.ShapeDtypeStruct(shape, jnp.float32)...  15.7 us
    all_to_all x1, starting transfers between devices, per_device(): lax.all_to_all(jnp.broadcast_to(whole[None], (PLANE, count, LANES)), 'wid...  13.1 us
    ppermute x4, starting transfers between devices, per_device(): lax.ppermute(part, ('wide', 'narrow'), pairs)  11.7 us
    ppermute x4, waiting for transfers between devices, per_device(): lax.ppermute(part, ('wide', 'narrow'), pairs)  11.6 us
    ppermute x3, waiting for transfers between devices, per_device(): lax.ppermute(part, 'wide', pairs)  11.1 us
    ppermute x1, starting transfers between devices, per_device(): other = lax.ppermute(sent, 'wide', SWAP)  7.93 us
    all_to_all x1, starting transfers between devices, per_device(): lax.all_to_all(pieces.astype(jnp.float16), 'wide', 0, 0, tiled=True, axis...  6.88 us
  transfers between devices with their start and end apart: 12, of which 3 were waited for; matrix products, arithmetic and copies ran while one was open for 4% of the time, Pallas kernels for 5%

profile of v8, /device:TPU:7, one launch (start us, length us, event | category | flops | bytes accessed | tf_op | source)
XLA Modules:
  0.0 189.8 jit_solution(11196279338611994453)
XLA Ops:
  0.6 1.4 copy.16
  2.1 0.3 copy.9
  2.5 0.0 copy-start.7
  2.5 0.1 copy.10
  2.8 0.1 slice_dynamic-update-slice_fusion
  3.0 0.2 copy-done.7
  3.2 0.0 copy-start
  3.2 0.0 copy-start.1
  3.2 0.0 copy-start.2
  3.2 89.8 %all_to_all.15.first = bf16[16,400,128]{2,1,0:T(8,128)(2,1)S(1)} all-to-all(bf16[16,400,128]{2,1,0:T(8,128)(2,1)S(1)} %pad_dynamic-update-slice_fusion), channel_id=1, replica_groups=mesh['wide'=32,'narrow'=16] {'narrow'}, dimensions={0} | all-to-all | bytes 3276800 | tf_op jit(solution)/shard_map/all_to_all | solution.py:243
  93.1 1.8 shard_map.86
  94.8 1.1 convert_element_type.26
  95.9 6.9 %all-to-all-start.1 = ((f16[16,208,128]{2,1,0:T(8,128)(2,1)}), f16[16,208,128]{2,1,0:T(8,128)(2,1)}, u32[]{:S(2)}, u32[]{:S(2)}) async-start(f16[16,208,128]{2,1,0:T(8,128)(2,1)} %convert_element_type.26), calls=%async_computation.1 | async-start | bytes 1703936 | tf_op jit(solution)/shard_map/all_to_all | solution.py:253
  102.8 1.3 collective-permute-start
  104.1 0.7 collective-permute-start.1
  104.8 1.3 collective-permute-start.2
  106.1 0.1 pad.12.clone
  106.2 0.8 slice.76
  107.1 11.1 %collective-permute-done = bf16[16,32,128]{2,1,0:T(8,128)(2,1)S(1)} collective-permute-done((bf16[16,32,128]{2,1,0:T(8,128)(2,1)S(1)}, bf16[16,32,128]{2,1,0:T(8,128)(2,1)S(1)}, u32[]{:S(2)}, u32[]{:S(2)}) %collective-permute-start) | collective-permute-done | bytes 131104 | tf_op jit(solution)/shard_map/ppermute | solution.py:247
  118.2 0.0 collective-permute-done.1
  118.2 0.6 copy-done.8
  118.8 0.7 copy-done.9
  119.5 1.8 collective-permute-start.4
  121.3 0.8 convert_reduce_fusion
  122.1 0.8 fusion.5
  122.9 1.3 fusion
  124.2 0.1 maximum_maximum_fusion
  124.3 7.9 %collective-permute-start.3 = (f16[208,128]{1,0:T(8,128)(2,1)S(1)}, f16[208,128]{1,0:T(8,128)(2,1)S(1)}, u32[]{:S(2)}, u32[]{:S(2)}) collective-permute-start(f16[208,128]{1,0:T(8,128)(2,1)S(1)} %maximum_maximum_fusion), channel_id=1, source_target_pairs={{0,64},{16,80},{32,96},{48,112},{64,0},{80,16},{96,32},{112,48},{1... | collective-permute-start | bytes 159752 | tf_op jit(solution)/shard_map/ppermute | solution.py:269
  132.2 7.8 %collective-permute-start.5 = (bf16[16,32,128]{2,1,0:T(8,128)(2,1)}, bf16[16,32,128]{2,1,0:T(8,128)(2,1)S(1)}, u32[]{:S(2)}, u32[]{:S(2)}) collective-permute-start(bf16[16,32,128]{2,1,0:T(8,128)(2,1)} %copy-done.8), channel_id=1, source_target_pairs={{0,65},{1,64},{2,67},{3,66},{4,69},{5,68},{6,71},{7,70},{8,73},{9,... | collective-permute-start | bytes 393224 | tf_op jit(solution)/shard_map/ppermute | solution.py:258
  140.0 1.3 collective-permute-start.6
  141.3 1.3 collective-permute-start.7
  142.6 0.0 collective-permute-done.3
  142.7 1.3 collective-permute-start.8
  144.0 0.0 copy-start.3
  144.0 0.8 copy-done.3
  144.8 1.1 broadcast_in_dim.5
  145.9 13.1 %all-to-all-start.2 = ((f16[16,192,128]{2,1,0:T(8,128)(2,1)}), f16[16,192,128]{2,1,0:T(8,128)(2,1)}, u32[]{:S(2)}, u32[]{:S(2)}) async-start(f16[16,192,128]{2,1,0:T(8,128)(2,1)} %broadcast_in_dim.5), calls=%async_computation.2 | async-start | bytes 1572864 | tf_op jit(solution)/shard_map/all_to_all | solution.py:278
  159.0 0.0 collective-permute-done.5
  159.0 6.5 %collective-permute-done.6 = bf16[16,32,128]{2,1,0:T(8,128)(2,1)} collective-permute-done((bf16[16,32,128]{2,1,0:T(8,128)(2,1)}, bf16[16,32,128]{2,1,0:T(8,128)(2,1)}, u32[]{:S(2)}, u32[]{:S(2)}) %collective-permute-start.6) | collective-permute-done | bytes 131104 | tf_op jit(solution)/shard_map/ppermute | solution.py:258
  165.5 5.1 %collective-permute-done.7 = bf16[16,32,128]{2,1,0:T(8,128)(2,1)} collective-permute-done((bf16[16,32,128]{2,1,0:T(8,128)(2,1)}, bf16[16,32,128]{2,1,0:T(8,128)(2,1)}, u32[]{:S(2)}, u32[]{:S(2)}) %collective-permute-start.7) | collective-permute-done | bytes 131104 | tf_op jit(solution)/shard_map/ppermute | solution.py:258
  170.6 0.0 collective-permute-done.8
  170.6 1.9 %pad_maximum_fusion = bf16[16,128,128]{2,1,0:T(8,128)(2,1)} fusion(bf16[16,32,128]{2,1,0:T(8,128)(2,1)} %collective-permute-done.8, bf16[16,32,128]{2,1,0:T(8,128)(2,1)} %collective-permute-done.7, bf16[16,32,128]{2,1,0:T(8,128)(2,1)} %collective-permute-done.6, bf16[16,32,128]{2,1,0:T(8,128)(2,1)S(1)} %collective-permute-done.5), kind=kLoop, calls=%fused_computation.3 | loop fusion | flops 2097152 | bytes 1048576 | tf_op jit(solution)/shard_map/concatenate | solution.py:286
  172.5 2.1 %collective-permute-start.9 = (bf16[16,128,128]{2,1,0:T(8,128)(2,1)}, bf16[16,128,128]{2,1,0:T(8,128)(2,1)}, u32[]{:S(2)}, u32[]{:S(2)}) collective-permute-start(bf16[16,128,128]{2,1,0:T(8,128)(2,1)} %pad_maximum_fusion), channel_id=1, source_target_pairs={{0,1},{1,0},{2,3},{3,2},{4,5},{5,4},{6,7},{7,6},{8,9},{9,8},{10,11... | collective-permute-start | bytes 1572872 | tf_op jit(solution)/shard_map/ppermute | solution.py:287
  174.6 0.0 all-to-all-done.2
  174.6 1.2 convert_element_type.32.every
  175.9 0.0 copy-start.4
  175.9 8.7 %shard_map.87 = f32[1024,128]{1,0:T(8,128)} custom-call(f32[8,128]{1,0:T(8,128)S(1)} %concatenate.16.powers, f32[16,192,128]{2,1,0:T(8,128)S(1)} %convert_element_type.32.every, f32[256,512]{1,0:T(8,128)S(1)} %bitcast.33, f32[256,512]{1,0:T(8,128)S(1)} %bitcast.35, f32[512,256]{1,0:T(8,128)S(1)} %bitcast.37, bf16[16,400,128]{2,1,0:T(8,128)(2,1)S(1)} %all_to_all.15.first), custom_call_target="tpu_custom_call" | custom-call | flops 1048576 | bytes 4194304 | tf_op jit(solution)/shard_map/pallas_call | solution.py:184
  184.7 5.2 %shard_map.88 = f32[1024,128]{1,0:T(8,128)} custom-call(s32[1]{0:T(128)} %bitcast.place, bf16[16,400,128]{2,1,0:T(8,128)(2,1)S(1)} %all_to_all.15.first, bf16[16,128,128]{2,1,0:T(8,128)(2,1)S(1)} %copy-done.4, bf16[16,128,128]{2,1,0:T(8,128)(2,1)} %collective-permute-done.9.edge), custom_call_target="tpu_custom_call" | custom-call | flops 1048576 | bytes 4194304 | tf_op jit(solution)/shard_map/pallas_call | solution.py:184
  (31 shorter events, 0.5 us)
Async XLA Ops:
  0.6 1.5 copy-start.5
  0.6 1.8 copy-start.6
  2.5 0.7 copy-start.7
  3.2 89.9 %copy-start = (f32[1,256,512]{2,1,0:T(8,128)S(1)}, f32[1,256,512]{2,1,0:T(8,128)}, u32[]{:S(2)}) copy-start(f32[1,256,512]{2,1,0:T(8,128)} %param.11) | copy-start | bytes 1572868
  3.2 89.9 %copy-start.1 = (f32[1,256,512]{2,1,0:T(8,128)S(1)}, f32[1,256,512]{2,1,0:T(8,128)}, u32[]{:S(2)}) copy-start(f32[1,256,512]{2,1,0:T(8,128)} %param.12) | copy-start | bytes 1572868
  3.2 89.9 %copy-start.2 = (f32[1,512,256]{2,1,0:T(8,128)S(1)}, f32[1,512,256]{2,1,0:T(8,128)}, u32[]{:S(2)}) copy-start(f32[1,512,256]{2,1,0:T(8,128)} %param.13) | copy-start | bytes 1572868
  95.9 23.6 %all-to-all-start.1 = ((f16[16,208,128]{2,1,0:T(8,128)(2,1)}), f16[16,208,128]{2,1,0:T(8,128)(2,1)}, u32[]{:S(2)}, u32[]{:S(2)}) async-start(f16[16,208,128]{2,1,0:T(8,128)(2,1)} %convert_element_type.26), calls=%async_computation.1 | async-start | bytes 1703936 | tf_op jit(solution)/shard_map/all_to_all | solution.py:253
  102.8 15.3 %collective-permute-start = (bf16[16,32,128]{2,1,0:T(8,128)(2,1)S(1)}, bf16[16,32,128]{2,1,0:T(8,128)(2,1)S(1)}, u32[]{:S(2)}, u32[]{:S(2)}) collective-permute-start(bf16[16,32,128]{2,1,0:T(8,128)(2,1)S(1)} %get-tuple-element.27), channel_id=1, source_target_pairs={{48,0},{112,64},{176,128},{240,192},{304,256},{368,320},{432,384},... | collective-permute-start | bytes 393224 | tf_op jit(solution)/shard_map/ppermute | solution.py:247
  104.1 14.1 %collective-permute-start.1 = (bf16[16,32,128]{2,1,0:T(8,128)(2,1)S(1)}, bf16[16,32,128]{2,1,0:T(8,128)(2,1)S(1)}, u32[]{:S(2)}, u32[]{:S(2)}) collective-permute-start(bf16[16,32,128]{2,1,0:T(8,128)(2,1)S(1)} %get-tuple-element.26), channel_id=1, source_target_pairs={{48,16},{112,80},{176,144},{240,208},{304,272},{368,336},{432,400}... | collective-permute-start | bytes 393224 | tf_op jit(solution)/shard_map/ppermute | solution.py:247
  104.8 14.7 %collective-permute-start.2 = (bf16[16,32,128]{2,1,0:T(8,128)(2,1)S(1)}, bf16[16,32,128]{2,1,0:T(8,128)(2,1)}, u32[]{:S(2)}, u32[]{:S(2)}) collective-permute-start(bf16[16,32,128]{2,1,0:T(8,128)(2,1)S(1)} %get-tuple-element.25), channel_id=1, source_target_pairs={{48,32},{112,96},{176,160},{240,224},{304,288},{368,352},{432,416}... | collective-permute-start | bytes 393224 | tf_op jit(solution)/shard_map/ppermute | solution.py:247
  118.2 0.6 copy-start.8
  118.8 0.7 copy-start.9
  119.5 24.5 %collective-permute-start.4 = (bf16[16,128,128]{2,1,0:T(8,128)(2,1)}, bf16[16,128,128]{2,1,0:T(8,128)(2,1)S(1)}, u32[]{:S(2)}, u32[]{:S(2)}) collective-permute-start(bf16[16,128,128]{2,1,0:T(8,128)(2,1)} %slice.76), channel_id=1, source_target_pairs={{0,16},{16,32},{32,48},{64,80},{80,96},{96,112},{128,144},{144,160... | collective-permute-start | bytes 1572872 | tf_op jit(solution)/shard_map/ppermute | solution.py:260
  124.3 18.3 %collective-permute-start.3 = (f16[208,128]{1,0:T(8,128)(2,1)S(1)}, f16[208,128]{1,0:T(8,128)(2,1)S(1)}, u32[]{:S(2)}, u32[]{:S(2)}) collective-permute-start(f16[208,128]{1,0:T(8,128)(2,1)S(1)} %maximum_maximum_fusion), channel_id=1, source_target_pairs={{0,64},{16,80},{32,96},{48,112},{64,0},{80,16},{96,32},{112,48},{1... | collective-permute-start | bytes 159752 | tf_op jit(solution)/shard_map/ppermute | solution.py:269
  132.2 26.7 %collective-permute-start.5 = (bf16[16,32,128]{2,1,0:T(8,128)(2,1)}, bf16[16,32,128]{2,1,0:T(8,128)(2,1)S(1)}, u32[]{:S(2)}, u32[]{:S(2)}) collective-permute-start(bf16[16,32,128]{2,1,0:T(8,128)(2,1)} %copy-done.8), channel_id=1, source_target_pairs={{0,65},{1,64},{2,67},{3,66},{4,69},{5,68},{6,71},{7,70},{8,73},{9,... | collective-permute-start | bytes 393224 | tf_op jit(solution)/shard_map/ppermute | solution.py:258
  140.0 25.4 %collective-permute-start.6 = (bf16[16,32,128]{2,1,0:T(8,128)(2,1)}, bf16[16,32,128]{2,1,0:T(8,128)(2,1)}, u32[]{:S(2)}, u32[]{:S(2)}) collective-permute-start(bf16[16,32,128]{2,1,0:T(8,128)(2,1)} %copy-done.9), channel_id=1, source_target_pairs={{16,65},{17,64},{18,67},{19,66},{20,69},{21,68},{22,71},{23,70},{2... | collective-permute-start | bytes 393224 | tf_op jit(solution)/shard_map/ppermute | solution.py:258
  141.3 29.3 %collective-permute-start.7 = (bf16[16,32,128]{2,1,0:T(8,128)(2,1)}, bf16[16,32,128]{2,1,0:T(8,128)(2,1)}, u32[]{:S(2)}, u32[]{:S(2)}) collective-permute-start(bf16[16,32,128]{2,1,0:T(8,128)(2,1)} %collective-permute-done.2), channel_id=1, source_target_pairs={{32,65},{33,64},{34,67},{35,66},{36,69},{37,68},{38,71},{39,70},{4... | collective-permute-start | bytes 393224 | tf_op jit(solution)/shard_map/ppermute | solution.py:258
  142.7 28.0 %collective-permute-start.8 = (bf16[16,32,128]{2,1,0:T(8,128)(2,1)S(1)}, bf16[16,32,128]{2,1,0:T(8,128)(2,1)}, u32[]{:S(2)}, u32[]{:S(2)}) collective-permute-start(bf16[16,32,128]{2,1,0:T(8,128)(2,1)S(1)} %get-tuple-element.18), channel_id=1, source_target_pairs={{48,65},{49,64},{50,67},{51,66},{52,69},{53,68},{54,71},{55,70},{5... | collective-permute-start | bytes 393224 | tf_op jit(solution)/shard_map/ppermute | solution.py:258
  144.0 0.8 copy-start.3
  145.9 28.8 %all-to-all-start.2 = ((f16[16,192,128]{2,1,0:T(8,128)(2,1)}), f16[16,192,128]{2,1,0:T(8,128)(2,1)}, u32[]{:S(2)}, u32[]{:S(2)}) async-start(f16[16,192,128]{2,1,0:T(8,128)(2,1)} %broadcast_in_dim.5), calls=%async_computation.2 | async-start | bytes 1572864 | tf_op jit(solution)/shard_map/all_to_all | solution.py:278
  172.5 12.1 %collective-permute-start.9 = (bf16[16,128,128]{2,1,0:T(8,128)(2,1)}, bf16[16,128,128]{2,1,0:T(8,128)(2,1)}, u32[]{:S(2)}, u32[]{:S(2)}) collective-permute-start(bf16[16,128,128]{2,1,0:T(8,128)(2,1)} %pad_maximum_fusion), channel_id=1, source_target_pairs={{0,1},{1,0},{2,3},{3,2},{4,5},{5,4},{6,7},{7,6},{8,9},{9,8},{10,11... | collective-permute-start | bytes 1572872 | tf_op jit(solution)/shard_map/ppermute | solution.py:287
  175.9 8.8 %copy-start.4 = (bf16[16,128,128]{2,1,0:T(8,128)(2,1)S(1)}, bf16[16,128,128]{2,1,0:T(8,128)(2,1)}, u32[]{:S(2)}) copy-start(bf16[16,128,128]{2,1,0:T(8,128)(2,1)} %copy-done.3) | copy-start | bytes 1572868

commit v9 on v8

--- a/solution.py
+++ b/solution.py
@@ -20,7 +20,6 @@
 
 XS, HALVES, YS = 4, 2, 4
 PLANE = XS * YS
-GROUP = 16
 VMEM_LIMIT = 48 * 1024 * 1024
 
 
@@ -89,7 +88,7 @@
     out[:, 3 * FHID // LANES * rows :, :] = jnp.broadcast_to(tag[None], (PLANE, 16, LANES))
 
 
-def attention_kernel(place, first, side, edge, out, earlier):
+def attention_kernel(place, first, side, edge0, edge1, edge2, edge3, out, earlier):
     span = first.shape[0] * TOK
     scale = 1.0 / math.sqrt(LANES)
     tile = 128
@@ -103,7 +102,8 @@
 
     @pl.when(on_edge)
     def _():
-        earlier[...] = edge[...]
+        for i, edge in enumerate((edge0, edge1, edge2, edge3)):
+            earlier[:, i * TOK : (i + 1) * TOK, :] = edge[...]
 
     @pl.when(jnp.logical_not(on_edge))
     def _():
@@ -212,18 +212,10 @@
 ]
 ENDS = [(x, half, x + half, 1 - half) for x in range(XS) for half in range(HALVES)][:-1]
 
-
-def other_core(pairs):
-    return [
-        (a * GROUP + i, b * GROUP + (i ^ 1)) for a, b in pairs for i in range(GROUP)
-    ]
-
-
 EDGES = [
-    other_core([(wide_index(x, half, y), wide_index(*after, 0)) for x, half, *after in ENDS])
+    [(wide_index(x, half, y), wide_index(*after, 0)) for x, half, *after in ENDS]
     for y in range(YS)
 ]
-CORES = other_core([(wide_index(*line, 0), wide_index(*line, 0)) for line in LINES])
 FLOPS = 1 << 20
 
 
@@ -254,9 +246,6 @@
         pieces.astype(jnp.float16), "wide", 0, 0, tiled=True, axis_index_groups=PLANES
     )
     got, tail, quarters = lax.optimization_barrier((got, tail, quarters))
-    edges = [
-        lax.ppermute(part, ("wide", "narrow"), pairs) for part, pairs in zip(quarters, EDGES)
-    ]
     side = lax.ppermute(tail, "wide", NEXT)
     powers = got[:, count : count + 3].astype(jnp.float32)
     top = jnp.max(powers, axis=0)
@@ -267,7 +256,8 @@
     )
     sent = sent.astype(jnp.float16)
     other = lax.ppermute(sent, "wide", SWAP)
-    other, side = lax.optimization_barrier((other, side))
+    other, side, quarters = lax.optimization_barrier((other, side, quarters))
+    edges = [lax.ppermute(part, "wide", pairs) for part, pairs in zip(quarters, EDGES)]
     other_top = other[count : count + 3].astype(jnp.float32)
     both = jnp.maximum(top, other_top)
     whole = half * (jnp.exp2(top - both) * 0.5)[:, None]
@@ -283,8 +273,6 @@
         tiled=True,
         axis_index_groups=PLANES,
     )
-    edge = jnp.concatenate(edges, axis=1)
-    edge = lax.ppermute(edge, ("wide", "narrow"), CORES)
     factors = jnp.concatenate([jnp.exp2(both - 8.0), jnp.zeros((5, LANES), jnp.float32)], axis=0)
     fast_out = call(
         apply_kernel,
@@ -293,11 +281,11 @@
         FLOPS,
     )
     place = lax.axis_index("wide").reshape(1)
-    edge, fast_out = lax.optimization_barrier((edge, fast_out))
+    edges, fast_out = lax.optimization_barrier((edges, fast_out))
     window_out = call(
         attention_kernel,
         (span * own, LANES),
-        (place, first, side, edge),
+        (place, first, side, *edges),
         FLOPS,
         1,
         [pltpu.VMEM((PLANE, 4 * TOK, LANES), jnp.bfloat16)],

time: 192 us -> 190 us (0.990)
  waiting for transfers between devices: 22.8 us -> 28.4 us
  starting transfers between devices: 46.8 us -> 41.7 us
    ppermute x3 -> x7, starting transfers between devices: 3.29 us -> 17.7 us  [per_device(): lax.ppermute(part, 'wide', pairs)]
    ppermute x5 -> x0, starting transfers between devices: 13.8 us -> none  [the longest x4 11.7 us: per_device(): lax.ppermute(part, ('wide', 'narrow'), pairs)]
    ppermute x5 -> x0, waiting for transfers between devices: 11.6 us -> none  [the longest x4 11.6 us: per_device(): lax.ppermute(part, ('wide', 'narrow'), pairs)]
    ppermute x3 -> x7, waiting for transfers between devices: 11.1 us -> 22.7 us  [per_device(): lax.ppermute(part, 'wide', pairs)]
    all_to_all x1, starting transfers between devices: 13.1 us -> 6.8 us  [per_device(): lax.all_to_all(jnp.broadcast_to(whole[None], (PLANE, count, LANES)), 'wid...]
    ppermute x1, waiting for transfers between devices: 0.01 us -> 5.69 us  [per_device(): other = lax.ppermute(sent, 'wide', SWAP)]
    unnamed x31 -> x29, local copies, waits for them, and re-layouts: 4.12 us -> 3.49 us
  transfers between devices with their start and end apart: 12 -> 11, of which waited for: 3 -> 5; matrix products, arithmetic and copies ran while one was open for 4% -> 3% of each run, Pallas kernels for 5% -> 5%
where the time goes in v9:
time: 190 us; the launch traced here: 188 us
  blocking collectives  89.8 us (47%)
  starting transfers between devices  41.7 us (22%)
  waiting for transfers between devices  28.4 us (15%)
  Pallas kernels  15.6 us (8%)
  local copies, waits for them, and re-layouts  6.59 us (3%)
  other arithmetic  5.34 us (3%)
    all_to_all x1, blocking collectives, per_device(): first = lax.all_to_all(first, 'narrow', 0, 0, tiled=True)  89.8 us
    ppermute x7, waiting for transfers between devices, per_device(): lax.ppermute(part, 'wide', pairs)  22.7 us
    ppermute x7, starting transfers between devices, per_device(): lax.ppermute(part, 'wide', pairs)  17.7 us
    pallas_call x3, Pallas kernels, call(): pl.pallas_call(kernel, out_shape=jax.ShapeDtypeStruct(shape, jnp.float32)...  15.6 us
    ppermute x1, starting transfers between devices, per_device(): other = lax.ppermute(sent, 'wide', SWAP)  7.93 us
    all_to_all x1, starting transfers between devices, per_device(): lax.all_to_all(pieces.astype(jnp.float16), 'wide', 0, 0, tiled=True, axis...  6.88 us
    all_to_all x1, starting transfers between devices, per_device(): lax.all_to_all(jnp.broadcast_to(whole[None], (PLANE, count, LANES)), 'wid...  6.8 us
    ppermute x1, waiting for transfers between devices, per_device(): other = lax.ppermute(sent, 'wide', SWAP)  5.69 us
  transfers between devices with their start and end apart: 11, of which 5 were waited for; matrix products, arithmetic and copies ran while one was open for 3% of the time, Pallas kernels for 5%

profile of v9, /device:TPU:7, one launch (start us, length us, event | category | flops | bytes accessed | tf_op | source)
XLA Modules:
  0.0 188.4 jit_solution(17717452026201243106)
XLA Ops:
  0.6 1.4 copy.16
  2.1 0.3 copy.9
  2.5 0.0 copy-start.7
  2.5 0.1 copy.10
  2.8 0.1 slice_dynamic-update-slice_fusion
  3.0 0.2 copy-done.7
  3.2 0.0 copy-start
  3.2 0.0 copy-start.1
  3.2 0.0 copy-start.2
  3.2 89.8 %all_to_all.15.first = bf16[16,400,128]{2,1,0:T(8,128)(2,1)S(1)} all-to-all(bf16[16,400,128]{2,1,0:T(8,128)(2,1)S(1)} %pad_dynamic-update-slice_fusion), channel_id=1, replica_groups=mesh['wide'=32,'narrow'=16] {'narrow'}, dimensions={0} | all-to-all | bytes 3276800 | tf_op jit(solution)/shard_map/all_to_all | solution.py:235
  93.1 1.8 shard_map.86
  94.8 1.1 convert_element_type.26
  95.9 6.9 %all-to-all-start.1 = ((f16[16,208,128]{2,1,0:T(8,128)(2,1)}), f16[16,208,128]{2,1,0:T(8,128)(2,1)}, u32[]{:S(2)}, u32[]{:S(2)}) async-start(f16[16,208,128]{2,1,0:T(8,128)(2,1)} %convert_element_type.26), calls=%async_computation.1 | async-start | bytes 1703936 | tf_op jit(solution)/shard_map/all_to_all | solution.py:245
  102.8 0.7 fusion.16
  103.5 1.3 collective-permute-start
  104.8 0.7 collective-permute-start.1
  105.4 1.3 collective-permute-start.2
  106.8 0.1 pad.8.clone
  106.9 0.8 slice.76
  107.7 10.6 %collective-permute-done = bf16[16,32,128]{2,1,0:T(8,128)(2,1)} collective-permute-done((bf16[16,32,128]{2,1,0:T(8,128)(2,1)S(1)}, bf16[16,32,128]{2,1,0:T(8,128)(2,1)}, u32[]{:S(2)}, u32[]{:S(2)}) %collective-permute-start) | collective-permute-done | bytes 131104 | tf_op jit(solution)/shard_map/ppermute | solution.py:239
  118.3 0.0 collective-permute-done.1
  118.3 0.7 copy-done.8
  119.0 0.0 collective-permute-done.2
  119.0 0.0 all-to-all-done.1
  119.0 2.3 %collective-permute-start.4 = (bf16[16,128,128]{2,1,0:T(8,128)(2,1)}, bf16[16,128,128]{2,1,0:T(8,128)(2,1)S(1)}, u32[]{:S(2)}, u32[]{:S(2)}) collective-permute-start(bf16[16,128,128]{2,1,0:T(8,128)(2,1)} %slice.76), channel_id=1, source_target_pairs={{0,16},{16,32},{32,48},{64,80},{80,96},{96,112},{128,144},{144,160... | collective-permute-start | bytes 1572872 | tf_op jit(solution)/shard_map/ppermute | solution.py:249
  121.3 0.8 convert_reduce_fusion
  122.1 0.8 fusion.5
  122.9 1.3 fusion
  124.2 0.1 maximum_maximum_fusion
  124.3 7.9 %collective-permute-start.3 = (f16[208,128]{1,0:T(8,128)(2,1)S(1)}, f16[208,128]{1,0:T(8,128)(2,1)S(1)}, u32[]{:S(2)}, u32[]{:S(2)}) collective-permute-start(f16[208,128]{1,0:T(8,128)(2,1)S(1)} %maximum_maximum_fusion), channel_id=1, source_target_pairs={{0,64},{16,80},{32,96},{48,112},{64,0},{80,16},{96,32},{112,48},{1... | collective-permute-start | bytes 159752 | tf_op jit(solution)/shard_map/ppermute | solution.py:258
  132.2 5.7 %collective-permute-done.3 = f16[208,128]{1,0:T(8,128)(2,1)S(1)} collective-permute-done((f16[208,128]{1,0:T(8,128)(2,1)S(1)}, f16[208,128]{1,0:T(8,128)(2,1)S(1)}, u32[]{:S(2)}, u32[]{:S(2)}) %collective-permute-start.3) | collective-permute-done | bytes 53280 | tf_op jit(solution)/shard_map/ppermute | solution.py:258
  137.9 0.0 collective-permute-done.4.side
  137.9 0.8 copy-done.3
  138.8 1.1 broadcast_in_dim.5
  139.8 6.8 %all-to-all-start.2 = ((f16[16,192,128]{2,1,0:T(8,128)(2,1)}), f16[16,192,128]{2,1,0:T(8,128)(2,1)}, u32[]{:S(2)}, u32[]{:S(2)}) async-start(f16[16,192,128]{2,1,0:T(8,128)(2,1)} %broadcast_in_dim.5), calls=%async_computation.2 | async-start | bytes 1572864 | tf_op jit(solution)/shard_map/all_to_all | solution.py:268
  146.6 10.4 %collective-permute-start.5 = (bf16[16,32,128]{2,1,0:T(8,128)(2,1)}, bf16[16,32,128]{2,1,0:T(8,128)(2,1)S(1)}, u32[]{:S(2)}, u32[]{:S(2)}) collective-permute-start(bf16[16,32,128]{2,1,0:T(8,128)(2,1)} %collective-permute-done), channel_id=1, source_target_pairs={{0,64},{64,128},{128,192},{192,256},{256,320},{320,384},{384,448},... | collective-permute-start | bytes 393224 | tf_op jit(solution)/shard_map/ppermute | solution.py:260
  157.0 1.3 collective-permute-start.6
  158.3 1.3 collective-permute-start.7
  159.6 1.5 collective-permute-start.8
  161.1 0.0 all-to-all-done.2
  161.1 1.2 convert_element_type.32.every
  162.4 0.0 copy-start.4
  162.4 8.7 %shard_map.87 = f32[1024,128]{1,0:T(8,128)} custom-call(f32[8,128]{1,0:T(8,128)S(1)} %concatenate.12.powers, f32[16,192,128]{2,1,0:T(8,128)S(1)} %convert_element_type.32.every, f32[256,512]{1,0:T(8,128)S(1)} %bitcast.33, f32[256,512]{1,0:T(8,128)S(1)} %bitcast.35, f32[512,256]{1,0:T(8,128)S(1)} %bitcast.37, bf16[16,400,128]{2,1,0:T(8,128)(2,1)S(1)} %all_to_all.15.first), custom_call_target="tpu_custom_call" | custom-call | flops 1048576 | bytes 4194304 | tf_op jit(solution)/shard_map/pallas_call | solution.py:184
  171.1 0.0 collective-permute-done.5.edge0
  171.1 7.7 %collective-permute-done.6.edge1 = bf16[16,32,128]{2,1,0:T(8,128)(2,1)S(1)} collective-permute-done((bf16[16,32,128]{2,1,0:T(8,128)(2,1)}, bf16[16,32,128]{2,1,0:T(8,128)(2,1)S(1)}, u32[]{:S(2)}, u32[]{:S(2)}) %collective-permute-start.6) | collective-permute-done | bytes 131104 | tf_op jit(solution)/shard_map/ppermute | solution.py:260
  178.8 2.8 %collective-permute-done.7.edge2 = bf16[16,32,128]{2,1,0:T(8,128)(2,1)} collective-permute-done((bf16[16,32,128]{2,1,0:T(8,128)(2,1)}, bf16[16,32,128]{2,1,0:T(8,128)(2,1)}, u32[]{:S(2)}, u32[]{:S(2)}) %collective-permute-start.7) | collective-permute-done | bytes 131104 | tf_op jit(solution)/shard_map/ppermute | solution.py:260
  181.6 1.7 collective-permute-done.8.edge3
  183.3 5.1 %shard_map.88 = f32[1024,128]{1,0:T(8,128)} custom-call(s32[1]{0:T(128)} %bitcast.place, bf16[16,400,128]{2,1,0:T(8,128)(2,1)S(1)} %all_to_all.15.first, bf16[16,128,128]{2,1,0:T(8,128)(2,1)S(1)} %copy-done.4, bf16[16,32,128]{2,1,0:T(8,128)(2,1)S(1)} %collective-permute-done.5.edge0, bf16[16,32,128]{2,1,0:T(8,128)(2,1)S(1)} %collective-permute-done.6.edge1, ...), custom_call_target="tpu_custom_call" | custom-call | flops 1048576 | bytes 4194304 | tf_op jit(solution)/shard_map/pallas_call | solution.py:184
  (26 shorter events, 0.4 us)
Async XLA Ops:
  0.6 1.5 copy-start.5
  0.6 1.8 copy-start.6
  2.5 0.7 copy-start.7
  3.2 89.9 %copy-start = (f32[1,256,512]{2,1,0:T(8,128)S(1)}, f32[1,256,512]{2,1,0:T(8,128)}, u32[]{:S(2)}) copy-start(f32[1,256,512]{2,1,0:T(8,128)} %param.11) | copy-start | bytes 1572868
  3.2 89.9 %copy-start.1 = (f32[1,256,512]{2,1,0:T(8,128)S(1)}, f32[1,256,512]{2,1,0:T(8,128)}, u32[]{:S(2)}) copy-start(f32[1,256,512]{2,1,0:T(8,128)} %param.12) | copy-start | bytes 1572868
  3.2 89.9 %copy-start.2 = (f32[1,512,256]{2,1,0:T(8,128)S(1)}, f32[1,512,256]{2,1,0:T(8,128)}, u32[]{:S(2)}) copy-start(f32[1,512,256]{2,1,0:T(8,128)} %param.13) | copy-start | bytes 1572868
  95.9 23.0 %all-to-all-start.1 = ((f16[16,208,128]{2,1,0:T(8,128)(2,1)}), f16[16,208,128]{2,1,0:T(8,128)(2,1)}, u32[]{:S(2)}, u32[]{:S(2)}) async-start(f16[16,208,128]{2,1,0:T(8,128)(2,1)} %convert_element_type.26), calls=%async_computation.1 | async-start | bytes 1703936 | tf_op jit(solution)/shard_map/all_to_all | solution.py:245
  103.5 14.8 %collective-permute-start = (bf16[16,32,128]{2,1,0:T(8,128)(2,1)S(1)}, bf16[16,32,128]{2,1,0:T(8,128)(2,1)}, u32[]{:S(2)}, u32[]{:S(2)}) collective-permute-start(bf16[16,32,128]{2,1,0:T(8,128)(2,1)S(1)} %get-tuple-element.41), channel_id=1, source_target_pairs={{48,0},{112,64},{176,128},{240,192},{304,256},{368,320},{432,384},... | collective-permute-start | bytes 393224 | tf_op jit(solution)/shard_map/ppermute | solution.py:239
  104.8 13.5 %collective-permute-start.1 = (bf16[16,32,128]{2,1,0:T(8,128)(2,1)S(1)}, bf16[16,32,128]{2,1,0:T(8,128)(2,1)S(1)}, u32[]{:S(2)}, u32[]{:S(2)}) collective-permute-start(bf16[16,32,128]{2,1,0:T(8,128)(2,1)S(1)} %get-tuple-element.40), channel_id=1, source_target_pairs={{48,16},{112,80},{176,144},{240,208},{304,272},{368,336},{432,400}... | collective-permute-start | bytes 393224 | tf_op jit(solution)/shard_map/ppermute | solution.py:239
  105.4 13.5 %collective-permute-start.2 = (bf16[16,32,128]{2,1,0:T(8,128)(2,1)S(1)}, bf16[16,32,128]{2,1,0:T(8,128)(2,1)}, u32[]{:S(2)}, u32[]{:S(2)}) collective-permute-start(bf16[16,32,128]{2,1,0:T(8,128)(2,1)S(1)} %get-tuple-element.39), channel_id=1, source_target_pairs={{48,32},{112,96},{176,160},{240,224},{304,288},{368,352},{432,416}... | collective-permute-start | bytes 393224 | tf_op jit(solution)/shard_map/ppermute | solution.py:239
  118.3 0.7 copy-start.8
  119.0 19.0 %collective-permute-start.4 = (bf16[16,128,128]{2,1,0:T(8,128)(2,1)}, bf16[16,128,128]{2,1,0:T(8,128)(2,1)S(1)}, u32[]{:S(2)}, u32[]{:S(2)}) collective-permute-start(bf16[16,128,128]{2,1,0:T(8,128)(2,1)} %slice.76), channel_id=1, source_target_pairs={{0,16},{16,32},{32,48},{64,80},{80,96},{96,112},{128,144},{144,160... | collective-permute-start | bytes 1572872 | tf_op jit(solution)/shard_map/ppermute | solution.py:249
  124.3 13.6 %collective-permute-start.3 = (f16[208,128]{1,0:T(8,128)(2,1)S(1)}, f16[208,128]{1,0:T(8,128)(2,1)S(1)}, u32[]{:S(2)}, u32[]{:S(2)}) collective-permute-start(f16[208,128]{1,0:T(8,128)(2,1)S(1)} %maximum_maximum_fusion), channel_id=1, source_target_pairs={{0,64},{16,80},{32,96},{48,112},{64,0},{80,16},{96,32},{112,48},{1... | collective-permute-start | bytes 159752 | tf_op jit(solution)/shard_map/ppermute | solution.py:258
  137.9 0.8 copy-start.3
  139.8 21.3 %all-to-all-start.2 = ((f16[16,192,128]{2,1,0:T(8,128)(2,1)}), f16[16,192,128]{2,1,0:T(8,128)(2,1)}, u32[]{:S(2)}, u32[]{:S(2)}) async-start(f16[16,192,128]{2,1,0:T(8,128)(2,1)} %broadcast_in_dim.5), calls=%async_computation.2 | async-start | bytes 1572864 | tf_op jit(solution)/shard_map/all_to_all | solution.py:268
  146.6 24.5 %collective-permute-start.5 = (bf16[16,32,128]{2,1,0:T(8,128)(2,1)}, bf16[16,32,128]{2,1,0:T(8,128)(2,1)S(1)}, u32[]{:S(2)}, u32[]{:S(2)}) collective-permute-start(bf16[16,32,128]{2,1,0:T(8,128)(2,1)} %collective-permute-done), channel_id=1, source_target_pairs={{0,64},{64,128},{128,192},{192,256},{256,320},{320,384},{384,448},... | collective-permute-start | bytes 393224 | tf_op jit(solution)/shard_map/ppermute | solution.py:260
  157.0 21.8 %collective-permute-start.6 = (bf16[16,32,128]{2,1,0:T(8,128)(2,1)}, bf16[16,32,128]{2,1,0:T(8,128)(2,1)S(1)}, u32[]{:S(2)}, u32[]{:S(2)}) collective-permute-start(bf16[16,32,128]{2,1,0:T(8,128)(2,1)} %copy-done.8), channel_id=1, source_target_pairs={{16,64},{80,128},{144,192},{208,256},{272,320},{336,384},{400,448}... | collective-permute-start | bytes 393224 | tf_op jit(solution)/shard_map/ppermute | solution.py:260
  158.3 23.3 %collective-permute-start.7 = (bf16[16,32,128]{2,1,0:T(8,128)(2,1)}, bf16[16,32,128]{2,1,0:T(8,128)(2,1)}, u32[]{:S(2)}, u32[]{:S(2)}) collective-permute-start(bf16[16,32,128]{2,1,0:T(8,128)(2,1)} %collective-permute-done.2), channel_id=1, source_target_pairs={{32,64},{96,128},{160,192},{224,256},{288,320},{352,384},{416,448}... | collective-permute-start | bytes 393224 | tf_op jit(solution)/shard_map/ppermute | solution.py:260
  159.6 23.7 %collective-permute-start.8 = (bf16[16,32,128]{2,1,0:T(8,128)(2,1)}, bf16[16,32,128]{2,1,0:T(8,128)(2,1)}, u32[]{:S(2)}, u32[]{:S(2)}) collective-permute-start(bf16[16,32,128]{2,1,0:T(8,128)(2,1)} %get-tuple-element.29), channel_id=1, source_target_pairs={{48,64},{112,128},{176,192},{240,256},{304,320},{368,384},{432,448... | collective-permute-start | bytes 393224 | tf_op jit(solution)/shard_map/ppermute | solution.py:260
  162.4 20.9 %copy-start.4 = (bf16[16,128,128]{2,1,0:T(8,128)(2,1)S(1)}, bf16[16,128,128]{2,1,0:T(8,128)(2,1)}, u32[]{:S(2)}) copy-start(bf16[16,128,128]{2,1,0:T(8,128)(2,1)} %copy-done.3) | copy-start | bytes 1572868

commit v10 on v6

--- a/solution.py
+++ b/solution.py
@@ -20,6 +20,7 @@
 
 XS, HALVES, YS = 4, 2, 4
 PLANE = XS * YS
+CUT = 80
 VMEM_LIMIT = 48 * 1024 * 1024
 
 
@@ -102,8 +103,8 @@
 
     @pl.when(edge)
     def _():
-        earlier[:, : 2 * TOK, :] = edge_low[...]
-        earlier[:, 2 * TOK :, :] = edge_high[...]
+        earlier[:, :CUT, :] = edge_low[...]
+        earlier[:, CUT:, :] = edge_high[...]
 
     @pl.when(jnp.logical_not(edge))
     def _():
@@ -230,7 +231,7 @@
     )
     first = lax.all_to_all(first, "narrow", 0, 0, tiled=True)
     tail = first[:, : 4 * rows]
-    edge_high = lax.ppermute(first[:, 2 * rows : 4 * rows], "wide", EDGE_HIGH)
+    edge_high = lax.ppermute(first[:, CUT : 4 * rows], "wide", EDGE_HIGH)
 
     weights = (gate_fast[0], up_fast[0], down_fast[0])
     count = 3 * FHID // LANES * FD // PLANE
@@ -249,7 +250,7 @@
     )
     sent = sent.astype(jnp.float16)
     other = lax.ppermute(sent, "wide", SWAP)
-    other, low_part, edge_high = lax.optimization_barrier((other, side[:, : 2 * rows], edge_high))
+    other, low_part, edge_high = lax.optimization_barrier((other, side[:, :CUT], edge_high))
     edge_low = lax.ppermute(low_part, "wide", EDGE_LOW)
     other_top = other[count : count + 3].astype(jnp.float32)
     both = jnp.maximum(top, other_top)

time: 189 us -> 190 us (level)
  the two profiles are of different devices: /device:TPU:7 before, /device:TPU:71 now
where the time goes in v10:
time: 190 us; the launch traced here: 189 us
  blocking collectives  87.2 us (46%)
  waiting for transfers between devices  38.8 us (20%)
  starting transfers between devices  35.5 us (19%)
  Pallas kernels  14.6 us (8%)
  local copies, waits for them, and re-layouts  6.73 us (4%)
  other arithmetic  5.31 us (3%)
    all_to_all x1, blocking collectives, per_device(): first = lax.all_to_all(first, 'narrow', 0, 0, tiled=True)  87.2 us
    ppermute x1, waiting for transfers between devices, per_device(): edge_low = lax.ppermute(low_part, 'wide', EDGE_LOW)  17.8 us
    pallas_call x3, Pallas kernels, call(): pl.pallas_call(kernel, out_shape=jax.ShapeDtypeStruct(shape, jnp.float32)...  14.6 us
    all_to_all x1, starting transfers between devices, per_device(): lax.all_to_all(jnp.broadcast_to(whole[None], (PLANE, count, LANES)), 'wid...  11.1 us
    all_to_all x1, waiting for transfers between devices, per_device(): lax.all_to_all(pieces.astype(jnp.float16), 'wide', 0, 0, tiled=True, axis...  9.3 us
    ppermute x1, starting transfers between devices, per_device(): other = lax.ppermute(sent, 'wide', SWAP)  7.95 us
    all_to_all x1, starting transfers between devices, per_device(): lax.all_to_all(pieces.astype(jnp.float16), 'wide', 0, 0, tiled=True, axis...  6.86 us
    ppermute x1, waiting for transfers between devices, per_device(): side = lax.ppermute(tail, 'wide', AROUND)  6.31 us
  transfers between devices with their start and end apart: 6, of which 4 were waited for; matrix products, arithmetic and copies ran while one was open for 3% of the time, Pallas kernels for 5%

profile of v10, /device:TPU:71, one launch (start us, length us, event | category | flops | bytes accessed | tf_op | source)
XLA Modules:
  0.0 189.1 jit_solution(2632511606223473883)
XLA Ops:
  0.6 0.0 copy-start.7
  0.6 0.0 copy-start.8
  0.6 1.4 copy.16
  2.1 0.0 copy-done.7
  2.1 0.3 copy.9
  2.5 0.0 copy-start.9
  2.5 0.0 copy-done.8
  2.5 0.1 copy.10
  2.8 0.1 slice_dynamic-update-slice_fusion
  3.0 0.2 copy-done.9
  3.2 0.0 copy-start
  3.2 0.0 copy-start.1
  3.2 0.0 copy-start.2
  3.2 87.2 %all_to_all.15.first = bf16[16,400,128]{2,1,0:T(8,128)(2,1)S(1)} all-to-all(bf16[16,400,128]{2,1,0:T(8,128)(2,1)S(1)} %pad_dynamic-update-slice_fusion), channel_id=1, replica_groups=mesh['wide'=32,'narrow'=16] {'narrow'}, dimensions={0} | all-to-all | bytes 3276800 | tf_op jit(solution)/shard_map/all_to_all | solution.py:232
  90.5 0.0 copy-done
  90.5 0.0 copy-done.1
  90.5 0.0 copy-done.2
  90.5 1.8 shard_map.86
  92.2 1.0 convert_element_type.26
  93.3 6.9 %all-to-all-start.1 = ((f16[16,208,128]{2,1,0:T(8,128)(2,1)}), f16[16,208,128]{2,1,0:T(8,128)(2,1)}, u32[]{:S(2)}, u32[]{:S(2)}) async-start(f16[16,208,128]{2,1,0:T(8,128)(2,1)} %convert_element_type.26), calls=%async_computation.1 | async-start | bytes 1703936 | tf_op jit(solution)/shard_map/all_to_all | solution.py:239
  100.1 0.1 pad.8.clone
  100.2 0.7 slice.70
  100.9 1.3 collective-permute-start.2
  102.2 0.8 slice.68
  103.1 9.3 %all-to-all-done.1 = f16[16,208,128]{2,1,0:T(8,128)(2,1)} async-done(((f16[16,208,128]{2,1,0:T(8,128)(2,1)}), f16[16,208,128]{2,1,0:T(8,128)(2,1)}, u32[]{:S(2)}, u32[]{:S(2)}) %all-to-all-start.1) | async-done | bytes 852000 | tf_op jit(solution)/shard_map/all_to_all | solution.py:239
  112.4 2.2 %collective-permute-start = (bf16[16,128,128]{2,1,0:T(8,128)(2,1)}, bf16[16,128,128]{2,1,0:T(8,128)(2,1)S(1)}, u32[]{:S(2)}, u32[]{:S(2)}) collective-permute-start(bf16[16,128,128]{2,1,0:T(8,128)(2,1)} %slice.68), channel_id=1, source_target_pairs={{0,16},{16,32},{32,48},{48,0},{64,80},{80,96},{96,112},{112,64},{1... | collective-permute-start | bytes 1572872 | tf_op jit(solution)/shard_map/ppermute | solution.py:243
  114.6 0.8 convert_reduce_fusion
  115.4 0.8 fusion.5
  116.1 1.3 fusion
  117.5 0.1 maximum_maximum_fusion
  117.6 8.0 %collective-permute-start.1 = (f16[208,128]{1,0:T(8,128)(2,1)S(1)}, f16[208,128]{1,0:T(8,128)(2,1)S(1)}, u32[]{:S(2)}, u32[]{:S(2)}) collective-permute-start(f16[208,128]{1,0:T(8,128)(2,1)S(1)} %maximum_maximum_fusion), channel_id=1, source_target_pairs={{0,64},{16,80},{32,96},{48,112},{64,0},{80,16},{96,32},{112,48},{1... | collective-permute-start | bytes 159752 | tf_op jit(solution)/shard_map/ppermute | solution.py:252
  125.5 6.3 %collective-permute-done.side = bf16[16,128,128]{2,1,0:T(8,128)(2,1)S(1)} collective-permute-done((bf16[16,128,128]{2,1,0:T(8,128)(2,1)}, bf16[16,128,128]{2,1,0:T(8,128)(2,1)S(1)}, u32[]{:S(2)}, u32[]{:S(2)}) %collective-permute-start) | collective-permute-done | bytes 524320 | tf_op jit(solution)/shard_map/ppermute | solution.py:243
  131.8 0.7 slice.69
  132.6 0.8 copy-done.3
  133.4 0.0 collective-permute-done.2.edge_high
  133.4 0.0 collective-permute-done.1
  133.4 1.1 broadcast_in_dim.5
  134.5 0.0 copy-done.5
  134.5 11.1 %all-to-all-start.2 = ((f16[16,192,128]{2,1,0:T(8,128)(2,1)}), f16[16,192,128]{2,1,0:T(8,128)(2,1)}, u32[]{:S(2)}, u32[]{:S(2)}) async-start(f16[16,192,128]{2,1,0:T(8,128)(2,1)} %broadcast_in_dim.5), calls=%async_computation.2 | async-start | bytes 1572864 | tf_op jit(solution)/shard_map/all_to_all | solution.py:262
  145.7 6.1 %collective-permute-start.3 = (bf16[16,80,128]{2,1,0:T(8,128)(2,1)}, bf16[16,80,128]{2,1,0:T(8,128)(2,1)S(1)}, u32[]{:S(2)}, u32[]{:S(2)}) collective-permute-start(bf16[16,80,128]{2,1,0:T(8,128)(2,1)} %slice.69), channel_id=1, source_target_pairs={{0,64},{64,128},{128,192},{192,256},{256,320},{320,384},{384,448},... | collective-permute-start | bytes 983048 | tf_op jit(solution)/shard_map/ppermute | solution.py:254
  151.8 5.4 %all-to-all-done.2 = f16[16,192,128]{2,1,0:T(8,128)(2,1)} async-done(((f16[16,192,128]{2,1,0:T(8,128)(2,1)}), f16[16,192,128]{2,1,0:T(8,128)(2,1)}, u32[]{:S(2)}, u32[]{:S(2)}) %all-to-all-start.2) | async-done | bytes 786464 | tf_op jit(solution)/shard_map/all_to_all | solution.py:262
  157.2 1.2 convert_element_type.32.every
  158.5 0.0 copy-start.4
  158.5 0.0 copy-start.6
  158.5 8.7 %shard_map.87 = f32[1024,128]{1,0:T(8,128)} custom-call(f32[8,128]{1,0:T(8,128)S(1)} %concatenate.12.powers, f32[16,192,128]{2,1,0:T(8,128)S(1)} %convert_element_type.32.every, f32[256,512]{1,0:T(8,128)S(1)} %bitcast.33, f32[256,512]{1,0:T(8,128)S(1)} %bitcast.35, f32[512,256]{1,0:T(8,128)S(1)} %bitcast.37, bf16[16,400,128]{2,1,0:T(8,128)(2,1)S(1)} %all_to_all.15.first), custom_call_target="tpu_custom_call" | custom-call | flops 1048576 | bytes 4194304 | tf_op jit(solution)/shard_map/pallas_call | solution.py:185
  167.2 17.8 %collective-permute-done.3.edge_low = bf16[16,80,128]{2,1,0:T(8,128)(2,1)S(1)} collective-permute-done((bf16[16,80,128]{2,1,0:T(8,128)(2,1)}, bf16[16,80,128]{2,1,0:T(8,128)(2,1)S(1)}, u32[]{:S(2)}, u32[]{:S(2)}) %collective-permute-start.3) | collective-permute-done | bytes 327712 | tf_op jit(solution)/shard_map/ppermute | solution.py:254
  185.0 0.0 copy-done.4
  185.0 4.1 %shard_map.88 = f32[1024,128]{1,0:T(8,128)} custom-call(s32[1]{0:T(128)} %bitcast.place, bf16[16,400,128]{2,1,0:T(8,128)(2,1)S(1)} %all_to_all.15.first, bf16[16,128,128]{2,1,0:T(8,128)(2,1)S(1)} %copy-done.4, bf16[16,80,128]{2,1,0:T(8,128)(2,1)S(1)} %collective-permute-done.3.edge_low, bf16[16,48,128]{2,1,0:T(8,128)(2,1)S(1)} %copy-done.6), custom_call_target="tpu_custom_call" | custom-call | flops 1048576 | bytes 4194304 | tf_op jit(solution)/shard_map/pallas_call | solution.py:185
  (19 shorter events, 0.4 us)
Async XLA Ops:
  0.6 1.5 copy-start.7
  0.6 1.8 copy-start.8
  2.5 0.7 copy-start.9
  3.2 87.3 %copy-start = (f32[1,256,512]{2,1,0:T(8,128)S(1)}, f32[1,256,512]{2,1,0:T(8,128)}, u32[]{:S(2)}) copy-start(f32[1,256,512]{2,1,0:T(8,128)} %param.11) | copy-start | bytes 1572868
  3.2 87.2 %copy-start.1 = (f32[1,256,512]{2,1,0:T(8,128)S(1)}, f32[1,256,512]{2,1,0:T(8,128)}, u32[]{:S(2)}) copy-start(f32[1,256,512]{2,1,0:T(8,128)} %param.12) | copy-start | bytes 1572868
  3.2 87.2 %copy-start.2 = (f32[1,512,256]{2,1,0:T(8,128)S(1)}, f32[1,512,256]{2,1,0:T(8,128)}, u32[]{:S(2)}) copy-start(f32[1,512,256]{2,1,0:T(8,128)} %param.13) | copy-start | bytes 1572868
  93.3 19.1 %all-to-all-start.1 = ((f16[16,208,128]{2,1,0:T(8,128)(2,1)}), f16[16,208,128]{2,1,0:T(8,128)(2,1)}, u32[]{:S(2)}, u32[]{:S(2)}) async-start(f16[16,208,128]{2,1,0:T(8,128)(2,1)} %convert_element_type.26), calls=%async_computation.1 | async-start | bytes 1703936 | tf_op jit(solution)/shard_map/all_to_all | solution.py:239
  100.9 32.4 %collective-permute-start.2 = (bf16[16,48,128]{2,1,0:T(8,128)(2,1)}, bf16[16,48,128]{2,1,0:T(8,128)(2,1)S(1)}, u32[]{:S(2)}, u32[]{:S(2)}) collective-permute-start(bf16[16,48,128]{2,1,0:T(8,128)(2,1)} %slice.70), channel_id=1, source_target_pairs={{48,64},{112,128},{176,192},{240,256},{304,320},{368,384},{432,448... | collective-permute-start | bytes 589832 | tf_op jit(solution)/shard_map/ppermute | solution.py:234
  112.4 19.5 %collective-permute-start = (bf16[16,128,128]{2,1,0:T(8,128)(2,1)}, bf16[16,128,128]{2,1,0:T(8,128)(2,1)S(1)}, u32[]{:S(2)}, u32[]{:S(2)}) collective-permute-start(bf16[16,128,128]{2,1,0:T(8,128)(2,1)} %slice.68), channel_id=1, source_target_pairs={{0,16},{16,32},{32,48},{48,0},{64,80},{80,96},{96,112},{112,64},{1... | collective-permute-start | bytes 1572872 | tf_op jit(solution)/shard_map/ppermute | solution.py:243
  117.6 15.8 %collective-permute-start.1 = (f16[208,128]{1,0:T(8,128)(2,1)S(1)}, f16[208,128]{1,0:T(8,128)(2,1)S(1)}, u32[]{:S(2)}, u32[]{:S(2)}) collective-permute-start(f16[208,128]{1,0:T(8,128)(2,1)S(1)} %maximum_maximum_fusion), channel_id=1, source_target_pairs={{0,64},{16,80},{32,96},{48,112},{64,0},{80,16},{96,32},{112,48},{1... | collective-permute-start | bytes 159752 | tf_op jit(solution)/shard_map/ppermute | solution.py:252
  132.6 0.8 copy-start.3
  133.4 1.1 copy-start.5
  134.5 22.7 %all-to-all-start.2 = ((f16[16,192,128]{2,1,0:T(8,128)(2,1)}), f16[16,192,128]{2,1,0:T(8,128)(2,1)}, u32[]{:S(2)}, u32[]{:S(2)}) async-start(f16[16,192,128]{2,1,0:T(8,128)(2,1)} %broadcast_in_dim.5), calls=%async_computation.2 | async-start | bytes 1572864 | tf_op jit(solution)/shard_map/all_to_all | solution.py:262
  145.7 39.3 %collective-permute-start.3 = (bf16[16,80,128]{2,1,0:T(8,128)(2,1)}, bf16[16,80,128]{2,1,0:T(8,128)(2,1)S(1)}, u32[]{:S(2)}, u32[]{:S(2)}) collective-permute-start(bf16[16,80,128]{2,1,0:T(8,128)(2,1)} %slice.69), channel_id=1, source_target_pairs={{0,64},{64,128},{128,192},{192,256},{256,320},{320,384},{384,448},... | collective-permute-start | bytes 983048 | tf_op jit(solution)/shard_map/ppermute | solution.py:254
  158.5 26.5 %copy-start.4 = (bf16[16,128,128]{2,1,0:T(8,128)(2,1)S(1)}, bf16[16,128,128]{2,1,0:T(8,128)(2,1)}, u32[]{:S(2)}) copy-start(bf16[16,128,128]{2,1,0:T(8,128)(2,1)} %copy-done.3) | copy-start | bytes 1572868
  158.5 26.5 %copy-start.6 = (bf16[16,48,128]{2,1,0:T(8,128)(2,1)S(1)}, bf16[16,48,128]{2,1,0:T(8,128)(2,1)}, u32[]{:S(2)}) copy-start(bf16[16,48,128]{2,1,0:T(8,128)(2,1)} %copy-done.5) | copy-start | bytes 589828

commit v11 on v6

--- a/solution.py
+++ b/solution.py
@@ -20,6 +20,7 @@
 
 XS, HALVES, YS = 4, 2, 4
 PLANE = XS * YS
+CUTS = (48, 80)
 VMEM_LIMIT = 48 * 1024 * 1024
 
 
@@ -88,7 +89,7 @@
     out[:, 3 * FHID // LANES * rows :, :] = jnp.broadcast_to(tag[None], (PLANE, 16, LANES))
 
 
-def attention_kernel(place, first, side, edge_low, edge_high, out, earlier):
+def attention_kernel(place, first, side, edge_low, edge_mid, edge_high, out, earlier):
     span = first.shape[0] * TOK
     scale = 1.0 / math.sqrt(LANES)
     tile = 128
@@ -102,8 +103,9 @@
 
     @pl.when(edge)
     def _():
-        earlier[:, : 2 * TOK, :] = edge_low[...]
-        earlier[:, 2 * TOK :, :] = edge_high[...]
+        earlier[:, : CUTS[0], :] = edge_low[...]
+        earlier[:, CUTS[0] : CUTS[1], :] = edge_mid[...]
+        earlier[:, CUTS[1] :, :] = edge_high[...]
 
     @pl.when(jnp.logical_not(edge))
     def _():
@@ -230,7 +232,7 @@
     )
     first = lax.all_to_all(first, "narrow", 0, 0, tiled=True)
     tail = first[:, : 4 * rows]
-    edge_high = lax.ppermute(first[:, 2 * rows : 4 * rows], "wide", EDGE_HIGH)
+    edge_high = lax.ppermute(first[:, CUTS[1] : 4 * rows], "wide", EDGE_HIGH)
 
     weights = (gate_fast[0], up_fast[0], down_fast[0])
     count = 3 * FHID // LANES * FD // PLANE
@@ -249,7 +251,10 @@
     )
     sent = sent.astype(jnp.float16)
     other = lax.ppermute(sent, "wide", SWAP)
-    other, low_part, edge_high = lax.optimization_barrier((other, side[:, : 2 * rows], edge_high))
+    other, low_part, mid_part, edge_high = lax.optimization_barrier(
+        (other, side[:, : CUTS[0]], tail[:, CUTS[0] : CUTS[1]], edge_high)
+    )
+    edge_mid = lax.ppermute(mid_part, "wide", EDGE_HIGH)
     edge_low = lax.ppermute(low_part, "wide", EDGE_LOW)
     other_top = other[count : count + 3].astype(jnp.float32)
     both = jnp.maximum(top, other_top)
@@ -274,11 +279,11 @@
         FLOPS,
     )
     place = lax.axis_index("wide").reshape(1)
-    edge_low, fast_out = lax.optimization_barrier((edge_low, fast_out))
+    edge_low, edge_mid, fast_out = lax.optimization_barrier((edge_low, edge_mid, fast_out))
     window_out = call(
         attention_kernel,
         (span * own, LANES),
-        (place, first, side, edge_low, edge_high),
+        (place, first, side, edge_low, edge_mid, edge_high),
         FLOPS,
         1,
         [pltpu.VMEM((PLANE, 4 * TOK, LANES), jnp.bfloat16)],

time: 189 us -> 181 us (0.958)
  the two profiles are of different devices: /device:TPU:7 before, /device:TPU:98 now
where the time goes in v11:
time: 181 us
  blocking collectives  85.6 us (47%)
  starting transfers between devices  38.5 us (21%)
  waiting for transfers between devices  26.5 us (15%)
  Pallas kernels  15.6 us (9%)
  local copies, waits for them, and re-layouts  8.21 us (5%)
  other arithmetic  5.32 us (3%)
    all_to_all x1, blocking collectives, per_device(): first = lax.all_to_all(first, 'narrow', 0, 0, tiled=True)  85.6 us
    pallas_call x3, Pallas kernels, call(): pl.pallas_call(kernel, out_shape=jax.ShapeDtypeStruct(shape, jnp.float32)...  15.6 us
    ppermute x1, waiting for transfers between devices, per_device(): edge_mid = lax.ppermute(mid_part, 'wide', EDGE_HIGH)  11.5 us
    all_to_all x1, waiting for transfers between devices, per_device(): lax.all_to_all(pieces.astype(jnp.float16), 'wide', 0, 0, tiled=True, axis...  10.3 us
    all_to_all x1, starting transfers between devices, per_device(): lax.all_to_all(jnp.broadcast_to(whole[None], (PLANE, count, LANES)), 'wid...  9.55 us
    ppermute x1, starting transfers between devices, per_device(): other = lax.ppermute(sent, 'wide', SWAP)  8.22 us
    ppermute x1, starting transfers between devices, per_device(): edge_low = lax.ppermute(low_part, 'wide', EDGE_LOW)  8.08 us
    all_to_all x1, starting transfers between devices, per_device(): lax.all_to_all(pieces.astype(jnp.float16), 'wide', 0, 0, tiled=True, axis...  7.48 us
  transfers between devices with their start and end apart: 7, of which 4 were waited for; matrix products, arithmetic and copies ran while one was open for 4% of the time, Pallas kernels for 5%

profile of v11, /device:TPU:98, one launch (start us, length us, event | category | flops | bytes accessed | tf_op | source)
XLA Modules:
  0.0 180.7 jit_solution(1646058050753258445)
XLA Ops:
  0.6 0.0 copy-start.5
  0.6 0.0 copy-start.6
  0.6 1.4 copy.16
  2.1 0.0 copy-done.5
  2.1 0.3 copy.9
  2.5 0.0 copy-start.7
  2.5 0.0 copy-done.6
  2.5 0.1 copy.10
  2.8 0.1 slice_dynamic-update-slice_fusion
  3.0 0.2 copy-done.7
  3.2 0.0 copy-start
  3.2 0.0 copy-start.1
  3.2 0.0 copy-start.2
  3.2 85.6 %all_to_all.15.first = bf16[16,400,128]{2,1,0:T(8,128)(2,1)S(1)} all-to-all(bf16[16,400,128]{2,1,0:T(8,128)(2,1)S(1)} %pad_dynamic-update-slice_fusion), channel_id=1, replica_groups=mesh['wide'=32,'narrow'=16] {'narrow'}, dimensions={0} | all-to-all | bytes 3276800 | tf_op jit(solution)/shard_map/all_to_all | solution.py:233
  88.9 0.0 copy-done
  88.9 0.0 copy-done.2
  88.9 1.8 shard_map.86
  90.6 1.1 convert_element_type.26
  91.7 7.5 %all-to-all-start.1 = ((f16[16,208,128]{2,1,0:T(8,128)(2,1)}), f16[16,208,128]{2,1,0:T(8,128)(2,1)}, u32[]{:S(2)}, u32[]{:S(2)}) async-start(f16[16,208,128]{2,1,0:T(8,128)(2,1)} %convert_element_type.26), calls=%async_computation.1 | async-start | bytes 1703936 | tf_op jit(solution)/shard_map/all_to_all | solution.py:240
  99.2 0.1 pad.8.clone
  99.3 0.7 slice.74
  100.0 1.3 collective-permute-start.2
  101.2 0.8 slice.72
  102.1 10.3 %all-to-all-done.1 = f16[16,208,128]{2,1,0:T(8,128)(2,1)} async-done(((f16[16,208,128]{2,1,0:T(8,128)(2,1)}), f16[16,208,128]{2,1,0:T(8,128)(2,1)}, u32[]{:S(2)}, u32[]{:S(2)}) %all-to-all-start.1) | async-done | bytes 852000 | tf_op jit(solution)/shard_map/all_to_all | solution.py:240
  112.4 2.5 %collective-permute-start = (bf16[16,128,128]{2,1,0:T(8,128)(2,1)}, bf16[16,128,128]{2,1,0:T(8,128)(2,1)S(1)}, u32[]{:S(2)}, u32[]{:S(2)}) collective-permute-start(bf16[16,128,128]{2,1,0:T(8,128)(2,1)} %slice.72), channel_id=1, source_target_pairs={{0,16},{16,32},{32,48},{48,0},{64,80},{80,96},{96,112},{112,64},{1... | collective-permute-start | bytes 1572872 | tf_op jit(solution)/shard_map/ppermute | solution.py:244
  114.9 0.8 convert_reduce_fusion
  115.7 0.8 fusion.5
  116.4 1.3 fusion
  117.8 0.1 maximum_maximum_fusion
  117.9 8.2 %collective-permute-start.1 = (f16[208,128]{1,0:T(8,128)(2,1)S(1)}, f16[208,128]{1,0:T(8,128)(2,1)S(1)}, u32[]{:S(2)}, u32[]{:S(2)}) collective-permute-start(f16[208,128]{1,0:T(8,128)(2,1)S(1)} %maximum_maximum_fusion), channel_id=1, source_target_pairs={{0,64},{16,80},{32,96},{48,112},{64,0},{80,16},{96,32},{112,48},{1... | collective-permute-start | bytes 159752 | tf_op jit(solution)/shard_map/ppermute | solution.py:253
  126.1 1.6 slice.60
  127.7 4.0 %collective-permute-done.side = bf16[16,128,128]{2,1,0:T(8,128)(2,1)S(1)} collective-permute-done((bf16[16,128,128]{2,1,0:T(8,128)(2,1)}, bf16[16,128,128]{2,1,0:T(8,128)(2,1)S(1)}, u32[]{:S(2)}, u32[]{:S(2)}) %collective-permute-start) | collective-permute-done | bytes 524320 | tf_op jit(solution)/shard_map/ppermute | solution.py:244
  131.7 0.7 slice.73
  132.4 0.8 copy-done.3
  133.2 0.0 collective-permute-done.2.edge_high
  133.2 0.6 collective-permute-done.1
  133.8 1.1 broadcast_in_dim.5
  134.9 9.6 %all-to-all-start.2 = ((f16[16,192,128]{2,1,0:T(8,128)(2,1)}), f16[16,192,128]{2,1,0:T(8,128)(2,1)}, u32[]{:S(2)}, u32[]{:S(2)}) async-start(f16[16,192,128]{2,1,0:T(8,128)(2,1)} %broadcast_in_dim.5), calls=%async_computation.2 | async-start | bytes 1572864 | tf_op jit(solution)/shard_map/all_to_all | solution.py:266
  144.5 8.1 %collective-permute-start.3 = (bf16[16,48,128]{2,1,0:T(8,128)(2,1)}, bf16[16,48,128]{2,1,0:T(8,128)(2,1)}, u32[]{:S(2)}, u32[]{:S(2)}) collective-permute-start(bf16[16,48,128]{2,1,0:T(8,128)(2,1)} %slice.73), channel_id=1, source_target_pairs={{0,64},{64,128},{128,192},{192,256},{256,320},{320,384},{384,448},... | collective-permute-start | bytes 589832 | tf_op jit(solution)/shard_map/ppermute | solution.py:258
  152.5 1.5 collective-permute-start.4
  154.0 0.0 all-to-all-done.2
  154.1 1.2 convert_element_type.32.every
  155.3 0.0 copy-start.4
  155.3 8.7 %shard_map.87 = f32[1024,128]{1,0:T(8,128)} custom-call(f32[8,128]{1,0:T(8,128)S(1)} %concatenate.12.powers, f32[16,192,128]{2,1,0:T(8,128)S(1)} %convert_element_type.32.every, f32[256,512]{1,0:T(8,128)S(1)} %bitcast.33, f32[256,512]{1,0:T(8,128)S(1)} %bitcast.35, f32[512,256]{1,0:T(8,128)S(1)} %bitcast.37, bf16[16,400,128]{2,1,0:T(8,128)(2,1)S(1)} %all_to_all.15.first), custom_call_target="tpu_custom_call" | custom-call | flops 1048576 | bytes 4194304 | tf_op jit(solution)/shard_map/pallas_call | solution.py:186
  164.1 11.5 %collective-permute-done.4.edge_mid = bf16[16,32,128]{2,1,0:T(8,128)(2,1)S(1)} collective-permute-done((bf16[16,32,128]{2,1,0:T(8,128)(2,1)}, bf16[16,32,128]{2,1,0:T(8,128)(2,1)S(1)}, u32[]{:S(2)}, u32[]{:S(2)}) %collective-permute-start.4) | collective-permute-done | bytes 131104 | tf_op jit(solution)/shard_map/ppermute | solution.py:257
  175.6 0.0 collective-permute-done.3.edge_low
  175.6 0.0 copy-done.4
  175.6 5.0 %shard_map.88 = f32[1024,128]{1,0:T(8,128)} custom-call(s32[1]{0:T(128)} %bitcast.place, bf16[16,400,128]{2,1,0:T(8,128)(2,1)S(1)} %all_to_all.15.first, bf16[16,128,128]{2,1,0:T(8,128)(2,1)S(1)} %copy-done.4, bf16[16,48,128]{2,1,0:T(8,128)(2,1)} %collective-permute-done.3.edge_low, bf16[16,32,128]{2,1,0:T(8,128)(2,1)S(1)} %collective-permute-done.4.edge_mid, ...), custom_call_target="tpu_custom_call" | custom-call | flops 1048576 | bytes 4194304 | tf_op jit(solution)/shard_map/pallas_call | solution.py:186
  (18 shorter events, 0.4 us)
Async XLA Ops:
  0.6 1.5 copy-start.5
  0.6 1.8 %copy-start.6 = (bf16[32,32,128]{2,1,0:T(8,128)(2,1)S(1)}, bf16[32,32,128]{2,1,0:T(8,128)(2,1)}, u32[]{:S(2)}) copy-start(bf16[32,32,128]{2,1,0:T(8,128)(2,1)} %param.8) | copy-start | bytes 786436
  2.5 0.7 copy-start.7
  3.2 85.7 %copy-start = (f32[1,256,512]{2,1,0:T(8,128)S(1)}, f32[1,256,512]{2,1,0:T(8,128)}, u32[]{:S(2)}) copy-start(f32[1,256,512]{2,1,0:T(8,128)} %param.11) | copy-start | bytes 1572868
  3.2 85.7 %copy-start.1 = (f32[1,256,512]{2,1,0:T(8,128)S(1)}, f32[1,256,512]{2,1,0:T(8,128)}, u32[]{:S(2)}) copy-start(f32[1,256,512]{2,1,0:T(8,128)} %param.12) | copy-start | bytes 1572868
  3.2 85.6 %copy-start.2 = (f32[1,512,256]{2,1,0:T(8,128)S(1)}, f32[1,512,256]{2,1,0:T(8,128)}, u32[]{:S(2)}) copy-start(f32[1,512,256]{2,1,0:T(8,128)} %param.13) | copy-start | bytes 1572868
  91.7 20.7 %all-to-all-start.1 = ((f16[16,208,128]{2,1,0:T(8,128)(2,1)}), f16[16,208,128]{2,1,0:T(8,128)(2,1)}, u32[]{:S(2)}, u32[]{:S(2)}) async-start(f16[16,208,128]{2,1,0:T(8,128)(2,1)} %convert_element_type.26), calls=%async_computation.1 | async-start | bytes 1703936 | tf_op jit(solution)/shard_map/all_to_all | solution.py:240
  100.0 33.3 %collective-permute-start.2 = (bf16[16,48,128]{2,1,0:T(8,128)(2,1)}, bf16[16,48,128]{2,1,0:T(8,128)(2,1)S(1)}, u32[]{:S(2)}, u32[]{:S(2)}) collective-permute-start(bf16[16,48,128]{2,1,0:T(8,128)(2,1)} %slice.74), channel_id=1, source_target_pairs={{48,64},{112,128},{176,192},{240,256},{304,320},{368,384},{432,448... | collective-permute-start | bytes 589832 | tf_op jit(solution)/shard_map/ppermute | solution.py:235
  112.4 19.3 %collective-permute-start = (bf16[16,128,128]{2,1,0:T(8,128)(2,1)}, bf16[16,128,128]{2,1,0:T(8,128)(2,1)S(1)}, u32[]{:S(2)}, u32[]{:S(2)}) collective-permute-start(bf16[16,128,128]{2,1,0:T(8,128)(2,1)} %slice.72), channel_id=1, source_target_pairs={{0,16},{16,32},{32,48},{48,0},{64,80},{80,96},{96,112},{112,64},{1... | collective-permute-start | bytes 1572872 | tf_op jit(solution)/shard_map/ppermute | solution.py:244
  117.9 15.9 %collective-permute-start.1 = (f16[208,128]{1,0:T(8,128)(2,1)S(1)}, f16[208,128]{1,0:T(8,128)(2,1)S(1)}, u32[]{:S(2)}, u32[]{:S(2)}) collective-permute-start(f16[208,128]{1,0:T(8,128)(2,1)S(1)} %maximum_maximum_fusion), channel_id=1, source_target_pairs={{0,64},{16,80},{32,96},{48,112},{64,0},{80,16},{96,32},{112,48},{1... | collective-permute-start | bytes 159752 | tf_op jit(solution)/shard_map/ppermute | solution.py:253
  132.4 0.8 copy-start.3
  134.9 19.1 %all-to-all-start.2 = ((f16[16,192,128]{2,1,0:T(8,128)(2,1)}), f16[16,192,128]{2,1,0:T(8,128)(2,1)}, u32[]{:S(2)}, u32[]{:S(2)}) async-start(f16[16,192,128]{2,1,0:T(8,128)(2,1)} %broadcast_in_dim.5), calls=%async_computation.2 | async-start | bytes 1572864 | tf_op jit(solution)/shard_map/all_to_all | solution.py:266
  144.5 31.2 %collective-permute-start.3 = (bf16[16,48,128]{2,1,0:T(8,128)(2,1)}, bf16[16,48,128]{2,1,0:T(8,128)(2,1)}, u32[]{:S(2)}, u32[]{:S(2)}) collective-permute-start(bf16[16,48,128]{2,1,0:T(8,128)(2,1)} %slice.73), channel_id=1, source_target_pairs={{0,64},{64,128},{128,192},{192,256},{256,320},{320,384},{384,448},... | collective-permute-start | bytes 589832 | tf_op jit(solution)/shard_map/ppermute | solution.py:258
  152.5 23.1 %collective-permute-start.4 = (bf16[16,32,128]{2,1,0:T(8,128)(2,1)}, bf16[16,32,128]{2,1,0:T(8,128)(2,1)S(1)}, u32[]{:S(2)}, u32[]{:S(2)}) collective-permute-start(bf16[16,32,128]{2,1,0:T(8,128)(2,1)} %slice.60), channel_id=1, source_target_pairs={{48,64},{112,128},{176,192},{240,256},{304,320},{368,384},{432,448... | collective-permute-start | bytes 393224 | tf_op jit(solution)/shard_map/ppermute | solution.py:257
  155.3 20.3 %copy-start.4 = (bf16[16,128,128]{2,1,0:T(8,128)(2,1)S(1)}, bf16[16,128,128]{2,1,0:T(8,128)(2,1)}, u32[]{:S(2)}) copy-start(bf16[16,128,128]{2,1,0:T(8,128)(2,1)} %copy-done.3) | copy-start | bytes 1572868

commit v12 on v11

--- a/solution.py
+++ b/solution.py
@@ -20,7 +20,7 @@
 
 XS, HALVES, YS = 4, 2, 4
 PLANE = XS * YS
-CUTS = (48, 80)
+CUTS = (48, 96)
 VMEM_LIMIT = 48 * 1024 * 1024
 
 

time: 181 us -> 187 us (1.033)
  the two profiles are of different devices: /device:TPU:98 before, /device:TPU:7 now
where the time goes in v12:
time: 187 us; the launch traced here: 186 us
  blocking collectives  89.8 us (48%)
  starting transfers between devices  33.9 us (18%)
  waiting for transfers between devices  33.3 us (18%)
  Pallas kernels  15.5 us (8%)
  local copies, waits for them, and re-layouts  7.58 us (4%)
  other arithmetic  5.31 us (3%)
    all_to_all x1, blocking collectives, per_device(): first = lax.all_to_all(first, 'narrow', 0, 0, tiled=True)  89.8 us
    pallas_call x3, Pallas kernels, call(): pl.pallas_call(kernel, out_shape=jax.ShapeDtypeStruct(shape, jnp.float32)...  15.5 us
    ppermute x1, waiting for transfers between devices, per_device(): edge_mid = lax.ppermute(mid_part, 'wide', EDGE_HIGH)  11.9 us
    all_to_all x1, waiting for transfers between devices, per_device(): lax.all_to_all(pieces.astype(jnp.float16), 'wide', 0, 0, tiled=True, axis...  9.99 us
    ppermute x1, waiting for transfers between devices, per_device(): edge_low = lax.ppermute(low_part, 'wide', EDGE_LOW)  8.68 us
    ppermute x1, starting transfers between devices, per_device(): other = lax.ppermute(sent, 'wide', SWAP)  7.93 us
    all_to_all x1, starting transfers between devices, per_device(): lax.all_to_all(jnp.broadcast_to(whole[None], (PLANE, count, LANES)), 'wid...  7.13 us
    ppermute x1, starting transfers between devices, per_device(): edge_low = lax.ppermute(low_part, 'wide', EDGE_LOW)  7.02 us
  transfers between devices with their start and end apart: 7, of which 6 were waited for; matrix products, arithmetic and copies ran while one was open for 4% of the time, Pallas kernels for 5%

profile of v12, /device:TPU:7, one launch (start us, length us, event | category | flops | bytes accessed | tf_op | source)
XLA Modules:
  0.0 186.4 jit_solution(17050947449759684937)
XLA Ops:
  0.6 0.0 copy-start.5
  0.6 0.0 copy-start.6
  0.6 1.4 copy.16
  2.1 0.0 copy-done.5
  2.1 0.3 copy.9
  2.5 0.0 copy-start.7
  2.5 0.0 copy-done.6
  2.5 0.1 copy.10
  2.8 0.1 slice_dynamic-update-slice_fusion
  3.0 0.2 copy-done.7
  3.2 0.0 copy-start
  3.2 0.0 copy-start.1
  3.2 0.0 copy-start.2
  3.2 89.8 %all_to_all.15.first = bf16[16,400,128]{2,1,0:T(8,128)(2,1)S(1)} all-to-all(bf16[16,400,128]{2,1,0:T(8,128)(2,1)S(1)} %pad_dynamic-update-slice_fusion), channel_id=1, replica_groups=mesh['wide'=32,'narrow'=16] {'narrow'}, dimensions={0} | all-to-all | bytes 3276800 | tf_op jit(solution)/shard_map/all_to_all | solution.py:233
  93.1 0.0 copy-done
  93.1 0.0 copy-done.1
  93.1 0.0 copy-done.2
  93.1 1.8 shard_map.86
  94.8 1.1 convert_element_type.26
  95.9 6.9 %all-to-all-start.1 = ((f16[16,208,128]{2,1,0:T(8,128)(2,1)}), f16[16,208,128]{2,1,0:T(8,128)(2,1)}, u32[]{:S(2)}, u32[]{:S(2)}) async-start(f16[16,208,128]{2,1,0:T(8,128)(2,1)} %convert_element_type.26), calls=%async_computation.1 | async-start | bytes 1703936 | tf_op jit(solution)/shard_map/all_to_all | solution.py:240
  102.8 0.1 pad.8.clone
  102.9 1.3 collective-permute-start.2
  104.2 0.8 slice.72
  105.0 10.0 %all-to-all-done.1 = f16[16,208,128]{2,1,0:T(8,128)(2,1)} async-done(((f16[16,208,128]{2,1,0:T(8,128)(2,1)}), f16[16,208,128]{2,1,0:T(8,128)(2,1)}, u32[]{:S(2)}, u32[]{:S(2)}) %all-to-all-start.1) | async-done | bytes 852000 | tf_op jit(solution)/shard_map/all_to_all | solution.py:240
  115.0 2.2 %collective-permute-start = (bf16[16,128,128]{2,1,0:T(8,128)(2,1)}, bf16[16,128,128]{2,1,0:T(8,128)(2,1)S(1)}, u32[]{:S(2)}, u32[]{:S(2)}) collective-permute-start(bf16[16,128,128]{2,1,0:T(8,128)(2,1)} %slice.72), channel_id=1, source_target_pairs={{0,16},{16,32},{32,48},{48,0},{64,80},{80,96},{96,112},{112,64},{1... | collective-permute-start | bytes 1572872 | tf_op jit(solution)/shard_map/ppermute | solution.py:244
  117.2 0.8 convert_reduce_fusion
  118.0 0.8 fusion.5
  118.8 1.3 fusion
  120.1 0.1 maximum_maximum_fusion
  120.2 7.9 %collective-permute-start.1 = (f16[208,128]{1,0:T(8,128)(2,1)S(1)}, f16[208,128]{1,0:T(8,128)(2,1)S(1)}, u32[]{:S(2)}, u32[]{:S(2)}) collective-permute-start(f16[208,128]{1,0:T(8,128)(2,1)S(1)} %maximum_maximum_fusion), channel_id=1, source_target_pairs={{0,64},{16,80},{32,96},{48,112},{64,0},{80,16},{96,32},{112,48},{1... | collective-permute-start | bytes 159752 | tf_op jit(solution)/shard_map/ppermute | solution.py:253
  128.1 1.6 slice.60
  129.8 2.3 %collective-permute-done.side = bf16[16,128,128]{2,1,0:T(8,128)(2,1)S(1)} collective-permute-done((bf16[16,128,128]{2,1,0:T(8,128)(2,1)}, bf16[16,128,128]{2,1,0:T(8,128)(2,1)S(1)}, u32[]{:S(2)}, u32[]{:S(2)}) %collective-permute-start) | collective-permute-done | bytes 524320 | tf_op jit(solution)/shard_map/ppermute | solution.py:244
  132.0 0.7 slice.73
  132.7 0.8 copy-done.3
  133.5 0.0 collective-permute-done.2.edge_high
  133.5 0.3 collective-permute-done.1
  133.8 1.1 broadcast_in_dim.5
  134.9 7.1 %all-to-all-start.2 = ((f16[16,192,128]{2,1,0:T(8,128)(2,1)}), f16[16,192,128]{2,1,0:T(8,128)(2,1)}, u32[]{:S(2)}, u32[]{:S(2)}) async-start(f16[16,192,128]{2,1,0:T(8,128)(2,1)} %broadcast_in_dim.5), calls=%async_computation.2 | async-start | bytes 1572864 | tf_op jit(solution)/shard_map/all_to_all | solution.py:266
  142.0 7.0 %collective-permute-start.3 = (bf16[16,48,128]{2,1,0:T(8,128)(2,1)}, bf16[16,48,128]{2,1,0:T(8,128)(2,1)S(1)}, u32[]{:S(2)}, u32[]{:S(2)}) collective-permute-start(bf16[16,48,128]{2,1,0:T(8,128)(2,1)} %slice.73), channel_id=1, source_target_pairs={{0,64},{64,128},{128,192},{192,256},{256,320},{320,384},{384,448},... | collective-permute-start | bytes 589832 | tf_op jit(solution)/shard_map/ppermute | solution.py:258
  149.1 1.5 collective-permute-start.4
  150.6 0.2 all-to-all-done.2
  150.7 1.2 convert_element_type.32.every
  152.0 0.0 copy-start.4
  152.0 8.7 %shard_map.87 = f32[1024,128]{1,0:T(8,128)} custom-call(f32[8,128]{1,0:T(8,128)S(1)} %concatenate.12.powers, f32[16,192,128]{2,1,0:T(8,128)S(1)} %convert_element_type.32.every, f32[256,512]{1,0:T(8,128)S(1)} %bitcast.33, f32[256,512]{1,0:T(8,128)S(1)} %bitcast.35, f32[512,256]{1,0:T(8,128)S(1)} %bitcast.37, bf16[16,400,128]{2,1,0:T(8,128)(2,1)S(1)} %all_to_all.15.first), custom_call_target="tpu_custom_call" | custom-call | flops 1048576 | bytes 4194304 | tf_op jit(solution)/shard_map/pallas_call | solution.py:186
  160.7 8.7 %collective-permute-done.3.edge_low = bf16[16,48,128]{2,1,0:T(8,128)(2,1)S(1)} collective-permute-done((bf16[16,48,128]{2,1,0:T(8,128)(2,1)}, bf16[16,48,128]{2,1,0:T(8,128)(2,1)S(1)}, u32[]{:S(2)}, u32[]{:S(2)}) %collective-permute-start.3) | collective-permute-done | bytes 196640 | tf_op jit(solution)/shard_map/ppermute | solution.py:258
  169.4 11.9 %collective-permute-done.4.edge_mid = bf16[16,48,128]{2,1,0:T(8,128)(2,1)} collective-permute-done((bf16[16,48,128]{2,1,0:T(8,128)(2,1)}, bf16[16,48,128]{2,1,0:T(8,128)(2,1)}, u32[]{:S(2)}, u32[]{:S(2)}) %collective-permute-start.4) | collective-permute-done | bytes 196640 | tf_op jit(solution)/shard_map/ppermute | solution.py:257
  181.4 0.0 copy-done.4
  181.4 5.0 %shard_map.88 = f32[1024,128]{1,0:T(8,128)} custom-call(s32[1]{0:T(128)} %bitcast.place, bf16[16,400,128]{2,1,0:T(8,128)(2,1)S(1)} %all_to_all.15.first, bf16[16,128,128]{2,1,0:T(8,128)(2,1)S(1)} %copy-done.4, bf16[16,48,128]{2,1,0:T(8,128)(2,1)S(1)} %collective-permute-done.3.edge_low, bf16[16,48,128]{2,1,0:T(8,128)(2,1)} %collective-permute-done.4.edge_mid, ...), custom_call_target="tpu_custom_call" | custom-call | flops 1048576 | bytes 4194304 | tf_op jit(solution)/shard_map/pallas_call | solution.py:186
  (18 shorter events, 0.4 us)
Async XLA Ops:
  0.6 1.5 copy-start.5
  0.6 1.8 copy-start.6
  2.5 0.7 copy-start.7
  3.2 89.9 %copy-start = (f32[1,256,512]{2,1,0:T(8,128)S(1)}, f32[1,256,512]{2,1,0:T(8,128)}, u32[]{:S(2)}) copy-start(f32[1,256,512]{2,1,0:T(8,128)} %param.11) | copy-start | bytes 1572868
  3.2 89.9 %copy-start.1 = (f32[1,256,512]{2,1,0:T(8,128)S(1)}, f32[1,256,512]{2,1,0:T(8,128)}, u32[]{:S(2)}) copy-start(f32[1,256,512]{2,1,0:T(8,128)} %param.12) | copy-start | bytes 1572868
  3.2 89.9 %copy-start.2 = (f32[1,512,256]{2,1,0:T(8,128)S(1)}, f32[1,512,256]{2,1,0:T(8,128)}, u32[]{:S(2)}) copy-start(f32[1,512,256]{2,1,0:T(8,128)} %param.13) | copy-start | bytes 1572868
  95.9 19.1 %all-to-all-start.1 = ((f16[16,208,128]{2,1,0:T(8,128)(2,1)}), f16[16,208,128]{2,1,0:T(8,128)(2,1)}, u32[]{:S(2)}, u32[]{:S(2)}) async-start(f16[16,208,128]{2,1,0:T(8,128)(2,1)} %convert_element_type.26), calls=%async_computation.1 | async-start | bytes 1703936 | tf_op jit(solution)/shard_map/all_to_all | solution.py:240
  102.9 30.6 %collective-permute-start.2 = (bf16[16,32,128]{2,1,0:T(8,128)(2,1)S(1)}, bf16[16,32,128]{2,1,0:T(8,128)(2,1)S(1)}, u32[]{:S(2)}, u32[]{:S(2)}) collective-permute-start(bf16[16,32,128]{2,1,0:T(8,128)(2,1)S(1)} %slice.74), channel_id=1, source_target_pairs={{48,64},{112,128},{176,192},{240,256},{304,320},{368,384},{432,448... | collective-permute-start | bytes 393224 | tf_op jit(solution)/shard_map/ppermute | solution.py:235
  115.0 17.0 %collective-permute-start = (bf16[16,128,128]{2,1,0:T(8,128)(2,1)}, bf16[16,128,128]{2,1,0:T(8,128)(2,1)S(1)}, u32[]{:S(2)}, u32[]{:S(2)}) collective-permute-start(bf16[16,128,128]{2,1,0:T(8,128)(2,1)} %slice.72), channel_id=1, source_target_pairs={{0,16},{16,32},{32,48},{48,0},{64,80},{80,96},{96,112},{112,64},{1... | collective-permute-start | bytes 1572872 | tf_op jit(solution)/shard_map/ppermute | solution.py:244
  120.2 13.6 %collective-permute-start.1 = (f16[208,128]{1,0:T(8,128)(2,1)S(1)}, f16[208,128]{1,0:T(8,128)(2,1)S(1)}, u32[]{:S(2)}, u32[]{:S(2)}) collective-permute-start(f16[208,128]{1,0:T(8,128)(2,1)S(1)} %maximum_maximum_fusion), channel_id=1, source_target_pairs={{0,64},{16,80},{32,96},{48,112},{64,0},{80,16},{96,32},{112,48},{1... | collective-permute-start | bytes 159752 | tf_op jit(solution)/shard_map/ppermute | solution.py:253
  132.7 0.8 copy-start.3
  134.9 15.8 %all-to-all-start.2 = ((f16[16,192,128]{2,1,0:T(8,128)(2,1)}), f16[16,192,128]{2,1,0:T(8,128)(2,1)}, u32[]{:S(2)}, u32[]{:S(2)}) async-start(f16[16,192,128]{2,1,0:T(8,128)(2,1)} %broadcast_in_dim.5), calls=%async_computation.2 | async-start | bytes 1572864 | tf_op jit(solution)/shard_map/all_to_all | solution.py:266
  142.0 27.4 %collective-permute-start.3 = (bf16[16,48,128]{2,1,0:T(8,128)(2,1)}, bf16[16,48,128]{2,1,0:T(8,128)(2,1)S(1)}, u32[]{:S(2)}, u32[]{:S(2)}) collective-permute-start(bf16[16,48,128]{2,1,0:T(8,128)(2,1)} %slice.73), channel_id=1, source_target_pairs={{0,64},{64,128},{128,192},{192,256},{256,320},{320,384},{384,448},... | collective-permute-start | bytes 589832 | tf_op jit(solution)/shard_map/ppermute | solution.py:258
  149.1 32.3 %collective-permute-start.4 = (bf16[16,48,128]{2,1,0:T(8,128)(2,1)}, bf16[16,48,128]{2,1,0:T(8,128)(2,1)}, u32[]{:S(2)}, u32[]{:S(2)}) collective-permute-start(bf16[16,48,128]{2,1,0:T(8,128)(2,1)} %slice.60), channel_id=1, source_target_pairs={{48,64},{112,128},{176,192},{240,256},{304,320},{368,384},{432,448... | collective-permute-start | bytes 589832 | tf_op jit(solution)/shard_map/ppermute | solution.py:257
  152.0 29.4 %copy-start.4 = (bf16[16,128,128]{2,1,0:T(8,128)(2,1)S(1)}, bf16[16,128,128]{2,1,0:T(8,128)(2,1)}, u32[]{:S(2)}) copy-start(bf16[16,128,128]{2,1,0:T(8,128)(2,1)} %copy-done.3) | copy-start | bytes 1572868

commit v13 on v12

--- a/solution.py
+++ b/solution.py
@@ -20,7 +20,7 @@
 
 XS, HALVES, YS = 4, 2, 4
 PLANE = XS * YS
-CUTS = (48, 96)
+CUTS = (64, 80)
 VMEM_LIMIT = 48 * 1024 * 1024
 
 

time: 187 us -> 184 us (0.984)
  the two profiles are of different devices: /device:TPU:7 before, /device:TPU:71 now
where the time goes in v13:
time: 184 us; the launch traced here: 183 us
  blocking collectives  87.2 us (47%)
  starting transfers between devices  36.8 us (20%)
  waiting for transfers between devices  30.3 us (16%)
  Pallas kernels  14.6 us (8%)
  local copies, waits for them, and re-layouts  8.23 us (4%)
  other arithmetic  5.31 us (3%)
    all_to_all x1, blocking collectives, per_device(): first = lax.all_to_all(first, 'narrow', 0, 0, tiled=True)  87.2 us
    pallas_call x3, Pallas kernels, call(): pl.pallas_call(kernel, out_shape=jax.ShapeDtypeStruct(shape, jnp.float32)...  14.6 us
    all_to_all x1, starting transfers between devices, per_device(): lax.all_to_all(jnp.broadcast_to(whole[None], (PLANE, count, LANES)), 'wid...  11.1 us
    ppermute x1, waiting for transfers between devices, per_device(): edge_low = lax.ppermute(low_part, 'wide', EDGE_LOW)  10.7 us
    all_to_all x1, waiting for transfers between devices, per_device(): lax.all_to_all(pieces.astype(jnp.float16), 'wide', 0, 0, tiled=True, axis...  9.3 us
    ppermute x1, starting transfers between devices, per_device(): other = lax.ppermute(sent, 'wide', SWAP)  7.95 us
    all_to_all x1, starting transfers between devices, per_device(): lax.all_to_all(pieces.astype(jnp.float16), 'wide', 0, 0, tiled=True, axis...  6.86 us
    ppermute x1, starting transfers between devices, per_device(): edge_low = lax.ppermute(low_part, 'wide', EDGE_LOW)  5.93 us
  transfers between devices with their start and end apart: 7, of which 5 were waited for; matrix products, arithmetic and copies ran while one was open for 4% of the time, Pallas kernels for 5%

profile of v13, /device:TPU:71, one launch (start us, length us, event | category | flops | bytes accessed | tf_op | source)
XLA Modules:
  0.0 183.4 jit_solution(9416273792115375914)
XLA Ops:
  0.6 0.0 copy-start.7
  0.6 0.0 copy-start.8
  0.6 1.4 copy.16
  2.1 0.0 copy-done.7
  2.1 0.3 copy.9
  2.5 0.0 copy-start.9
  2.5 0.0 copy-done.8
  2.5 0.1 copy.10
  2.8 0.1 slice_dynamic-update-slice_fusion
  3.0 0.2 copy-done.9
  3.2 0.0 copy-start
  3.2 0.0 copy-start.1
  3.2 0.0 copy-start.2
  3.2 87.2 %all_to_all.15.first = bf16[16,400,128]{2,1,0:T(8,128)(2,1)S(1)} all-to-all(bf16[16,400,128]{2,1,0:T(8,128)(2,1)S(1)} %pad_dynamic-update-slice_fusion), channel_id=1, replica_groups=mesh['wide'=32,'narrow'=16] {'narrow'}, dimensions={0} | all-to-all | bytes 3276800 | tf_op jit(solution)/shard_map/all_to_all | solution.py:233
  90.5 0.0 copy-done
  90.5 0.0 copy-done.1
  90.5 0.0 copy-done.2
  90.5 1.8 shard_map.86
  92.2 1.0 convert_element_type.26
  93.3 6.9 %all-to-all-start.1 = ((f16[16,208,128]{2,1,0:T(8,128)(2,1)}), f16[16,208,128]{2,1,0:T(8,128)(2,1)}, u32[]{:S(2)}, u32[]{:S(2)}) async-start(f16[16,208,128]{2,1,0:T(8,128)(2,1)} %convert_element_type.26), calls=%async_computation.1 | async-start | bytes 1703936 | tf_op jit(solution)/shard_map/all_to_all | solution.py:240
  100.1 0.1 pad.8.clone
  100.2 0.7 slice.74
  100.9 1.3 collective-permute-start.2
  102.2 0.8 slice.72
  103.1 9.3 %all-to-all-done.1 = f16[16,208,128]{2,1,0:T(8,128)(2,1)} async-done(((f16[16,208,128]{2,1,0:T(8,128)(2,1)}), f16[16,208,128]{2,1,0:T(8,128)(2,1)}, u32[]{:S(2)}, u32[]{:S(2)}) %all-to-all-start.1) | async-done | bytes 852000 | tf_op jit(solution)/shard_map/all_to_all | solution.py:240
  112.4 2.2 %collective-permute-start = (bf16[16,128,128]{2,1,0:T(8,128)(2,1)}, bf16[16,128,128]{2,1,0:T(8,128)(2,1)S(1)}, u32[]{:S(2)}, u32[]{:S(2)}) collective-permute-start(bf16[16,128,128]{2,1,0:T(8,128)(2,1)} %slice.72), channel_id=1, source_target_pairs={{0,16},{16,32},{32,48},{48,0},{64,80},{80,96},{96,112},{112,64},{1... | collective-permute-start | bytes 1572872 | tf_op jit(solution)/shard_map/ppermute | solution.py:244
  114.6 0.8 convert_reduce_fusion
  115.4 0.8 fusion.5
  116.1 1.3 fusion
  117.5 0.1 maximum_maximum_fusion
  117.6 8.0 %collective-permute-start.1 = (f16[208,128]{1,0:T(8,128)(2,1)S(1)}, f16[208,128]{1,0:T(8,128)(2,1)S(1)}, u32[]{:S(2)}, u32[]{:S(2)}) collective-permute-start(f16[208,128]{1,0:T(8,128)(2,1)S(1)} %maximum_maximum_fusion), channel_id=1, source_target_pairs={{0,64},{16,80},{32,96},{48,112},{64,0},{80,16},{96,32},{112,48},{1... | collective-permute-start | bytes 159752 | tf_op jit(solution)/shard_map/ppermute | solution.py:253
  125.5 1.5 slice.60
  127.0 4.8 %collective-permute-done.side = bf16[16,128,128]{2,1,0:T(8,128)(2,1)S(1)} collective-permute-done((bf16[16,128,128]{2,1,0:T(8,128)(2,1)}, bf16[16,128,128]{2,1,0:T(8,128)(2,1)S(1)}, u32[]{:S(2)}, u32[]{:S(2)}) %collective-permute-start) | collective-permute-done | bytes 524320 | tf_op jit(solution)/shard_map/ppermute | solution.py:244
  131.8 0.7 slice.73
  132.6 0.8 copy-done.3
  133.4 0.0 collective-permute-done.2.edge_high
  133.4 0.0 collective-permute-done.1
  133.4 1.1 broadcast_in_dim.5
  134.5 11.1 %all-to-all-start.2 = ((f16[16,192,128]{2,1,0:T(8,128)(2,1)}), f16[16,192,128]{2,1,0:T(8,128)(2,1)}, u32[]{:S(2)}, u32[]{:S(2)}) async-start(f16[16,192,128]{2,1,0:T(8,128)(2,1)} %broadcast_in_dim.5), calls=%async_computation.2 | async-start | bytes 1572864 | tf_op jit(solution)/shard_map/all_to_all | solution.py:266
  145.7 5.9 %collective-permute-start.3 = (bf16[16,64,128]{2,1,0:T(8,128)(2,1)}, bf16[16,64,128]{2,1,0:T(8,128)(2,1)S(1)}, u32[]{:S(2)}, u32[]{:S(2)}) collective-permute-start(bf16[16,64,128]{2,1,0:T(8,128)(2,1)} %slice.73), channel_id=1, source_target_pairs={{0,64},{64,128},{128,192},{192,256},{256,320},{320,384},{384,448},... | collective-permute-start | bytes 786440 | tf_op jit(solution)/shard_map/ppermute | solution.py:258
  151.6 1.5 collective-permute-start.4
  153.1 4.1 %all-to-all-done.2 = f16[16,192,128]{2,1,0:T(8,128)(2,1)} async-done(((f16[16,192,128]{2,1,0:T(8,128)(2,1)}), f16[16,192,128]{2,1,0:T(8,128)(2,1)}, u32[]{:S(2)}, u32[]{:S(2)}) %all-to-all-start.2) | async-done | bytes 786464 | tf_op jit(solution)/shard_map/all_to_all | solution.py:266
  157.2 1.2 convert_element_type.32.every
  158.5 0.0 copy-start.4
  158.5 8.7 %shard_map.87 = f32[1024,128]{1,0:T(8,128)} custom-call(f32[8,128]{1,0:T(8,128)S(1)} %concatenate.12.powers, f32[16,192,128]{2,1,0:T(8,128)S(1)} %convert_element_type.32.every, f32[256,512]{1,0:T(8,128)S(1)} %bitcast.33, f32[256,512]{1,0:T(8,128)S(1)} %bitcast.35, f32[512,256]{1,0:T(8,128)S(1)} %bitcast.37, bf16[16,400,128]{2,1,0:T(8,128)(2,1)S(1)} %all_to_all.15.first), custom_call_target="tpu_custom_call" | custom-call | flops 1048576 | bytes 4194304 | tf_op jit(solution)/shard_map/pallas_call | solution.py:186
  167.2 1.4 collective-permute-done.4.edge_mid
  168.6 10.7 %collective-permute-done.3.edge_low = bf16[16,64,128]{2,1,0:T(8,128)(2,1)S(1)} collective-permute-done((bf16[16,64,128]{2,1,0:T(8,128)(2,1)}, bf16[16,64,128]{2,1,0:T(8,128)(2,1)S(1)}, u32[]{:S(2)}, u32[]{:S(2)}) %collective-permute-start.3) | collective-permute-done | bytes 262176 | tf_op jit(solution)/shard_map/ppermute | solution.py:258
  179.3 4.1 %shard_map.88 = f32[1024,128]{1,0:T(8,128)} custom-call(s32[1]{0:T(128)} %bitcast.place, bf16[16,400,128]{2,1,0:T(8,128)(2,1)S(1)} %all_to_all.15.first, bf16[16,128,128]{2,1,0:T(8,128)(2,1)S(1)} %copy-done.4, bf16[16,64,128]{2,1,0:T(8,128)(2,1)S(1)} %collective-permute-done.3.edge_low, bf16[16,16,128]{2,1,0:T(8,128)(2,1)S(1)} %collective-permute-done.4.edge_mid, ...), custom_call_target="tpu_custom_call" | custom-call | flops 1048576 | bytes 4194304 | tf_op jit(solution)/shard_map/pallas_call | solution.py:186
  (22 shorter events, 0.4 us)
Async XLA Ops:
  0.6 1.5 copy-start.7
  0.6 1.8 copy-start.8
  2.5 0.7 copy-start.9
  3.2 87.3 %copy-start = (f32[1,256,512]{2,1,0:T(8,128)S(1)}, f32[1,256,512]{2,1,0:T(8,128)}, u32[]{:S(2)}) copy-start(f32[1,256,512]{2,1,0:T(8,128)} %param.11) | copy-start | bytes 1572868
  3.2 87.2 %copy-start.1 = (f32[1,256,512]{2,1,0:T(8,128)S(1)}, f32[1,256,512]{2,1,0:T(8,128)}, u32[]{:S(2)}) copy-start(f32[1,256,512]{2,1,0:T(8,128)} %param.12) | copy-start | bytes 1572868
  3.2 87.2 %copy-start.2 = (f32[1,512,256]{2,1,0:T(8,128)S(1)}, f32[1,512,256]{2,1,0:T(8,128)}, u32[]{:S(2)}) copy-start(f32[1,512,256]{2,1,0:T(8,128)} %param.13) | copy-start | bytes 1572868
  93.3 19.1 %all-to-all-start.1 = ((f16[16,208,128]{2,1,0:T(8,128)(2,1)}), f16[16,208,128]{2,1,0:T(8,128)(2,1)}, u32[]{:S(2)}, u32[]{:S(2)}) async-start(f16[16,208,128]{2,1,0:T(8,128)(2,1)} %convert_element_type.26), calls=%async_computation.1 | async-start | bytes 1703936 | tf_op jit(solution)/shard_map/all_to_all | solution.py:240
  100.9 32.4 %collective-permute-start.2 = (bf16[16,48,128]{2,1,0:T(8,128)(2,1)}, bf16[16,48,128]{2,1,0:T(8,128)(2,1)S(1)}, u32[]{:S(2)}, u32[]{:S(2)}) collective-permute-start(bf16[16,48,128]{2,1,0:T(8,128)(2,1)} %slice.74), channel_id=1, source_target_pairs={{48,64},{112,128},{176,192},{240,256},{304,320},{368,384},{432,448... | collective-permute-start | bytes 589832 | tf_op jit(solution)/shard_map/ppermute | solution.py:235
  112.4 19.5 %collective-permute-start = (bf16[16,128,128]{2,1,0:T(8,128)(2,1)}, bf16[16,128,128]{2,1,0:T(8,128)(2,1)S(1)}, u32[]{:S(2)}, u32[]{:S(2)}) collective-permute-start(bf16[16,128,128]{2,1,0:T(8,128)(2,1)} %slice.72), channel_id=1, source_target_pairs={{0,16},{16,32},{32,48},{48,0},{64,80},{80,96},{96,112},{112,64},{1... | collective-permute-start | bytes 1572872 | tf_op jit(solution)/shard_map/ppermute | solution.py:244
  117.6 15.8 %collective-permute-start.1 = (f16[208,128]{1,0:T(8,128)(2,1)S(1)}, f16[208,128]{1,0:T(8,128)(2,1)S(1)}, u32[]{:S(2)}, u32[]{:S(2)}) collective-permute-start(f16[208,128]{1,0:T(8,128)(2,1)S(1)} %maximum_maximum_fusion), channel_id=1, source_target_pairs={{0,64},{16,80},{32,96},{48,112},{64,0},{80,16},{96,32},{112,48},{1... | collective-permute-start | bytes 159752 | tf_op jit(solution)/shard_map/ppermute | solution.py:253
  132.6 0.8 copy-start.3
  133.4 1.1 copy-start.5
  134.5 22.7 %all-to-all-start.2 = ((f16[16,192,128]{2,1,0:T(8,128)(2,1)}), f16[16,192,128]{2,1,0:T(8,128)(2,1)}, u32[]{:S(2)}, u32[]{:S(2)}) async-start(f16[16,192,128]{2,1,0:T(8,128)(2,1)} %broadcast_in_dim.5), calls=%async_computation.2 | async-start | bytes 1572864 | tf_op jit(solution)/shard_map/all_to_all | solution.py:266
  145.7 33.6 %collective-permute-start.3 = (bf16[16,64,128]{2,1,0:T(8,128)(2,1)}, bf16[16,64,128]{2,1,0:T(8,128)(2,1)S(1)}, u32[]{:S(2)}, u32[]{:S(2)}) collective-permute-start(bf16[16,64,128]{2,1,0:T(8,128)(2,1)} %slice.73), channel_id=1, source_target_pairs={{0,64},{64,128},{128,192},{192,256},{256,320},{320,384},{384,448},... | collective-permute-start | bytes 786440 | tf_op jit(solution)/shard_map/ppermute | solution.py:258
  151.6 17.0 %collective-permute-start.4 = (bf16[16,16,128]{2,1,0:T(8,128)(2,1)}, bf16[16,16,128]{2,1,0:T(8,128)(2,1)S(1)}, u32[]{:S(2)}, u32[]{:S(2)}) collective-permute-start(bf16[16,16,128]{2,1,0:T(8,128)(2,1)} %slice.60), channel_id=1, source_target_pairs={{48,64},{112,128},{176,192},{240,256},{304,320},{368,384},{432,448... | collective-permute-start | bytes 196616 | tf_op jit(solution)/shard_map/ppermute | solution.py:257
  158.5 20.8 %copy-start.4 = (bf16[16,128,128]{2,1,0:T(8,128)(2,1)S(1)}, bf16[16,128,128]{2,1,0:T(8,128)(2,1)}, u32[]{:S(2)}) copy-start(bf16[16,128,128]{2,1,0:T(8,128)(2,1)} %copy-done.3) | copy-start | bytes 1572868
  158.5 20.8 %copy-start.6 = (bf16[16,48,128]{2,1,0:T(8,128)(2,1)S(1)}, bf16[16,48,128]{2,1,0:T(8,128)(2,1)}, u32[]{:S(2)}) copy-start(bf16[16,48,128]{2,1,0:T(8,128)(2,1)} %copy-done.5) | copy-start | bytes 589828
